TPU v7x, 512 devices: a whole 4x8x8 slice. The times are simulated.
512 devices in a mesh: dp: 16 (over z, y_hi), seq: 32 (over y_lo, x, core).
Axes of the slice: x: 4, y: 8 (y_hi: 2, y_lo: 4; y = y_hi * 4 + y_lo), z: 8, core: 2. Of those that a mesh axis runs over, the one named last changes fastest.
Arguments:
- latents: bfloat16 [16, 32, 256, 3072], P('dp', 'seq'), may hold values from -6 to 6
- cotangent: bfloat16 [16, 32, 256, 3072], P('dp', 'seq'), may hold values from -6 to 6
- weights: bfloat16 [3072, 512], P('seq'), may hold values from -0.109375 to 0.109375
Outputs:
- grad_weights: float32 [3072, 512], P('seq')
All inputs are finite; a program needn't handle non-finite values.
Results may differ from a plain program's by a relative error of at most 0.035.
Values may be sent and summed in bfloat16 or wider, within the bound.
No kernel may reach another device: no remote copies, remote signals or barrier semaphores. Data moves between devices by JAX's collectives and lax.ppermute only.
A program may use at most 64 MiB of HBM per device.

v0:
```python
import jax
import jax.numpy as jnp
from jax import lax
from jax.sharding import PartitionSpec as P


def normalize(rows):
    wide = rows.astype(jnp.float32)
    mean_square = jnp.mean(wide * wide, axis=-1, keepdims=True)
    return (wide * lax.rsqrt(mean_square + 1e-06)).astype(jnp.bfloat16)


def attend_block(block):
    packed = block[:, 0]
    head = packed.shape[-1] // 4
    scale = 1.0 / head**0.5
    query = packed[..., :head]
    keys = packed[..., head : 2 * head]
    values = packed[..., 2 * head : 3 * head]
    grad_out = packed[..., 3 * head :]
    scores = jnp.einsum("fpd,gpd->pfg", query, keys, preferred_element_type=jnp.float32) * scale
    probs = jax.nn.softmax(scores, axis=-1)
    probs_b = probs.astype(jnp.bfloat16)
    out = jnp.einsum("pfg,gpd->fpd", probs_b, values, preferred_element_type=jnp.float32).astype(
        jnp.bfloat16
    )
    grad_v = jnp.einsum(
        "pfg,fpd->gpd", probs_b, grad_out, preferred_element_type=jnp.float32
    ).astype(jnp.bfloat16)
    grad_probs = jnp.einsum("fpd,gpd->pfg", grad_out, values, preferred_element_type=jnp.float32)
    delta = jnp.sum(grad_out.astype(jnp.float32) * out.astype(jnp.float32), axis=-1)
    grad_scores = (probs * (grad_probs - jnp.transpose(delta)[:, :, None])).astype(jnp.bfloat16)
    grad_q = (
        jnp.einsum("pfg,gpd->fpd", grad_scores, keys, preferred_element_type=jnp.float32) * scale
    ).astype(jnp.bfloat16)
    grad_k = (
        jnp.einsum("pfg,fpd->gpd", grad_scores, query, preferred_element_type=jnp.float32) * scale
    ).astype(jnp.bfloat16)
    return jnp.concatenate([out, grad_q, grad_k, grad_v], axis=-1)[:, None]


def shards(latents, cotangent, weights):
    width = latents.shape[-1]
    frames_here, patches = (latents.shape[1], latents.shape[2])
    head = weights.shape[1] // 4
    groups = lax.axis_size("seq")
    normed = normalize(latents.reshape(-1, width))
    tangent = cotangent.reshape(-1, width)
    piece = lax.all_gather(weights, "seq", axis=0, tiled=True)
    normed_cols = normed
    tangent_cols = tangent
    first = jnp.dot(normed_cols, piece[:, : 3 * head], preferred_element_type=jnp.float32)
    second = jnp.dot(tangent_cols, piece[:, 3 * head :], preferred_element_type=jnp.float32)
    qkv = first
    grad_out = second
    packed = jnp.concatenate([qkv.astype(jnp.bfloat16), grad_out.astype(jnp.bfloat16)], axis=-1)
    packed = packed.reshape(frames_here, groups, patches // groups, 4 * head)
    arrived = lax.all_to_all(packed, "seq", split_axis=1, concat_axis=0, tiled=True)
    result = attend_block(arrived)
    back = lax.all_to_all(result, "seq", split_axis=0, concat_axis=1, tiled=True)
    back = back.reshape(-1, 4 * head)
    outputs = back[:, :head]
    grads = back[:, head:]
    contract = (((0,), (0,)), ((), ()))
    normed_cols = normed
    tangent_cols = tangent
    first = lax.dot_general(normed_cols, grads, contract, preferred_element_type=jnp.float32)
    second = lax.dot_general(tangent_cols, outputs, contract, preferred_element_type=jnp.float32)
    shard = lax.psum_scatter(
        jnp.concatenate([first, second], axis=-1).astype(jnp.bfloat16),
        "seq",
        scatter_dimension=0,
        tiled=True,
    )
    return lax.psum(shard, "dp").astype(jnp.float32)


def solution(mesh):
    placed = (P("dp", "seq", None, None), P("dp", "seq", None, None), P("seq", None))
    return jax.shard_map(
        shards, mesh=mesh, in_specs=placed, out_specs=P("seq", None), check_vma=False
    )
```

profile of v0, /device:TPU:6, one launch (start us, length us, event | category | flops | bytes accessed | tf_op | source)
XLA Modules:
  0.0 479.2 jit_solution(12642419695066945532)
XLA Ops:
  6.5 0.7 all-gather.2.cloned.1.call-update
  7.3 0.0 reduce-scatter.4.cloned.1.call-start
  7.3 2.0 fusion.2
  9.3 68.3 %all-gather.2.cloned.1.call-done = bf16[3072,512]{1,0:T(8,128)(2,1)} async-done(((bf16[96,512]{1,0:T(8,128)(2,1)}), bf16[3072,512]{1,0:T(8,128)(2,1)}) %all-gather.2.cloned.1.call-update) | async-done | bytes 3145744 | tf_op jit(solution)/shard_map/all_gather | solution.py:49
  77.5 1.7 fusion.16
  79.3 2.7 fusion.9
  82.0 15.3 %all_to_all.8 = bf16[1,32,8,512]{3,2,0,1:T(8,128)(2,1)S(1)} all-to-all(bf16[1,32,8,512]{3,2,0,1:T(8,128)(2,1)S(1)} %maximum_bitcast_fusion), channel_id=1, replica_groups=mesh['dp'=16,'seq'=32] {'seq'}, dimensions={1} | all-to-all | bytes 524288 | tf_op jit(solution)/shard_map/all_to_all | solution.py:58
  97.3 0.1 copy.40
  97.4 0.8 fusion.67
  98.2 0.3 fusion.22
  98.5 0.5 multiply_reduce_fusion
  99.0 1.1 fusion.15
  100.0 0.1 fusion.23
  100.2 0.2 fusion.24
  100.4 0.2 copy.31
  100.6 14.7 %all_to_all.9 = bf16[32,1,8,512]{3,2,1,0:T(8,128)(2,1)S(1)} all-to-all(bf16[32,1,8,512]{3,2,1,0:T(8,128)(2,1)S(1)} %copy.31), channel_id=1, replica_groups=mesh['dp'=16,'seq'=32] {'seq'}, dimensions={0} | all-to-all | bytes 524288 | tf_op jit(solution)/shard_map/all_to_all | solution.py:60
  115.3 0.4 fusion.1
  115.7 0.9 convolution_convert_fusion
  116.6 1.9 pad_maximum_fusion
  118.5 4.7 copy.37
  123.2 0.0 all-reduce.2.cloned.1.call-start
  123.3 134.1 %reduce-scatter.4.cloned.1.call-done = bf16[96,512]{1,0:T(8,128)(2,1)} async-done(((bf16[3072,512]{1,0:T(8,128)(2,1)}), bf16[96,512]{1,0:T(8,128)(2,1)}) %reduce-scatter.4.cloned.1.call-update) | async-done | bytes 98320 | tf_op jit(solution)/shard_map/reduce_scatter | solution.py:69
  257.4 213.7 %all-reduce.2.cloned.1.call-done = bf16[96,512]{1,0:T(8,128)(2,1)} async-done(((bf16[96,512]{1,0:T(8,128)(2,1)}), bf16[96,512]{1,0:T(8,128)(2,1)}) %all-reduce.2.cloned.1.call-update) | async-done | bytes 98320 | tf_op jit(solution)/shard_map/psum | solution.py:75
  471.1 1.6 convert_element_type.72
  (10 shorter events, 0.1 us)
Async XLA Ops:
  6.5 71.0 %copy-start = (bf16[1,1,256,3072]{3,2,1,0:T(8,128)(2,1)S(1)}, bf16[1,1,256,3072]{3,2,1,0:T(8,128)(2,1)}, u32[]{:S(2)}) copy-start(bf16[1,1,256,3072]{3,2,1,0:T(8,128)(2,1)} %param.4) | copy-start | bytes 4718596
  6.5 72.7 %copy-start.1 = (bf16[1,1,256,3072]{3,2,1,0:T(8,128)(2,1)S(1)}, bf16[1,1,256,3072]{3,2,1,0:T(8,128)(2,1)}, u32[]{:S(2)}) copy-start(bf16[1,1,256,3072]{3,2,1,0:T(8,128)(2,1)} %param.3) | copy-start | bytes 4718596
  6.5 71.0 %all-gather.2.cloned.1.call-start = ((), (), s32[]{:S(2)}) async-start(), calls=%async_computation.3 | async-start | bytes 3244032 | tf_op jit(solution)/shard_map/all_gather | solution.py:49
  7.3 250.1 %reduce-scatter.4.cloned.1.call-start = ((), (), s32[]{:S(2)}) async-start(), calls=%async_computation.5 | async-start | bytes 3244032 | tf_op jit(solution)/shard_map/reduce_scatter | solution.py:69
  123.2 347.9 %all-reduce.2.cloned.1.call-start = ((), (), s32[]{:S(2)}) async-start(), calls=%async_computation.4 | async-start | bytes 196608 | tf_op jit(solution)/shard_map/psum | solution.py:75
Sparse Core Ops, SparseCore 0:
  9.5 67.9 all-gather.1
  123.3 133.9 reduce-scatter.3
  260.5 210.4 all-reduce.1
where the time goes:
time: 480 us; the launch traced here: 479 us
  waiting for transfers between devices  417 us (87%)
  blocking collectives  30 us (6%)
  between operations  13.2 us (3%)
  matrix products  8.68 us (2%)
  other arithmetic  5.53 us (1%)
  local copies, waits for them, and re-layouts  4.89 us (1%)
    psum x1, waiting for transfers between devices, shards(): return lax.psum(shard, 'dp').astype(jnp.float32)  214 us
    reduce_scatter x1, waiting for transfers between devices, shards(): lax.psum_scatter(jnp.concatenate([first, second], axis=-1).astype(jnp.bfl...  134 us
    all_gather x1, waiting for transfers between devices, shards(): piece = lax.all_gather(weights, 'seq', axis=0, tiled=True)  68.3 us
    all_to_all x1, blocking collectives, shards(): lax.all_to_all(packed, 'seq', split_axis=1, concat_axis=0, tiled=True)  15.3 us
    all_to_all x1, blocking collectives, shards(): lax.all_to_all(result, 'seq', split_axis=0, concat_axis=1, tiled=True)  14.7 us
  transfers between devices with their start and end apart: 3, of which 3 were waited for; matrix products, arithmetic and copies ran while one was open for 0% of the time, Pallas kernels for 0%

commit v1 on v0

v1 whole, which is shorter than its diff:
```python
import itertools

import jax
import jax.numpy as jnp
from jax import lax
from jax.experimental import pallas as pl
from jax.experimental.pallas import tpu as pltpu
from jax.sharding import Mesh
from jax.sharding import PartitionSpec as P

NZ, NYH, NYL, NX, NC = 8, 2, 4, 4, 2
AXES = ("z", "yh", "yl", "x", "c")
BF = jnp.bfloat16
F32 = jnp.float32
VMEM = pl.BlockSpec(memory_space=pltpu.VMEM)
ANY = pl.BlockSpec(memory_space=pl.ANY)


def device(z, yh, yl, x, c):
    return (((z * NYH + yh) * NYL + yl) * NX + x) * NC + c


def everyone():
    return itertools.product(range(NZ), range(NYH), range(NYL), range(NX), range(NC))


def groups(key, order):
    found = {}
    for at in everyone():
        found.setdefault(key(*at), []).append((order(*at), device(*at)))
    return [[d for _, d in sorted(members)] for members in found.values()]


LIGHT = groups(
    lambda z, yh, yl, x, c: (c, z, yh, yl if c else x),
    lambda z, yh, yl, x, c: x if c else yl,
)
SPREAD = groups(
    lambda z, yh, yl, x, c: (c, yh, yl if c else x),
    lambda z, yh, yl, x, c: (x if c else yl, z),
)


def heavy_pairs(step):
    pairs = []
    for z, yh, yl, x, c in everyone():
        y = (yh * NYL + yl + step) % (NYH * NYL)
        to = (z, y // NYL, y % NYL, x, c) if c else (z, yh, yl, (x + step) % NX, c)
        pairs.append((device(z, yh, yl, x, c), device(*to)))
    return pairs


def send(v, step):
    return lax.ppermute(v, AXES, heavy_pairs(step))


def other_core(v):
    return lax.ppermute(v, "c", [(0, 1), (1, 0)])


def exchange(v, members):
    return lax.all_to_all(v, AXES, split_axis=0, concat_axis=0, axis_index_groups=members, tiled=True)


def project_kernel(mine, other, lat, cot, packed, scale, w, sems):
    x, yl, c = lax.axis_index("x"), lax.axis_index("yl"), lax.axis_index("c")
    rows = mine.shape[1]
    copies = []
    for a, b in itertools.product(range(NYL), range(NX)):
        even = lax.rem(b - x + NX, NX) * NYL + a
        odd = lax.rem(a - yl + NYL, NYL) * NX + b
        own, theirs = jnp.where(c == 0, even, odd), jnp.where(c == 0, odd, even)
        base = (a * NX + b) * NC * rows
        for src, index, parity, sem in ((mine, own, c, 0), (other, theirs, 1 - c, 1)):
            at = pl.multiple_of(base + parity * rows, 16)
            copies.append(
                pltpu.make_async_copy(src.at[index], w.at[pl.ds(at, rows)], sems.at[sem, a * NX + b])
            )
    for copy in copies:
        copy.start()
    wide = lat[...].astype(F32)
    r = lax.rsqrt(jnp.mean(wide * wide, axis=-1, keepdims=True) + 1e-06)
    scale[...] = jnp.broadcast_to(r, scale.shape)
    for copy in copies:
        copy.wait()
    head = w.shape[1] // 4
    qkv = jnp.dot(lat[...], w[:, : 3 * head], preferred_element_type=F32) * r
    packed[:, : 3 * head] = qkv.astype(BF)
    packed[:, 3 * head :] = jnp.dot(cot[...], w[:, 3 * head :], preferred_element_type=F32).astype(BF)


def project(mine, other, lat, cot):
    tokens, width = lat.shape
    columns = mine.shape[-1]
    return pl.pallas_call(
        project_kernel,
        out_shape=(
            jax.ShapeDtypeStruct((tokens, columns), BF),
            jax.ShapeDtypeStruct((tokens, 128), F32),
        ),
        in_specs=[ANY, ANY, VMEM, VMEM],
        out_specs=(VMEM, VMEM),
        scratch_shapes=[pltpu.VMEM((width, columns), BF), pltpu.SemaphoreType.DMA((2, NYL * NX))],
        compiler_params=pltpu.CompilerParams(vmem_limit_bytes=24 * 2**20),
        name="project",
    )(mine, other, lat, cot)


def weight_kernel(back, scale, lat, cot, mine, other):
    c = lax.axis_index("c")
    head = back.shape[1] // 4
    rows = mine.shape[1]
    outs = back[:, :head]
    r = jnp.concatenate([scale[...]] * 3, axis=-1)
    grads = (back[:, head:].astype(F32) * r).astype(BF)
    contract = (((0,), (0,)), ((), ()))
    wide = NX * NC * rows
    for a in range(NYL):
        part = slice(a * wide, (a + 1) * wide)
        first = lax.dot_general(lat[:, part], grads, contract, preferred_element_type=F32)
        second = lax.dot_general(cot[:, part], outs, contract, preferred_element_type=F32)
        for b in range(NX):
            even = slice(2 * b * rows, (2 * b + 1) * rows)
            odd = slice((2 * b + 1) * rows, (2 * b + 2) * rows)
            for value, at in ((first, slice(0, 3 * head)), (second, slice(3 * head, 4 * head))):
                mine[a * NX + b, :, at] = jnp.where(c == 0, value[even], value[odd]).astype(BF)
                other[a * NX + b, :, at] = jnp.where(c == 0, value[odd], value[even]).astype(BF)


def weight_parts(back, scale, lat, cot):
    width, columns = lat.shape[1], back.shape[1]
    rows = width // (NYL * NX * NC)
    shape = jax.ShapeDtypeStruct((NYL * NX, rows, columns), BF)
    return pl.pallas_call(
        weight_kernel,
        out_shape=(shape, shape),
        in_specs=[VMEM] * 4,
        out_specs=(VMEM, VMEM),
        compiler_params=pltpu.CompilerParams(vmem_limit_bytes=32 * 2**20),
        name="weight_parts",
    )(back, scale, lat, cot)


def split_kernel(mine, arrived, own, plus, minus, two_a, two_b):
    x, yl, c = lax.axis_index("x"), lax.axis_index("yl"), lax.axis_index("c")

    def total(offset, t):
        even = t * NX + lax.rem(x + offset, NX)
        odd = lax.rem(yl + offset, NYL) * NX + t
        index = jnp.where(c == 0, even, odd)
        return (mine[index].astype(F32) + arrived[index].astype(F32)).astype(BF)

    for t in range(4):
        own[t] = total(0, t)
        plus[t] = total(1, t)
        minus[t] = total(3, t)
    for t in range(2):
        two_a[t] = total(2, t)
        two_b[t] = total(2, t + 2)


def split_sum(mine, arrived):
    _, rows, columns = mine.shape
    four = jax.ShapeDtypeStruct((4, rows, columns), BF)
    two = jax.ShapeDtypeStruct((2, rows, columns), BF)
    return pl.pallas_call(
        split_kernel,
        out_shape=(four, four, four, two, two),
        in_specs=[VMEM] * 2,
        out_specs=(VMEM,) * 5,
        compiler_params=pltpu.CompilerParams(vmem_limit_bytes=24 * 2**20),
        name="split_sum",
    )(mine, arrived)


def attend_block(packed):
    head = packed.shape[-1] // 4
    scale = 1.0 / head**0.5
    query = packed[..., :head]
    keys = packed[..., head : 2 * head]
    values = packed[..., 2 * head : 3 * head]
    grad_out = packed[..., 3 * head :]
    scores = jnp.einsum("fpd,gpd->pfg", query, keys, preferred_element_type=F32) * scale
    probs = jax.nn.softmax(scores, axis=-1)
    probs_b = probs.astype(BF)
    out = jnp.einsum("pfg,gpd->fpd", probs_b, values, preferred_element_type=F32).astype(BF)
    grad_v = jnp.einsum("pfg,fpd->gpd", probs_b, grad_out, preferred_element_type=F32).astype(BF)
    grad_probs = jnp.einsum("fpd,gpd->pfg", grad_out, values, preferred_element_type=F32)
    delta = jnp.sum(grad_out.astype(F32) * out.astype(F32), axis=-1)
    grad_scores = (probs * (grad_probs - jnp.transpose(delta)[:, :, None])).astype(BF)
    grad_q = (jnp.einsum("pfg,gpd->fpd", grad_scores, keys, preferred_element_type=F32) * scale).astype(BF)
    grad_k = (jnp.einsum("pfg,fpd->gpd", grad_scores, query, preferred_element_type=F32) * scale).astype(BF)
    return jnp.concatenate([out, grad_q, grad_k, grad_v], axis=-1)


def gather(weights):
    rows, columns = weights.shape
    four = exchange(jnp.broadcast_to(weights[None], (4, rows, columns)), LIGHT)
    before = send(four, 1)
    after = send(four, -1)
    far_a = send(four[:2], 2)
    far_b = send(four[2:], -2)
    mine = jnp.concatenate([four, after, far_a, far_b, before])
    return mine, other_core(mine)


def reduce(mine, other):
    rows, columns = mine.shape[1:]
    own, plus, minus, two_a, two_b = split_sum(mine, other_core(other))
    far_a = send(two_a, 2)
    far_b = send(two_b, -2)
    from_before = send(plus, 1)
    from_after = send(minus, -1)
    total = own.astype(F32) + from_before.astype(F32) + from_after.astype(F32)
    total = total + jnp.concatenate([far_a, far_b]).astype(F32)
    pieces = total.astype(BF).reshape(4, 2, rows // 2, 4, columns // 4).transpose(0, 1, 3, 2, 4)
    pieces = pieces.reshape(4 * NZ, rows // 2, columns // 4)
    piece = jnp.sum(exchange(pieces, SPREAD).astype(F32), axis=0).astype(BF)
    copies = jnp.broadcast_to(piece[None], (NZ * NYH, *piece.shape))
    copies = lax.all_to_all(copies, ("z", "yh"), split_axis=0, concat_axis=0, tiled=True)
    copies = copies.reshape(2, 4, NYH, rows // 2, columns // 4).astype(F32)
    return jnp.sum(copies, axis=2).transpose(0, 2, 1, 3).reshape(rows, columns)


def shards(latents, cotangent, weights):
    width = latents.shape[-1]
    patches = latents.shape[2]
    columns = weights.shape[1]
    frames = NYL * NX * NC
    lat = latents.reshape(-1, width)
    cot = cotangent.reshape(-1, width)
    mine, other = gather(weights)
    packed, scale = project(mine, other, lat, cot)
    packed = packed.reshape(frames, patches // frames, columns)
    seq = ("yl", "x", "c")
    arrived = lax.all_to_all(packed, seq, split_axis=0, concat_axis=0, tiled=True)
    result = attend_block(arrived)
    back = lax.all_to_all(result, seq, split_axis=0, concat_axis=0, tiled=True)
    mine, other = weight_parts(back.reshape(-1, columns), scale, lat, cot)
    return reduce(mine, other)


def solution(mesh):
    fine = Mesh(mesh.devices.reshape(NZ, NYH, NYL, NX, NC), AXES)
    dp, seq = ("z", "yh"), ("yl", "x", "c")
    placed = (P(dp, seq, None, None), P(dp, seq, None, None), P(seq, None))
    return jax.shard_map(shards, mesh=fine, in_specs=placed, out_specs=P(seq, None), check_vma=False)
```

time: 480 us -> 156 us (0.33)
  the two profiles are of different devices: /device:TPU:6 before, /device:TPU:1 now
where the time goes in v1:
time: 156 us; the launch traced here: 155 us
  blocking collectives  83.6 us (54%)
  starting transfers between devices  36.4 us (23%)
  waiting for transfers between devices  19.8 us (13%)
  Pallas kernels  8.05 us (5%)
  matrix products  3.96 us (3%)
  local copies, waits for them, and re-layouts  2.83 us (2%)
    all_to_all x2, blocking collectives, exchange(): lax.all_to_all(v, AXES, split_axis=0, concat_axis=0, axis_index_groups=me...  36.3 us
    ppermute x8, starting transfers between devices, send(): return lax.ppermute(v, AXES, heavy_pairs(step))  27.5 us
    all_to_all x1, blocking collectives, reduce(): lax.all_to_all(copies, ('z', 'yh'), split_axis=0, concat_axis=0, tiled=True)  18.4 us
    all_to_all x1, blocking collectives, shards(): back = lax.all_to_all(result, seq, split_axis=0, concat_axis=0, tiled=True)  14.6 us
    all_to_all x1, blocking collectives, shards(): lax.all_to_all(packed, seq, split_axis=0, concat_axis=0, tiled=True)  14.2 us
    ppermute x8, waiting for transfers between devices, send(): return lax.ppermute(v, AXES, heavy_pairs(step))  13.6 us
    ppermute x2, starting transfers between devices, other_core(): return lax.ppermute(v, 'c', [(0, 1), (1, 0)])  8.98 us
    pallas_call x1, Pallas kernels, project(): pl.pallas_call(project_kernel, out_shape=(jax.ShapeDtypeStruct((tokens, c...  6.25 us
  transfers between devices with their start and end apart: 10, of which 6 were waited for; matrix products, arithmetic and copies ran while one was open for 0% of the time, Pallas kernels for 0%

profile of v1, /device:TPU:1, one launch (start us, length us, event | category | flops | bytes accessed | tf_op | source)
XLA Modules:
  0.0 155.2 jit_solution(8541600933967386636)
XLA Ops:
  0.9 10.9 %all_to_all.25 = bf16[4,96,512]{2,1,0:T(8,128)(2,1)S(1)} all-to-all(bf16[4,96,512]{2,1,0:T(8,128)(2,1)S(1)} %broadcast_in_dim.4), channel_id=1, replica_groups={{0,8,16,24},{1,3,5,7},{2,10,18,26},{4,12,20,28},{6,14,22,30},{9,11,13,1..., dimensions={0} | all-to-all | bytes 786432 | tf_op jit(solution)/shard_map/all_to_all | solution.py:62
  11.8 5.2 %collective-permute-start = (bf16[4,96,512]{2,1,0:T(8,128)(2,1)S(1)}, bf16[4,96,512]{2,1,0:T(8,128)(2,1)S(1)}, u32[]{:S(2)}, u32[]{:S(2)}) collective-permute-start(bf16[4,96,512]{2,1,0:T(8,128)(2,1)S(1)} %all_to_all.25), channel_id=1, source_target_pairs={{0,6},{1,57},{2,0},{3,59},{4,2},{5,61},{6,4},{7,63},{8,14},{9,1},{... | collective-permute-start | bytes 1179656 | tf_op jit(solution)/shard_map/ppermute | solution.py:54
  17.1 3.6 %collective-permute-start.2 = (bf16[2,96,512]{2,1,0:T(8,128)(2,1)S(1)}, bf16[2,96,512]{2,1,0:T(8,128)(2,1)S(1)}, u32[]{:S(2)}, u32[]{:S(2)}) collective-permute-start(bf16[2,96,512]{2,1,0:T(8,128)(2,1)S(1)} %get-tuple-element.23), channel_id=1, source_target_pairs={{0,4},{1,49},{2,6},{3,51},{4,0},{5,53},{6,2},{7,55},{8,12},{9,57},... | collective-permute-start | bytes 589832 | tf_op jit(solution)/shard_map/ppermute | solution.py:54
  20.7 2.8 %collective-permute-start.1 = (bf16[2,96,512]{2,1,0:T(8,128)(2,1)S(1)}, bf16[2,96,512]{2,1,0:T(8,128)(2,1)S(1)}, u32[]{:S(2)}, u32[]{:S(2)}) collective-permute-start(bf16[2,96,512]{2,1,0:T(8,128)(2,1)S(1)} %get-tuple-element.24), channel_id=1, source_target_pairs={{0,4},{1,17},{2,6},{3,19},{4,0},{5,21},{6,2},{7,23},{8,12},{9,25},... | collective-permute-start | bytes 589832 | tf_op jit(solution)/shard_map/ppermute | solution.py:54
  23.5 1.9 %collective-permute-start.3 = (bf16[4,96,512]{2,1,0:T(8,128)(2,1)S(1)}, bf16[4,96,512]{2,1,0:T(8,128)(2,1)S(1)}, u32[]{:S(2)}, u32[]{:S(2)}) collective-permute-start(bf16[4,96,512]{2,1,0:T(8,128)(2,1)S(1)} %all_to_all.25), channel_id=1, source_target_pairs={{0,2},{1,9},{2,4},{3,11},{4,6},{5,13},{6,0},{7,15},{8,10},{9,17},{... | collective-permute-start | bytes 1179656 | tf_op jit(solution)/shard_map/ppermute | solution.py:54
  25.5 6.3 %collective-permute-done.1 = bf16[2,96,512]{2,1,0:T(8,128)(2,1)S(1)} collective-permute-done((bf16[2,96,512]{2,1,0:T(8,128)(2,1)S(1)}, bf16[2,96,512]{2,1,0:T(8,128)(2,1)S(1)}, u32[]{:S(2)}, u32[]{:S(2)}) %collective-permute-start.1) | collective-permute-done | bytes 196640 | tf_op jit(solution)/shard_map/ppermute | solution.py:54
  31.9 3.1 %collective-permute-done.3 = bf16[4,96,512]{2,1,0:T(8,128)(2,1)S(1)} collective-permute-done((bf16[4,96,512]{2,1,0:T(8,128)(2,1)S(1)}, bf16[4,96,512]{2,1,0:T(8,128)(2,1)S(1)}, u32[]{:S(2)}, u32[]{:S(2)}) %collective-permute-start.3) | collective-permute-done | bytes 393248 | tf_op jit(solution)/shard_map/ppermute | solution.py:54
  35.1 6.8 %collective-permute-start.4 = (bf16[16,96,512]{2,1,0:T(8,128)(2,1)S(1)}, bf16[16,96,512]{2,1,0:T(8,128)(2,1)S(1)}, u32[]{:S(2)}, u32[]{:S(2)}) collective-permute-start(bf16[16,96,512]{2,1,0:T(8,128)(2,1)S(1)} %constant_dynamic-update-slice_fusion.mine), channel_id=1, source_target_pairs={{0,1},{1,0},{2,3},{3,2},{4,5},{5,4},{6,7},{7,6},{8,9},{9,8},{10,11... | collective-permute-start | bytes 4718600 | tf_op jit(solution)/shard_map/ppermute | solution.py:58
  41.9 3.0 %collective-permute-done.4.other = bf16[16,96,512]{2,1,0:T(8,128)(2,1)S(1)} collective-permute-done((bf16[16,96,512]{2,1,0:T(8,128)(2,1)S(1)}, bf16[16,96,512]{2,1,0:T(8,128)(2,1)S(1)}, u32[]{:S(2)}, u32[]{:S(2)}) %collective-permute-start.4) | collective-permute-done | bytes 1572896 | tf_op jit(solution)/shard_map/ppermute | solution.py:58
  44.9 6.3 %project.1 = (bf16[256,512]{1,0:T(8,128)(2,1)S(1)}, f32[256,128]{1,0:T(8,128)S(1)}) custom-call(bf16[16,96,512]{2,1,0:T(8,128)(2,1)S(1)} %constant_dynamic-update-slice_fusion.mine, bf16[16,96,512]{2,1,0:T(8,128)(2,1)S(1)} %collective-permute-done.4.other, bf16[256,3072]{1,0:T(8,128)(2,1)S(1)} %bitcast.27, bf16[256,3072]{1,0:T(8,128)(2,1)S(1)} %bitcast.29), custom_call_target="tpu_custom_call" | custom-call | tf_op jit(solution)/shard_map/project/pallas_call | solution.py:95
  51.2 14.2 %all_to_all.26 = bf16[32,8,512]{2,1,0:T(8,128)(2,1)S(1)} all-to-all(bf16[32,8,512]{2,1,0:T(8,128)(2,1)S(1)} %bitcast.32), channel_id=1, replica_groups=mesh['z'=8,'yh'=2,'yl'=4,'x'=4,'c'=2] {'yl','x','c'}, dimensions={0} | all-to-all | bytes 524288 | tf_op jit(solution)/shard_map/all_to_all | solution.py:236
  67.2 1.3 multiply_reduce_fusion
  70.3 14.6 %all_to_all.27 = bf16[32,8,512]{2,1,0:T(8,128)(2,1)S(1)} all-to-all(bf16[32,8,512]{2,1,0:T(8,128)(2,1)S(1)} %copy.40), channel_id=1, replica_groups=mesh['z'=8,'yh'=2,'yl'=4,'x'=4,'c'=2] {'yl','x','c'}, dimensions={0} | all-to-all | bytes 524288 | tf_op jit(solution)/shard_map/all_to_all | solution.py:238
  84.9 1.4 weight_parts.1
  86.4 2.1 %collective-permute-start.5 = (bf16[16,96,512]{2,1,0:T(8,128)(2,1)S(1)}, bf16[16,96,512]{2,1,0:T(8,128)(2,1)S(1)}, u32[]{:S(2)}, u32[]{:S(2)}) collective-permute-start(bf16[16,96,512]{2,1,0:T(8,128)(2,1)S(1)} %get-tuple-element.17), channel_id=1, source_target_pairs={{0,1},{1,0},{2,3},{3,2},{4,5},{5,4},{6,7},{7,6},{8,9},{9,8},{10,11... | collective-permute-start | bytes 4718600 | tf_op jit(solution)/shard_map/ppermute | solution.py:58
  88.5 3.2 %collective-permute-done.5.arrived = bf16[16,96,512]{2,1,0:T(8,128)(2,1)S(1)} collective-permute-done((bf16[16,96,512]{2,1,0:T(8,128)(2,1)S(1)}, bf16[16,96,512]{2,1,0:T(8,128)(2,1)S(1)}, u32[]{:S(2)}, u32[]{:S(2)}) %collective-permute-start.5) | collective-permute-done | bytes 1572896 | tf_op jit(solution)/shard_map/ppermute | solution.py:58
  92.0 2.4 %collective-permute-start.6 = (bf16[4,96,512]{2,1,0:T(8,128)(2,1)S(1)}, bf16[4,96,512]{2,1,0:T(8,128)(2,1)S(1)}, u32[]{:S(2)}, u32[]{:S(2)}) collective-permute-start(bf16[4,96,512]{2,1,0:T(8,128)(2,1)S(1)} %get-tuple-element.19), channel_id=1, source_target_pairs={{0,2},{1,9},{2,4},{3,11},{4,6},{5,13},{6,0},{7,15},{8,10},{9,17},{... | collective-permute-start | bytes 1179656 | tf_op jit(solution)/shard_map/ppermute | solution.py:54
  94.4 4.1 %collective-permute-start.7 = (bf16[4,96,512]{2,1,0:T(8,128)(2,1)S(1)}, bf16[4,96,512]{2,1,0:T(8,128)(2,1)S(1)}, u32[]{:S(2)}, u32[]{:S(2)}) collective-permute-start(bf16[4,96,512]{2,1,0:T(8,128)(2,1)S(1)} %get-tuple-element.20), channel_id=1, source_target_pairs={{0,6},{1,57},{2,0},{3,59},{4,2},{5,61},{6,4},{7,63},{8,14},{9,1},{... | collective-permute-start | bytes 1179656 | tf_op jit(solution)/shard_map/ppermute | solution.py:54
  98.5 1.9 %collective-permute-start.8 = (bf16[2,96,512]{2,1,0:T(8,128)(2,1)S(1)}, bf16[2,96,512]{2,1,0:T(8,128)(2,1)S(1)}, u32[]{:S(2)}, u32[]{:S(2)}) collective-permute-start(bf16[2,96,512]{2,1,0:T(8,128)(2,1)S(1)} %get-tuple-element.21), channel_id=1, source_target_pairs={{0,4},{1,17},{2,6},{3,19},{4,0},{5,21},{6,2},{7,23},{8,12},{9,25},... | collective-permute-start | bytes 589832 | tf_op jit(solution)/shard_map/ppermute | solution.py:54
  100.5 5.5 %collective-permute-start.9 = (bf16[2,96,512]{2,1,0:T(8,128)(2,1)S(1)}, bf16[2,96,512]{2,1,0:T(8,128)(2,1)S(1)}, u32[]{:S(2)}, u32[]{:S(2)}) collective-permute-start(bf16[2,96,512]{2,1,0:T(8,128)(2,1)S(1)} %get-tuple-element.22), channel_id=1, source_target_pairs={{0,4},{1,49},{2,6},{3,51},{4,0},{5,53},{6,2},{7,55},{8,12},{9,57},... | collective-permute-start | bytes 589832 | tf_op jit(solution)/shard_map/ppermute | solution.py:54
  106.0 3.0 %collective-permute-done.8 = bf16[2,96,512]{2,1,0:T(8,128)(2,1)S(1)} collective-permute-done((bf16[2,96,512]{2,1,0:T(8,128)(2,1)S(1)}, bf16[2,96,512]{2,1,0:T(8,128)(2,1)S(1)}, u32[]{:S(2)}, u32[]{:S(2)}) %collective-permute-start.8) | collective-permute-done | bytes 196640 | tf_op jit(solution)/shard_map/ppermute | solution.py:54
  108.9 1.2 collective-permute-done.9
  110.5 25.4 %all_to_all.28 = bf16[32,48,128]{2,1,0:T(8,128)(2,1)S(1)} all-to-all(bf16[32,48,128]{2,1,0:T(8,128)(2,1)S(1)} %bitcast.33), channel_id=1, replica_groups={{0,64,128,192,256,320,384,448,8,72,136,200,264,328,392,456,16,80,144,20..., dimensions={0} | all-to-all | bytes 786432 | tf_op jit(solution)/shard_map/all_to_all | solution.py:62
  136.0 18.4 %all_to_all.29 = bf16[16,48,128]{2,1,0:T(8,128)(2,1)S(1)} all-to-all(bf16[16,48,128]{2,1,0:T(8,128)(2,1)S(1)} %broadcast_in_dim.5), channel_id=1, replica_groups=mesh['z'=8,'yh'=2,'yl'=4,'x'=4,'c'=2] {'z','yh'}, dimensions={0} | all-to-all | bytes 393216 | tf_op jit(solution)/shard_map/all_to_all | solution.py:220
  (34 shorter events, 6.2 us)
Async XLA Ops:
  11.8 13.7 %collective-permute-start = (bf16[4,96,512]{2,1,0:T(8,128)(2,1)S(1)}, bf16[4,96,512]{2,1,0:T(8,128)(2,1)S(1)}, u32[]{:S(2)}, u32[]{:S(2)}) collective-permute-start(bf16[4,96,512]{2,1,0:T(8,128)(2,1)S(1)} %all_to_all.25), channel_id=1, source_target_pairs={{0,6},{1,57},{2,0},{3,59},{4,2},{5,61},{6,4},{7,63},{8,14},{9,1},{... | collective-permute-start | bytes 1179656 | tf_op jit(solution)/shard_map/ppermute | solution.py:54
  17.1 14.8 %collective-permute-start.2 = (bf16[2,96,512]{2,1,0:T(8,128)(2,1)S(1)}, bf16[2,96,512]{2,1,0:T(8,128)(2,1)S(1)}, u32[]{:S(2)}, u32[]{:S(2)}) collective-permute-start(bf16[2,96,512]{2,1,0:T(8,128)(2,1)S(1)} %get-tuple-element.23), channel_id=1, source_target_pairs={{0,4},{1,49},{2,6},{3,51},{4,0},{5,53},{6,2},{7,55},{8,12},{9,57},... | collective-permute-start | bytes 589832 | tf_op jit(solution)/shard_map/ppermute | solution.py:54
  20.7 24.2 %copy-start = (bf16[1,1,256,3072]{3,2,1,0:T(8,128)(2,1)S(1)}, bf16[1,1,256,3072]{3,2,1,0:T(8,128)(2,1)}, u32[]{:S(2)}) copy-start(bf16[1,1,256,3072]{3,2,1,0:T(8,128)(2,1)} %param.3) | copy-start | bytes 4718596
  20.7 24.2 %copy-start.1 = (bf16[1,1,256,3072]{3,2,1,0:T(8,128)(2,1)S(1)}, bf16[1,1,256,3072]{3,2,1,0:T(8,128)(2,1)}, u32[]{:S(2)}) copy-start(bf16[1,1,256,3072]{3,2,1,0:T(8,128)(2,1)} %param.4) | copy-start | bytes 4718596
  20.7 11.2 %collective-permute-start.1 = (bf16[2,96,512]{2,1,0:T(8,128)(2,1)S(1)}, bf16[2,96,512]{2,1,0:T(8,128)(2,1)S(1)}, u32[]{:S(2)}, u32[]{:S(2)}) collective-permute-start(bf16[2,96,512]{2,1,0:T(8,128)(2,1)S(1)} %get-tuple-element.24), channel_id=1, source_target_pairs={{0,4},{1,17},{2,6},{3,19},{4,0},{5,21},{6,2},{7,23},{8,12},{9,25},... | collective-permute-start | bytes 589832 | tf_op jit(solution)/shard_map/ppermute | solution.py:54
  23.5 11.5 %collective-permute-start.3 = (bf16[4,96,512]{2,1,0:T(8,128)(2,1)S(1)}, bf16[4,96,512]{2,1,0:T(8,128)(2,1)S(1)}, u32[]{:S(2)}, u32[]{:S(2)}) collective-permute-start(bf16[4,96,512]{2,1,0:T(8,128)(2,1)S(1)} %all_to_all.25), channel_id=1, source_target_pairs={{0,2},{1,9},{2,4},{3,11},{4,6},{5,13},{6,0},{7,15},{8,10},{9,17},{... | collective-permute-start | bytes 1179656 | tf_op jit(solution)/shard_map/ppermute | solution.py:54
  35.1 9.9 %collective-permute-start.4 = (bf16[16,96,512]{2,1,0:T(8,128)(2,1)S(1)}, bf16[16,96,512]{2,1,0:T(8,128)(2,1)S(1)}, u32[]{:S(2)}, u32[]{:S(2)}) collective-permute-start(bf16[16,96,512]{2,1,0:T(8,128)(2,1)S(1)} %constant_dynamic-update-slice_fusion.mine), channel_id=1, source_target_pairs={{0,1},{1,0},{2,3},{3,2},{4,5},{5,4},{6,7},{7,6},{8,9},{9,8},{10,11... | collective-permute-start | bytes 4718600 | tf_op jit(solution)/shard_map/ppermute | solution.py:58
  66.1 1.1 copy-start.2
  86.4 5.3 %collective-permute-start.5 = (bf16[16,96,512]{2,1,0:T(8,128)(2,1)S(1)}, bf16[16,96,512]{2,1,0:T(8,128)(2,1)S(1)}, u32[]{:S(2)}, u32[]{:S(2)}) collective-permute-start(bf16[16,96,512]{2,1,0:T(8,128)(2,1)S(1)} %get-tuple-element.17), channel_id=1, source_target_pairs={{0,1},{1,0},{2,3},{3,2},{4,5},{5,4},{6,7},{7,6},{8,9},{9,8},{10,11... | collective-permute-start | bytes 4718600 | tf_op jit(solution)/shard_map/ppermute | solution.py:58
  92.0 18.1 %collective-permute-start.6 = (bf16[4,96,512]{2,1,0:T(8,128)(2,1)S(1)}, bf16[4,96,512]{2,1,0:T(8,128)(2,1)S(1)}, u32[]{:S(2)}, u32[]{:S(2)}) collective-permute-start(bf16[4,96,512]{2,1,0:T(8,128)(2,1)S(1)} %get-tuple-element.19), channel_id=1, source_target_pairs={{0,2},{1,9},{2,4},{3,11},{4,6},{5,13},{6,0},{7,15},{8,10},{9,17},{... | collective-permute-start | bytes 1179656 | tf_op jit(solution)/shard_map/ppermute | solution.py:54
  94.4 15.7 %collective-permute-start.7 = (bf16[4,96,512]{2,1,0:T(8,128)(2,1)S(1)}, bf16[4,96,512]{2,1,0:T(8,128)(2,1)S(1)}, u32[]{:S(2)}, u32[]{:S(2)}) collective-permute-start(bf16[4,96,512]{2,1,0:T(8,128)(2,1)S(1)} %get-tuple-element.20), channel_id=1, source_target_pairs={{0,6},{1,57},{2,0},{3,59},{4,2},{5,61},{6,4},{7,63},{8,14},{9,1},{... | collective-permute-start | bytes 1179656 | tf_op jit(solution)/shard_map/ppermute | solution.py:54
  98.5 10.4 %collective-permute-start.8 = (bf16[2,96,512]{2,1,0:T(8,128)(2,1)S(1)}, bf16[2,96,512]{2,1,0:T(8,128)(2,1)S(1)}, u32[]{:S(2)}, u32[]{:S(2)}) collective-permute-start(bf16[2,96,512]{2,1,0:T(8,128)(2,1)S(1)} %get-tuple-element.21), channel_id=1, source_target_pairs={{0,4},{1,17},{2,6},{3,19},{4,0},{5,21},{6,2},{7,23},{8,12},{9,25},... | collective-permute-start | bytes 589832 | tf_op jit(solution)/shard_map/ppermute | solution.py:54
  100.5 9.6 %collective-permute-start.9 = (bf16[2,96,512]{2,1,0:T(8,128)(2,1)S(1)}, bf16[2,96,512]{2,1,0:T(8,128)(2,1)S(1)}, u32[]{:S(2)}, u32[]{:S(2)}) collective-permute-start(bf16[2,96,512]{2,1,0:T(8,128)(2,1)S(1)} %get-tuple-element.22), channel_id=1, source_target_pairs={{0,4},{1,49},{2,6},{3,51},{4,0},{5,53},{6,2},{7,55},{8,12},{9,57},... | collective-permute-start | bytes 589832 | tf_op jit(solution)/shard_map/ppermute | solution.py:54

commit v2 on v1

v2 whole, which is shorter than its diff:
```python
import itertools

import jax
import jax.numpy as jnp
from jax import lax
from jax.experimental import pallas as pl
from jax.experimental.pallas import tpu as pltpu
from jax.sharding import Mesh
from jax.sharding import PartitionSpec as P

NZ, NYH, NYL, NX, NC = 8, 2, 4, 4, 2
AXES = ("z", "yh", "yl", "x", "c")
BF = jnp.bfloat16
F32 = jnp.float32
VMEM = pl.BlockSpec(memory_space=pltpu.VMEM)
ANY = pl.BlockSpec(memory_space=pl.ANY)


def device(z, yh, yl, x, c):
    return (((z * NYH + yh) * NYL + yl) * NX + x) * NC + c


def everyone():
    return itertools.product(range(NZ), range(NYH), range(NYL), range(NX), range(NC))


def groups(key, order):
    found = {}
    for at in everyone():
        found.setdefault(key(*at), []).append((order(*at), device(*at)))
    return [[d for _, d in sorted(members)] for members in found.values()]


LIGHT = groups(
    lambda z, yh, yl, x, c: (c, z, yh, yl % 2) if c else (c, z // 2, yh, x),
    lambda z, yh, yl, x, c: (yl // 2, x) if c else (yl, z % 2),
)
HEAVY = groups(
    lambda z, yh, yl, x, c: (c, z // 2, yh, yl // 2, x) if c else (c, z, yh, yl),
    lambda z, yh, yl, x, c: (yl % 2, z % 2) if c else (x,),
)
SPREAD = groups(
    lambda z, yh, yl, x, c: (c, yh, yl % 2, z % 2) if c else (c, yh, x),
    lambda z, yh, yl, x, c: (yl // 2, x, z // 2) if c else (yl, z % 2, z // 2),
)


def other_core(v):
    return lax.ppermute(v, "c", [(0, 1), (1, 0)])


def exchange(v, members):
    return lax.all_to_all(v, AXES, split_axis=0, concat_axis=0, axis_index_groups=members, tiled=True)


def half_shards():
    for yl, x, half in itertools.product(range(NYL), range(NX), range(2)):
        yield yl, x, half, x * 8 + yl * 2 + half, (yl % 2 * 2 + half) * 8 + yl // 2 * NX + x


def prepare_kernel(lat, cot, own, away):
    c = lax.axis_index("c")
    tokens, width = lat.shape
    rows = width // (NYL * NX * NC)
    block = NX * NC * rows
    part = block // 2
    source = lax.broadcasted_iota(jnp.int32, (block, block), 0)
    k = lax.broadcasted_iota(jnp.int32, (block, block), 1)
    second = (k >= part).astype(jnp.int32)
    k = k - part * second
    wanted = k + rows * (second + c - 2 * c * second)
    for b in range(1, NX):
        wanted = wanted + rows * (k >= b * rows).astype(jnp.int32)
    pick = (source == wanted).astype(F32).astype(BF)
    wide = lat[...].astype(F32)
    r = lax.rsqrt(jnp.mean(wide * wide, axis=-1, keepdims=True) + 1e-06)
    for a in range(NYL):
        at = slice(a * block, (a + 1) * block)
        to = slice(a * part, (a + 1) * part)
        normed = (lat[:, at].astype(F32) * r).astype(BF)
        for index, value in ((0, normed), (1, cot[:, at])):
            moved = jnp.dot(value, pick, preferred_element_type=F32).astype(BF)
            own[index, :, to] = moved[:, :part]
            away[index, :, to] = moved[:, part:]


def prepare(lat, cot):
    tokens, width = lat.shape
    shape = jax.ShapeDtypeStruct((2, tokens, width // 2), BF)
    return pl.pallas_call(
        prepare_kernel,
        out_shape=(shape, shape),
        in_specs=[VMEM] * 2,
        out_specs=(VMEM,) * 2,
        compiler_params=pltpu.CompilerParams(vmem_limit_bytes=24 * 2**20),
        name="prepare",
    )(lat, cot)


def project_kernel(blocks, own, arrived, mine, theirs, w, sums, sems):
    c = lax.axis_index("c")
    rows = blocks.shape[1]
    copies = []
    for yl, x, half, even, odd in half_shards():
        place = (yl * NX + x) * 2 + half
        copies.append(
            pltpu.make_async_copy(
                blocks.at[jnp.where(c == 0, even, odd)], w.at[pl.ds(place * rows, rows)], sems.at[place]
            )
        )
    for copy in copies:
        copy.start()
    for copy in copies:
        copy.wait()
    head = w.shape[1] // 4
    for index, tokens in ((0, own), (1, arrived)):
        sums[index, :, : 3 * head] = jnp.dot(tokens[0], w[:, : 3 * head], preferred_element_type=F32)
        sums[index, :, 3 * head :] = jnp.dot(tokens[1], w[:, 3 * head :], preferred_element_type=F32)
    count = own.shape[1] // 2
    for index, frame in ((0, c), (1, 1 - c)):
        for to, half in ((mine, c), (theirs, 1 - c)):
            value = sums[index, pl.ds(pl.multiple_of(half * count, 128), count), :]
            to[:, frame] = value.reshape(to.shape[0], to.shape[2], to.shape[3])


def project(blocks, own, arrived):
    _, tokens, width = own.shape
    columns = blocks.shape[-1]
    chips = NYL * NX
    shape = jax.ShapeDtypeStruct((chips, NC, tokens // (chips * NC), columns), F32)
    return pl.pallas_call(
        project_kernel,
        out_shape=(shape, shape),
        in_specs=[ANY, VMEM, VMEM],
        out_specs=(VMEM, VMEM),
        scratch_shapes=[
            pltpu.VMEM((width, columns), BF),
            pltpu.VMEM((2, tokens, columns), F32),
            pltpu.SemaphoreType.DMA((NYL * NX * 2,)),
        ],
        compiler_params=pltpu.CompilerParams(vmem_limit_bytes=24 * 2**20),
        name="project",
    )(blocks, own, arrived)


def weight_kernel(back, theirs, own, arrived, blocks, grads):
    c = lax.axis_index("c")
    chips, _, patches, columns = back.shape
    head = columns // 4
    count = chips * patches
    rows = blocks.shape[1]
    for index, frame in ((0, c), (1, 1 - c)):
        for half in range(2):
            value = jnp.where(c == half, back[:, frame].astype(F32), theirs[:, frame].astype(F32))
            grads[index, half * count : (half + 1) * count] = value.reshape(count, columns).astype(BF)
    contract = (((0,), (0,)), ((), ()))
    wide = NX * 2 * rows
    parts = []
    for yl in range(NYL):
        at = slice(yl * wide, (yl + 1) * wide)
        first, second = 0.0, 0.0
        for index, tokens in ((0, own), (1, arrived)):
            first = first + lax.dot_general(
                tokens[0, :, at], grads[index, :, head:], contract, preferred_element_type=F32
            )
            second = second + lax.dot_general(
                tokens[1, :, at], grads[index, :, :head], contract, preferred_element_type=F32
            )
        parts.append((first.astype(BF), second.astype(BF)))
    for yl, x, half, even, odd in half_shards():
        to = jnp.where(c == 0, even, odd)
        at = slice((x * 2 + half) * rows, (x * 2 + half + 1) * rows)
        blocks[to, :, : 3 * head] = parts[yl][0][at]
        blocks[to, :, 3 * head :] = parts[yl][1][at]


def weight_parts(back, theirs, own, arrived):
    _, tokens, width = own.shape
    columns = back.shape[-1]
    count = NYL * NX * 2
    return pl.pallas_call(
        weight_kernel,
        out_shape=jax.ShapeDtypeStruct((count, width // count, columns), BF),
        in_specs=[VMEM] * 4,
        out_specs=VMEM,
        scratch_shapes=[pltpu.VMEM((2, tokens, columns), BF)],
        compiler_params=pltpu.CompilerParams(vmem_limit_bytes=32 * 2**20),
        name="weight_parts",
    )(back, theirs, own, arrived)


def attend_block(packed):
    head = packed.shape[-1] // 4
    scale = 1.0 / head**0.5
    query = packed[..., :head]
    keys = packed[..., head : 2 * head]
    values = packed[..., 2 * head : 3 * head]
    grad_out = packed[..., 3 * head :]
    scores = jnp.einsum("fpd,gpd->pfg", query, keys, preferred_element_type=F32) * scale
    probs = jax.nn.softmax(scores, axis=-1)
    probs_b = probs.astype(BF)
    out = jnp.einsum("pfg,gpd->fpd", probs_b, values, preferred_element_type=F32).astype(BF)
    grad_v = jnp.einsum("pfg,fpd->gpd", probs_b, grad_out, preferred_element_type=F32).astype(BF)
    grad_probs = jnp.einsum("fpd,gpd->pfg", grad_out, values, preferred_element_type=F32)
    delta = jnp.sum(grad_out.astype(F32) * out.astype(F32), axis=-1)
    grad_scores = (probs * (grad_probs - jnp.transpose(delta)[:, :, None])).astype(BF)
    grad_q = (jnp.einsum("pfg,gpd->fpd", grad_scores, keys, preferred_element_type=F32) * scale).astype(BF)
    grad_k = (jnp.einsum("pfg,fpd->gpd", grad_scores, query, preferred_element_type=F32) * scale).astype(BF)
    return jnp.concatenate([out, grad_q, grad_k, grad_v], axis=-1)


def gather(weights):
    rows, columns = weights.shape
    half = lax.dynamic_slice_in_dim(weights, lax.rem(lax.axis_index("z"), 2) * (rows // 2), rows // 2)
    eight = exchange(jnp.broadcast_to(half[None], (8, rows // 2, columns)), LIGHT)
    blocks = exchange(jnp.broadcast_to(eight[None], (4, *eight.shape)), HEAVY)
    return blocks.reshape(32, rows // 2, columns)


def reduce(blocks):
    _, rows, columns = blocks.shape
    heavy = exchange(blocks.reshape(4, 8, rows, columns), HEAVY)
    eight = jnp.sum(heavy.astype(F32), axis=0).astype(BF)
    pieces = eight.reshape(8, rows, 4, columns // 4).transpose(0, 2, 1, 3).reshape(32, rows, columns // 4)
    piece = jnp.sum(exchange(pieces, SPREAD).astype(F32), axis=0).astype(BF)
    copies = jnp.broadcast_to(piece[None], (NZ * NYH, *piece.shape))
    copies = lax.all_to_all(copies, ("z", "yh"), split_axis=0, concat_axis=0, tiled=True)
    copies = copies.reshape(4, 2, NYH, rows, columns // 4).astype(F32)
    return jnp.sum(copies, axis=2).transpose(1, 2, 0, 3).reshape(2 * rows, columns)


def shards(latents, cotangent, weights):
    width = latents.shape[-1]
    columns = weights.shape[1]
    own, away = prepare(latents.reshape(-1, width), cotangent.reshape(-1, width))
    arrived = other_core(away)
    blocks = gather(weights)
    mine, theirs = project(blocks, own, arrived)
    packed = (mine + other_core(theirs)).astype(BF)
    plane = ("yl", "x")
    packed = lax.all_to_all(packed, plane, split_axis=0, concat_axis=0, tiled=True)
    result = attend_block(packed.reshape(-1, *packed.shape[2:]))
    back = lax.all_to_all(result.reshape(packed.shape), plane, split_axis=0, concat_axis=0, tiled=True)
    return reduce(weight_parts(back, other_core(back), own, arrived))


def solution(mesh):
    fine = Mesh(mesh.devices.reshape(NZ, NYH, NYL, NX, NC), AXES)
    dp, seq = ("z", "yh"), ("yl", "x", "c")
    placed = (P(dp, seq, None, None), P(dp, seq, None, None), P(seq, None))
    return jax.shard_map(shards, mesh=fine, in_specs=placed, out_specs=P(seq, None), check_vma=False)
```

time: 156 us -> 151 us (0.968)
  blocking collectives: 83.6 us -> 106 us
  starting transfers between devices: 36.4 us -> 15.6 us
  waiting for transfers between devices: 19.8 us -> 5.67 us
  local copies, waits for them, and re-layouts: 2.83 us -> 9.37 us
    ppermute x8 -> x0, starting transfers between devices: 27.5 us -> none  [send(): return lax.ppermute(v, AXES, heavy_pairs(step))]
    all_to_all x2 -> x3, blocking collectives: 36.3 us -> 60.9 us  [exchange(): lax.all_to_all(v, AXES, split_axis=0, concat_axis=0, axis_index_groups=me...]
    ppermute x8 -> x0, waiting for transfers between devices: 13.6 us -> none  [send(): return lax.ppermute(v, AXES, heavy_pairs(step))]
    unnamed x11 -> x15, local copies, waits for them, and re-layouts: 0.79 us -> 6.97 us
    all_to_all x0 -> x1, starting transfers between devices: none -> 3.6 us  [exchange(): lax.all_to_all(v, AXES, split_axis=0, concat_axis=0, axis_index_groups=me...]
    ppermute x2 -> x3, starting transfers between devices: 8.98 us -> 12 us  [other_core(): return lax.ppermute(v, 'c', [(0, 1), (1, 0)])]
    all_to_all x2, blocking collectives: 28.9 us -> 26.6 us  [the longest x1 13.4 us: shards(): lax.all_to_all(packed, plane, split_axis=0, concat_axis=0, tiled=True)]
    ppermute x2 -> x3, waiting for transfers between devices: 6.17 us -> 5.67 us  [other_core(): return lax.ppermute(v, 'c', [(0, 1), (1, 0)])]
  transfers between devices with their start and end apart: 10 -> 4, of which waited for: 6 -> 3; matrix products, arithmetic and copies ran while one was open for 0% -> 0% of each run, Pallas kernels for 0% -> 2%
where the time goes in v2:
time: 151 us; the launch traced here: 150 us
  blocking collectives  106 us (70%)
  starting transfers between devices  15.6 us (10%)
  local copies, waits for them, and re-layouts  9.37 us (6%)
  Pallas kernels  8.46 us (6%)
  waiting for transfers between devices  5.67 us (4%)
  matrix products  4.08 us (3%)
    all_to_all x3, blocking collectives, exchange(): lax.all_to_all(v, AXES, split_axis=0, concat_axis=0, axis_index_groups=me...  60.9 us
    all_to_all x1, blocking collectives, reduce(): lax.all_to_all(copies, ('z', 'yh'), split_axis=0, concat_axis=0, tiled=True)  18.8 us
    all_to_all x1, blocking collectives, shards(): lax.all_to_all(packed, plane, split_axis=0, concat_axis=0, tiled=True)  13.4 us
    all_to_all x1, blocking collectives, shards(): lax.all_to_all(result.reshape(packed.shape), plane, split_axis=0, concat_...  13.2 us
    ppermute x3, starting transfers between devices, other_core(): return lax.ppermute(v, 'c', [(0, 1), (1, 0)])  12 us
    unnamed x15, local copies, waits for them, and re-layouts  6.97 us
    ppermute x3, waiting for transfers between devices, other_core(): return lax.ppermute(v, 'c', [(0, 1), (1, 0)])  5.67 us
    pallas_call x1, Pallas kernels, project(): pl.pallas_call(project_kernel, out_shape=(shape, shape), in_specs=[ANY, V...  4 us
  transfers between devices with their start and end apart: 4, of which 3 were waited for; matrix products, arithmetic and copies ran while one was open for 0% of the time, Pallas kernels for 2%

profile of v2, /device:TPU:1, one launch (start us, length us, event | category | flops | bytes accessed | tf_op | source)
XLA Modules:
  0.0 150.2 jit_solution(15027379190265169062)
XLA Ops:
  0.0 0.9 copy-done
  0.9 19.2 %all_to_all.35 = bf16[8,48,512]{2,1,0:T(8,128)(2,1)S(1)} all-to-all(bf16[8,48,512]{2,1,0:T(8,128)(2,1)S(1)} %broadcast_in_dim.6), channel_id=1, replica_groups={{0,64,8,72,16,80,24,88},{1,3,5,7,17,19,21,23},{2,66,10,74,18,82,26,90},..., dimensions={0} | all-to-all | bytes 786432 | tf_op jit(solution)/shard_map/all_to_all | solution.py:53
  20.1 1.3 broadcast_in_dim.7
  21.5 3.6 %all-to-all-start.1 = ((bf16[4,8,48,512]{3,2,1,0:T(8,128)(2,1)}), bf16[4,8,48,512]{3,2,1,0:T(8,128)(2,1)S(1)}, u32[]{:S(2)}, u32[]{:S(2)}) async-start(bf16[4,8,48,512]{3,2,1,0:T(8,128)(2,1)} %broadcast_in_dim.7), calls=%async_computation.1 | async-start | bytes 3145728 | tf_op jit(solution)/shard_map/all_to_all | solution.py:53
  25.1 1.4 copy-done.4
  26.5 1.4 copy-done.5
  27.9 3.0 %prepare.1 = (bf16[2,256,1536]{2,1,0:T(8,128)(2,1)S(1)}, bf16[2,256,1536]{2,1,0:T(8,128)(2,1)S(1)}) custom-call(bf16[256,3072]{1,0:T(8,128)(2,1)S(1)} %bitcast.29, bf16[256,3072]{1,0:T(8,128)(2,1)S(1)} %bitcast.30), custom_call_target="tpu_custom_call" | custom-call | tf_op jit(solution)/shard_map/prepare/pallas_call | solution.py:90
  30.9 3.9 %collective-permute-start = (bf16[2,256,1536]{2,1,0:T(8,128)(2,1)S(1)}, bf16[2,256,1536]{2,1,0:T(8,128)(2,1)S(1)}, u32[]{:S(2)}, u32[]{:S(2)}) collective-permute-start(bf16[2,256,1536]{2,1,0:T(8,128)(2,1)S(1)} %get-tuple-element.10), channel_id=1, source_target_pairs={{0,1},{1,0},{2,3},{3,2},{4,5},{5,4},{6,7},{7,6},{8,9},{9,8},{10,11... | collective-permute-start | bytes 4718600 | tf_op jit(solution)/shard_map/ppermute | solution.py:49
  34.8 3.0 %collective-permute-done.arrived = bf16[2,256,1536]{2,1,0:T(8,128)(2,1)S(1)} collective-permute-done((bf16[2,256,1536]{2,1,0:T(8,128)(2,1)S(1)}, bf16[2,256,1536]{2,1,0:T(8,128)(2,1)S(1)}, u32[]{:S(2)}, u32[]{:S(2)}) %collective-permute-start) | collective-permute-done | bytes 1572896 | tf_op jit(solution)/shard_map/ppermute | solution.py:49
  37.8 1.2 copy-done.1
  39.0 1.4 copy-done.2
  40.4 4.0 %project.1 = (f32[16,2,8,512]{3,2,1,0:T(8,128)S(1)}, f32[16,2,8,512]{3,2,1,0:T(8,128)S(1)}) custom-call(bf16[32,48,512]{2,1,0:T(8,128)(2,1)S(1)} %bitcast.27, bf16[2,256,1536]{2,1,0:T(8,128)(2,1)S(1)} %get-tuple-element.9.own, bf16[2,256,1536]{2,1,0:T(8,128)(2,1)S(1)} %copy-done.2), custom_call_target="tpu_custom_call" | custom-call | tf_op jit(solution)/shard_map/project/pallas_call | solution.py:131
  44.4 3.7 %collective-permute-start.1 = (f32[16,2,8,512]{3,2,1,0:T(8,128)S(1)}, f32[16,2,8,512]{3,2,1,0:T(8,128)S(1)}, u32[]{:S(2)}, u32[]{:S(2)}) collective-permute-start(f32[16,2,8,512]{3,2,1,0:T(8,128)S(1)} %get-tuple-element.12), channel_id=1, source_target_pairs={{0,1},{1,0},{2,3},{3,2},{4,5},{5,4},{6,7},{7,6},{8,9},{9,8},{10,11... | collective-permute-start | bytes 1572872 | tf_op jit(solution)/shard_map/ppermute | solution.py:49
  48.1 1.5 %collective-permute-done.1 = f32[16,2,8,512]{3,2,1,0:T(8,128)S(1)} collective-permute-done((f32[16,2,8,512]{3,2,1,0:T(8,128)S(1)}, f32[16,2,8,512]{3,2,1,0:T(8,128)S(1)}, u32[]{:S(2)}, u32[]{:S(2)}) %collective-permute-start.1) | collective-permute-done | bytes 524320 | tf_op jit(solution)/shard_map/ppermute | solution.py:49
  49.7 13.4 %all_to_all.36 = bf16[16,2,8,512]{3,2,1,0:T(8,128)(2,1)S(1)} all-to-all(bf16[16,2,8,512]{3,2,1,0:T(8,128)(2,1)S(1)} %add_convert_fusion), channel_id=1, replica_groups=mesh['z'=8,'yh'=2,'yl'=4,'x'=4,'c'=2] {'yl','x'}, dimensions={0} | all-to-all | bytes 524288 | tf_op jit(solution)/shard_map/all_to_all | solution.py:241
  65.0 1.4 multiply_reduce_fusion
  66.4 1.1 fusion.4
  68.1 13.2 %all_to_all.37.back = bf16[16,2,8,512]{3,2,1,0:T(8,128)(2,1)S(1)} all-to-all(bf16[16,2,8,512]{3,2,1,0:T(8,128)(2,1)S(1)} %bitcast.33), channel_id=1, replica_groups=mesh['z'=8,'yh'=2,'yl'=4,'x'=4,'c'=2] {'yl','x'}, dimensions={0} | all-to-all | bytes 524288 | tf_op jit(solution)/shard_map/all_to_all | solution.py:243
  81.3 4.4 %collective-permute-start.2 = (bf16[16,2,8,512]{3,2,1,0:T(8,128)(2,1)S(1)}, bf16[16,2,8,512]{3,2,1,0:T(8,128)(2,1)S(1)}, u32[]{:S(2)}, u32[]{:S(2)}) collective-permute-start(bf16[16,2,8,512]{3,2,1,0:T(8,128)(2,1)S(1)} %all_to_all.37.back), channel_id=1, source_target_pairs={{0,1},{1,0},{2,3},{3,2},{4,5},{5,4},{6,7},{7,6},{8,9},{9,8},{10,11... | collective-permute-start | bytes 786440 | tf_op jit(solution)/shard_map/ppermute | solution.py:49
  85.7 1.1 collective-permute-done.2.theirs
  86.8 1.5 weight_parts.1
  88.3 14.3 %all_to_all.38 = bf16[4,8,48,512]{3,2,1,0:T(8,128)(2,1)S(1)} all-to-all(bf16[4,8,48,512]{3,2,1,0:T(8,128)(2,1)S(1)} %bitcast.28), channel_id=1, replica_groups={{0,2,4,6},{1,65,9,73},{3,67,11,75},{5,69,13,77},{7,71,15,79},{8,10,12,1..., dimensions={0} | all-to-all | bytes 3145728 | tf_op jit(solution)/shard_map/all_to_all | solution.py:53
  103.1 27.4 %all_to_all.39 = bf16[32,48,128]{2,1,0:T(8,128)(2,1)S(1)} all-to-all(bf16[32,48,128]{2,1,0:T(8,128)(2,1)S(1)} %bitcast.31), channel_id=1, replica_groups={{0,128,256,384,64,192,320,448,8,136,264,392,72,200,328,456,16,144,272,4..., dimensions={0} | all-to-all | bytes 786432 | tf_op jit(solution)/shard_map/all_to_all | solution.py:53
  130.6 18.8 %all_to_all.40 = bf16[16,48,128]{2,1,0:T(8,128)(2,1)S(1)} all-to-all(bf16[16,48,128]{2,1,0:T(8,128)(2,1)S(1)} %broadcast_in_dim.8), channel_id=1, replica_groups=mesh['z'=8,'yh'=2,'yl'=4,'x'=4,'c'=2] {'z','yh'}, dimensions={0} | all-to-all | bytes 393216 | tf_op jit(solution)/shard_map/all_to_all | solution.py:227
  (28 shorter events, 3.9 us)
Async XLA Ops:
  0.0 0.9 copy-start
  21.5 17.5 %all-to-all-start.1 = ((bf16[4,8,48,512]{3,2,1,0:T(8,128)(2,1)}), bf16[4,8,48,512]{3,2,1,0:T(8,128)(2,1)S(1)}, u32[]{:S(2)}, u32[]{:S(2)}) async-start(bf16[4,8,48,512]{3,2,1,0:T(8,128)(2,1)} %broadcast_in_dim.7), calls=%async_computation.1 | async-start | bytes 3145728 | tf_op jit(solution)/shard_map/all_to_all | solution.py:53
  25.1 1.4 copy-start.4
  26.5 1.4 copy-start.5
  30.9 7.0 %collective-permute-start = (bf16[2,256,1536]{2,1,0:T(8,128)(2,1)S(1)}, bf16[2,256,1536]{2,1,0:T(8,128)(2,1)S(1)}, u32[]{:S(2)}, u32[]{:S(2)}) collective-permute-start(bf16[2,256,1536]{2,1,0:T(8,128)(2,1)S(1)} %get-tuple-element.10), channel_id=1, source_target_pairs={{0,1},{1,0},{2,3},{3,2},{4,5},{5,4},{6,7},{7,6},{8,9},{9,8},{10,11... | collective-permute-start | bytes 4718600 | tf_op jit(solution)/shard_map/ppermute | solution.py:49
  37.8 1.2 copy-start.1
  39.0 1.4 copy-start.2
  44.4 5.2 %collective-permute-start.1 = (f32[16,2,8,512]{3,2,1,0:T(8,128)S(1)}, f32[16,2,8,512]{3,2,1,0:T(8,128)S(1)}, u32[]{:S(2)}, u32[]{:S(2)}) collective-permute-start(f32[16,2,8,512]{3,2,1,0:T(8,128)S(1)} %get-tuple-element.12), channel_id=1, source_target_pairs={{0,1},{1,0},{2,3},{3,2},{4,5},{5,4},{6,7},{7,6},{8,9},{9,8},{10,11... | collective-permute-start | bytes 1572872 | tf_op jit(solution)/shard_map/ppermute | solution.py:49
  63.8 1.2 copy-start.6
  64.9 21.9 %copy-start.3 = (bf16[2,256,1536]{2,1,0:T(8,128)(2,1)S(1)}, bf16[2,256,1536]{2,1,0:T(8,128)(2,1)}, u32[]{:S(2)}) copy-start(bf16[2,256,1536]{2,1,0:T(8,128)(2,1)} %copy-done.1) | copy-start | bytes 4718596
  81.3 5.5 %collective-permute-start.2 = (bf16[16,2,8,512]{3,2,1,0:T(8,128)(2,1)S(1)}, bf16[16,2,8,512]{3,2,1,0:T(8,128)(2,1)S(1)}, u32[]{:S(2)}, u32[]{:S(2)}) collective-permute-start(bf16[16,2,8,512]{3,2,1,0:T(8,128)(2,1)S(1)} %all_to_all.37.back), channel_id=1, source_target_pairs={{0,1},{1,0},{2,3},{3,2},{4,5},{5,4},{6,7},{7,6},{8,9},{9,8},{10,11... | collective-permute-start | bytes 786440 | tf_op jit(solution)/shard_map/ppermute | solution.py:49

commit v3 on v2

--- a/solution.py
+++ b/solution.py
@@ -13,7 +13,7 @@
 BF = jnp.bfloat16
 F32 = jnp.float32
 VMEM = pl.BlockSpec(memory_space=pltpu.VMEM)
-ANY = pl.BlockSpec(memory_space=pl.ANY)
+LIMIT = 16 * 2**20
 
 
 def device(z, yh, yl, x, c):
@@ -92,35 +92,30 @@
         out_shape=(shape, shape),
         in_specs=[VMEM] * 2,
         out_specs=(VMEM,) * 2,
-        compiler_params=pltpu.CompilerParams(vmem_limit_bytes=24 * 2**20),
+        compiler_params=pltpu.CompilerParams(vmem_limit_bytes=LIMIT),
         name="prepare",
     )(lat, cot)
 
 
-def project_kernel(blocks, own, arrived, mine, theirs, w, sums, sems):
+def project_kernel(blocks, own, arrived, mine, theirs, w):
     c = lax.axis_index("c")
     rows = blocks.shape[1]
-    copies = []
     for yl, x, half, even, odd in half_shards():
         place = (yl * NX + x) * 2 + half
-        copies.append(
-            pltpu.make_async_copy(
-                blocks.at[jnp.where(c == 0, even, odd)], w.at[pl.ds(place * rows, rows)], sems.at[place]
-            )
-        )
-    for copy in copies:
-        copy.start()
-    for copy in copies:
-        copy.wait()
+        w[place * rows : (place + 1) * rows] = blocks[jnp.where(c == 0, even, odd)]
     head = w.shape[1] // 4
-    for index, tokens in ((0, own), (1, arrived)):
-        sums[index, :, : 3 * head] = jnp.dot(tokens[0], w[:, : 3 * head], preferred_element_type=F32)
-        sums[index, :, 3 * head :] = jnp.dot(tokens[1], w[:, 3 * head :], preferred_element_type=F32)
     count = own.shape[1] // 2
-    for index, frame in ((0, c), (1, 1 - c)):
-        for to, half in ((mine, c), (theirs, 1 - c)):
-            value = sums[index, pl.ds(pl.multiple_of(half * count, 128), count), :]
-            to[:, frame] = value.reshape(to.shape[0], to.shape[2], to.shape[3])
+    shape = (mine.shape[0], mine.shape[2], 3 * head), (mine.shape[0], mine.shape[2], head)
+    for tokens, frame in ((own, c), (arrived, 1 - c)):
+        first = jnp.dot(tokens[0], w[:, : 3 * head], preferred_element_type=F32)
+        second = jnp.dot(tokens[1], w[:, 3 * head :], preferred_element_type=F32)
+        for value, at, to in (
+            (first, slice(0, 3 * head), shape[0]),
+            (second, slice(3 * head, 4 * head), shape[1]),
+        ):
+            low, high = value[:count], value[count:]
+            mine[:, frame, :, at] = jnp.where(c == 0, low, high).reshape(to)
+            theirs[:, frame, :, at] = jnp.where(c == 0, high, low).reshape(to)
 
 
 def project(blocks, own, arrived):
@@ -131,14 +126,10 @@
     return pl.pallas_call(
         project_kernel,
         out_shape=(shape, shape),
-        in_specs=[ANY, VMEM, VMEM],
+        in_specs=[VMEM] * 3,
         out_specs=(VMEM, VMEM),
-        scratch_shapes=[
-            pltpu.VMEM((width, columns), BF),
-            pltpu.VMEM((2, tokens, columns), F32),
-            pltpu.SemaphoreType.DMA((NYL * NX * 2,)),
-        ],
-        compiler_params=pltpu.CompilerParams(vmem_limit_bytes=24 * 2**20),
+        scratch_shapes=[pltpu.VMEM((width, columns), BF)],
+        compiler_params=pltpu.CompilerParams(vmem_limit_bytes=LIMIT),
         name="project",
     )(blocks, own, arrived)
 
@@ -184,37 +175,57 @@
         in_specs=[VMEM] * 4,
         out_specs=VMEM,
         scratch_shapes=[pltpu.VMEM((2, tokens, columns), BF)],
-        compiler_params=pltpu.CompilerParams(vmem_limit_bytes=32 * 2**20),
+        compiler_params=pltpu.CompilerParams(vmem_limit_bytes=LIMIT),
         name="weight_parts",
     )(back, theirs, own, arrived)
 
 
-def attend_block(packed):
-    head = packed.shape[-1] // 4
+def attend_kernel(packed, result):
+    tokens, columns = packed.shape
+    head = columns // 4
     scale = 1.0 / head**0.5
-    query = packed[..., :head]
-    keys = packed[..., head : 2 * head]
-    values = packed[..., 2 * head : 3 * head]
-    grad_out = packed[..., 3 * head :]
-    scores = jnp.einsum("fpd,gpd->pfg", query, keys, preferred_element_type=F32) * scale
-    probs = jax.nn.softmax(scores, axis=-1)
+    patches = tokens // (NYL * NX * NC)
+    query, keys, values, grad_out = (packed[:, i * head : (i + 1) * head] for i in range(4))
+    row = lax.broadcasted_iota(jnp.int32, (tokens, tokens), 0)
+    column = lax.broadcasted_iota(jnp.int32, (tokens, tokens), 1)
+    same = lax.rem(row, patches) == lax.rem(column, patches)
+    across, down = (((1,), (1,)), ((), ())), (((0,), (0,)), ((), ()))
+    scores = lax.dot_general(query, keys, across, preferred_element_type=F32) * scale
+    scores = jnp.where(same, scores, -jnp.inf)
+    weights = jnp.exp(scores - jnp.max(scores, axis=-1, keepdims=True))
+    probs = weights / jnp.sum(weights, axis=-1, keepdims=True)
     probs_b = probs.astype(BF)
-    out = jnp.einsum("pfg,gpd->fpd", probs_b, values, preferred_element_type=F32).astype(BF)
-    grad_v = jnp.einsum("pfg,fpd->gpd", probs_b, grad_out, preferred_element_type=F32).astype(BF)
-    grad_probs = jnp.einsum("fpd,gpd->pfg", grad_out, values, preferred_element_type=F32)
-    delta = jnp.sum(grad_out.astype(F32) * out.astype(F32), axis=-1)
-    grad_scores = (probs * (grad_probs - jnp.transpose(delta)[:, :, None])).astype(BF)
-    grad_q = (jnp.einsum("pfg,gpd->fpd", grad_scores, keys, preferred_element_type=F32) * scale).astype(BF)
-    grad_k = (jnp.einsum("pfg,fpd->gpd", grad_scores, query, preferred_element_type=F32) * scale).astype(BF)
-    return jnp.concatenate([out, grad_q, grad_k, grad_v], axis=-1)
-
-
-def gather(weights):
+    out = jnp.dot(probs_b, values, preferred_element_type=F32).astype(BF)
+    result[:, :head] = out
+    grad_v = lax.dot_general(probs_b, grad_out, down, preferred_element_type=F32)
+    result[:, 3 * head :] = grad_v.astype(BF)
+    grad_probs = lax.dot_general(grad_out, values, across, preferred_element_type=F32)
+    delta = jnp.sum(grad_out.astype(F32) * out.astype(F32), axis=-1, keepdims=True)
+    grad_scores = jnp.where(same, probs * (grad_probs - delta), 0.0).astype(BF)
+    grad_q = jnp.dot(grad_scores, keys, preferred_element_type=F32) * scale
+    result[:, head : 2 * head] = grad_q.astype(BF)
+    grad_k = lax.dot_general(grad_scores, query, down, preferred_element_type=F32) * scale
+    result[:, 2 * head : 3 * head] = grad_k.astype(BF)
+
+
+def attend(packed):
+    return pl.pallas_call(
+        attend_kernel,
+        out_shape=jax.ShapeDtypeStruct(packed.shape, BF),
+        in_specs=[VMEM],
+        out_specs=VMEM,
+        compiler_params=pltpu.CompilerParams(vmem_limit_bytes=LIMIT),
+        name="attend",
+    )(packed)
+
+
+def gather(weights, own):
     rows, columns = weights.shape
     half = lax.dynamic_slice_in_dim(weights, lax.rem(lax.axis_index("z"), 2) * (rows // 2), rows // 2)
     eight = exchange(jnp.broadcast_to(half[None], (8, rows // 2, columns)), LIGHT)
+    eight, own = lax.optimization_barrier((eight, own))
     blocks = exchange(jnp.broadcast_to(eight[None], (4, *eight.shape)), HEAVY)
-    return blocks.reshape(32, rows // 2, columns)
+    return blocks.reshape(32, rows // 2, columns), own
 
 
 def reduce(blocks):
@@ -234,12 +245,12 @@
     columns = weights.shape[1]
     own, away = prepare(latents.reshape(-1, width), cotangent.reshape(-1, width))
     arrived = other_core(away)
-    blocks = gather(weights)
+    blocks, own = gather(weights, own)
     mine, theirs = project(blocks, own, arrived)
     packed = (mine + other_core(theirs)).astype(BF)
     plane = ("yl", "x")
     packed = lax.all_to_all(packed, plane, split_axis=0, concat_axis=0, tiled=True)
-    result = attend_block(packed.reshape(-1, *packed.shape[2:]))
+    result = attend(packed.reshape(-1, columns))
     back = lax.all_to_all(result.reshape(packed.shape), plane, split_axis=0, concat_axis=0, tiled=True)
     return reduce(weight_parts(back, other_core(back), own, arrived))
 

time: 151 us -> 145 us (0.960)
  blocking collectives: 106 us -> 87.9 us
  starting transfers between devices: 15.6 us -> 24.8 us
  waiting for transfers between devices: 5.67 us -> 13.6 us
  matrix products: 4.08 us -> 0 us
  Pallas kernels: 8.46 us -> 6.72 us
    all_to_all x3 -> x2, blocking collectives: 60.9 us -> 42.2 us  [exchange(): lax.all_to_all(v, AXES, split_axis=0, concat_axis=0, axis_index_groups=me...]
    all_to_all x1 -> x2, starting transfers between devices: 3.6 us -> 12.1 us  [exchange(): lax.all_to_all(v, AXES, split_axis=0, concat_axis=0, axis_index_groups=me...]
    all_to_all x1 -> x2, waiting for transfers between devices: 0.01 us -> 7.69 us  [exchange(): lax.all_to_all(v, AXES, split_axis=0, concat_axis=0, axis_index_groups=me...]
    dot_general x5 -> x0, matrix products: 3.24 us -> none  [the longest x1 1.44 us: attend_block(): jnp.einsum('pfg,gpd->fpd', probs_b, values, preferred_element_type=F32)]
    pallas_call x1 -> x2, Pallas kernels: 4 us -> 2.26 us  [the longest x1 1.4 us: project(): pl.pallas_call(project_kernel, out_shape=(shape, shape), in_specs=[VMEM]...]
  transfers between devices with their start and end apart: 4 -> 5, of which waited for: 3 -> 5; matrix products, arithmetic and copies ran while one was open for 0% -> 0% of each run, Pallas kernels for 2% -> 2%
where the time goes in v3:
time: 145 us; the launch traced here: 144 us
  blocking collectives  87.9 us (61%)
  starting transfers between devices  24.8 us (17%)
  waiting for transfers between devices  13.6 us (9%)
  local copies, waits for them, and re-layouts  10.4 us (7%)
  Pallas kernels  6.72 us (5%)
    all_to_all x2, blocking collectives, exchange(): lax.all_to_all(v, AXES, split_axis=0, concat_axis=0, axis_index_groups=me...  42.2 us
    all_to_all x1, blocking collectives, reduce(): lax.all_to_all(copies, ('z', 'yh'), split_axis=0, concat_axis=0, tiled=True)  19.3 us
    all_to_all x1, blocking collectives, shards(): lax.all_to_all(packed, plane, split_axis=0, concat_axis=0, tiled=True)  13.3 us
    all_to_all x1, blocking collectives, shards(): lax.all_to_all(result.reshape(packed.shape), plane, split_axis=0, concat_...  13.2 us
    ppermute x3, starting transfers between devices, other_core(): return lax.ppermute(v, 'c', [(0, 1), (1, 0)])  12.8 us
    all_to_all x2, starting transfers between devices, exchange(): lax.all_to_all(v, AXES, split_axis=0, concat_axis=0, axis_index_groups=me...  12.1 us
    unnamed x15, local copies, waits for them, and re-layouts  8.1 us
    all_to_all x2, waiting for transfers between devices, exchange(): lax.all_to_all(v, AXES, split_axis=0, concat_axis=0, axis_index_groups=me...  7.69 us
  transfers between devices with their start and end apart: 5, of which 5 were waited for; matrix products, arithmetic and copies ran while one was open for 0% of the time, Pallas kernels for 2%

profile of v3, /device:TPU:1, one launch (start us, length us, event | category | flops | bytes accessed | tf_op | source)
XLA Modules:
  0.0 144.2 jit_solution(4881386637773604922)
XLA Ops:
  1.7 6.9 %all-to-all-start = ((bf16[8,48,512]{2,1,0:T(8,128)(2,1)}), bf16[8,48,512]{2,1,0:T(8,128)(2,1)S(1)}, u32[]{:S(2)}, u32[]{:S(2)}) async-start(bf16[8,48,512]{2,1,0:T(8,128)(2,1)} %broadcast_in_dim.6), calls=%async_computation | async-start | bytes 786432 | tf_op jit(solution)/shard_map/all_to_all | solution.py:53
  8.6 1.4 copy-done.4
  10.0 1.4 copy-done.5
  11.4 3.0 %prepare.1 = (bf16[2,256,1536]{2,1,0:T(8,128)(2,1)S(1)}, bf16[2,256,1536]{2,1,0:T(8,128)(2,1)S(1)}) custom-call(bf16[256,3072]{1,0:T(8,128)(2,1)S(1)} %bitcast.18, bf16[256,3072]{1,0:T(8,128)(2,1)S(1)} %bitcast.19), custom_call_target="tpu_custom_call" | custom-call | tf_op jit(solution)/shard_map/prepare/pallas_call | solution.py:90
  14.4 1.1 copy-done.6
  15.5 3.3 %all-to-all-done = bf16[8,48,512]{2,1,0:T(8,128)(2,1)S(1)} async-done(((bf16[8,48,512]{2,1,0:T(8,128)(2,1)}), bf16[8,48,512]{2,1,0:T(8,128)(2,1)S(1)}, u32[]{:S(2)}, u32[]{:S(2)}) %all-to-all-start) | async-done | bytes 393248 | tf_op jit(solution)/shard_map/all_to_all | solution.py:53
  18.8 1.3 broadcast_in_dim.7
  20.1 5.2 %all-to-all-start.1 = ((bf16[4,8,48,512]{3,2,1,0:T(8,128)(2,1)}), bf16[4,8,48,512]{3,2,1,0:T(8,128)(2,1)S(1)}, u32[]{:S(2)}, u32[]{:S(2)}) async-start(bf16[4,8,48,512]{3,2,1,0:T(8,128)(2,1)} %broadcast_in_dim.7), calls=%async_computation.1 | async-start | bytes 3145728 | tf_op jit(solution)/shard_map/all_to_all | solution.py:53
  25.3 3.3 %collective-permute-start = (bf16[2,256,1536]{2,1,0:T(8,128)(2,1)}, bf16[2,256,1536]{2,1,0:T(8,128)(2,1)S(1)}, u32[]{:S(2)}, u32[]{:S(2)}) collective-permute-start(bf16[2,256,1536]{2,1,0:T(8,128)(2,1)} %copy-done.6), channel_id=1, source_target_pairs={{0,1},{1,0},{2,3},{3,2},{4,5},{5,4},{6,7},{7,6},{8,9},{9,8},{10,11... | collective-permute-start | bytes 4718600 | tf_op jit(solution)/shard_map/ppermute | solution.py:49
  28.7 3.2 %collective-permute-done.arrived = bf16[2,256,1536]{2,1,0:T(8,128)(2,1)S(1)} collective-permute-done((bf16[2,256,1536]{2,1,0:T(8,128)(2,1)}, bf16[2,256,1536]{2,1,0:T(8,128)(2,1)S(1)}, u32[]{:S(2)}, u32[]{:S(2)}) %collective-permute-start) | collective-permute-done | bytes 1572896 | tf_op jit(solution)/shard_map/ppermute | solution.py:49
  31.9 1.1 copy-done.1
  33.0 4.4 %all-to-all-done.1 = bf16[4,8,48,512]{3,2,1,0:T(8,128)(2,1)S(1)} async-done(((bf16[4,8,48,512]{3,2,1,0:T(8,128)(2,1)}), bf16[4,8,48,512]{3,2,1,0:T(8,128)(2,1)S(1)}, u32[]{:S(2)}, u32[]{:S(2)}) %all-to-all-start.1) | async-done | bytes 1572896 | tf_op jit(solution)/shard_map/all_to_all | solution.py:53
  37.5 1.4 copy-done.2
  38.9 1.4 project.1
  40.3 5.0 %collective-permute-start.1 = (f32[16,2,8,512]{3,2,1,0:T(8,128)S(1)}, f32[16,2,8,512]{3,2,1,0:T(8,128)S(1)}, u32[]{:S(2)}, u32[]{:S(2)}) collective-permute-start(f32[16,2,8,512]{3,2,1,0:T(8,128)S(1)} %get-tuple-element.16), channel_id=1, source_target_pairs={{0,1},{1,0},{2,3},{3,2},{4,5},{5,4},{6,7},{7,6},{8,9},{9,8},{10,11... | collective-permute-start | bytes 1572872 | tf_op jit(solution)/shard_map/ppermute | solution.py:49
  45.3 1.5 %collective-permute-done.1 = f32[16,2,8,512]{3,2,1,0:T(8,128)S(1)} collective-permute-done((f32[16,2,8,512]{3,2,1,0:T(8,128)S(1)}, f32[16,2,8,512]{3,2,1,0:T(8,128)S(1)}, u32[]{:S(2)}, u32[]{:S(2)}) %collective-permute-start.1) | collective-permute-done | bytes 524320 | tf_op jit(solution)/shard_map/ppermute | solution.py:49
  47.0 13.3 %all_to_all.35 = bf16[16,2,8,512]{3,2,1,0:T(8,128)(2,1)S(1)} all-to-all(bf16[16,2,8,512]{3,2,1,0:T(8,128)(2,1)S(1)} %add_convert_fusion), channel_id=1, replica_groups=mesh['z'=8,'yh'=2,'yl'=4,'x'=4,'c'=2] {'yl','x'}, dimensions={0} | all-to-all | bytes 524288 | tf_op jit(solution)/shard_map/all_to_all | solution.py:252
  61.1 13.2 %all_to_all.36.back = bf16[16,2,8,512]{3,2,1,0:T(8,128)(2,1)S(1)} all-to-all(bf16[16,2,8,512]{3,2,1,0:T(8,128)(2,1)S(1)} %bitcast.21), channel_id=1, replica_groups=mesh['z'=8,'yh'=2,'yl'=4,'x'=4,'c'=2] {'yl','x'}, dimensions={0} | all-to-all | bytes 524288 | tf_op jit(solution)/shard_map/all_to_all | solution.py:254
  74.2 4.4 %collective-permute-start.2 = (bf16[16,2,8,512]{3,2,1,0:T(8,128)(2,1)S(1)}, bf16[16,2,8,512]{3,2,1,0:T(8,128)(2,1)S(1)}, u32[]{:S(2)}, u32[]{:S(2)}) collective-permute-start(bf16[16,2,8,512]{3,2,1,0:T(8,128)(2,1)S(1)} %all_to_all.36.back), channel_id=1, source_target_pairs={{0,1},{1,0},{2,3},{3,2},{4,5},{5,4},{6,7},{7,6},{8,9},{9,8},{10,11... | collective-permute-start | bytes 786440 | tf_op jit(solution)/shard_map/ppermute | solution.py:49
  78.6 1.1 collective-permute-done.2.theirs
  79.8 1.5 %weight_parts.1 = bf16[32,48,512]{2,1,0:T(8,128)(2,1)S(1)} custom-call(bf16[16,2,8,512]{3,2,1,0:T(8,128)(2,1)S(1)} %all_to_all.36.back, bf16[16,2,8,512]{3,2,1,0:T(8,128)(2,1)S(1)} %collective-permute-done.2.theirs, bf16[2,256,1536]{2,1,0:T(8,128)(2,1)S(1)} %get-tuple-element.13.own, bf16[2,256,1536]{2,1,0:T(8,128)(2,1)S(1)} %copy-done.3), custom_call_target="tpu_custom_call" | custom-call | tf_op jit(solution)/shard_map/weight_parts/pallas_call | solution.py:172
  81.2 14.7 %all_to_all.37 = bf16[4,8,48,512]{3,2,1,0:T(8,128)(2,1)S(1)} all-to-all(bf16[4,8,48,512]{3,2,1,0:T(8,128)(2,1)S(1)} %bitcast.17), channel_id=1, replica_groups={{0,2,4,6},{1,65,9,73},{3,67,11,75},{5,69,13,77},{7,71,15,79},{8,10,12,1..., dimensions={0} | all-to-all | bytes 3145728 | tf_op jit(solution)/shard_map/all_to_all | solution.py:53
  96.4 27.5 %all_to_all.38 = bf16[32,48,128]{2,1,0:T(8,128)(2,1)S(1)} all-to-all(bf16[32,48,128]{2,1,0:T(8,128)(2,1)S(1)} %bitcast.22), channel_id=1, replica_groups={{0,128,256,384,64,192,320,448,8,136,264,392,72,200,328,456,16,144,272,4..., dimensions={0} | all-to-all | bytes 786432 | tf_op jit(solution)/shard_map/all_to_all | solution.py:53
  124.0 19.3 %all_to_all.39 = bf16[16,48,128]{2,1,0:T(8,128)(2,1)S(1)} all-to-all(bf16[16,48,128]{2,1,0:T(8,128)(2,1)S(1)} %broadcast_in_dim.8), channel_id=1, replica_groups=mesh['z'=8,'yh'=2,'yl'=4,'x'=4,'c'=2] {'z','yh'}, dimensions={0} | all-to-all | bytes 393216 | tf_op jit(solution)/shard_map/all_to_all | solution.py:238
  (21 shorter events, 4.0 us)
Async XLA Ops:
  0.0 0.9 copy-start
  1.7 17.1 %all-to-all-start = ((bf16[8,48,512]{2,1,0:T(8,128)(2,1)}), bf16[8,48,512]{2,1,0:T(8,128)(2,1)S(1)}, u32[]{:S(2)}, u32[]{:S(2)}) async-start(bf16[8,48,512]{2,1,0:T(8,128)(2,1)} %broadcast_in_dim.6), calls=%async_computation | async-start | bytes 786432 | tf_op jit(solution)/shard_map/all_to_all | solution.py:53
  8.5 1.4 copy-start.4
  10.0 1.4 copy-start.5
  14.4 1.2 copy-start.6
  20.1 17.3 %all-to-all-start.1 = ((bf16[4,8,48,512]{3,2,1,0:T(8,128)(2,1)}), bf16[4,8,48,512]{3,2,1,0:T(8,128)(2,1)S(1)}, u32[]{:S(2)}, u32[]{:S(2)}) async-start(bf16[4,8,48,512]{3,2,1,0:T(8,128)(2,1)} %broadcast_in_dim.7), calls=%async_computation.1 | async-start | bytes 3145728 | tf_op jit(solution)/shard_map/all_to_all | solution.py:53
  25.3 6.6 %collective-permute-start = (bf16[2,256,1536]{2,1,0:T(8,128)(2,1)}, bf16[2,256,1536]{2,1,0:T(8,128)(2,1)S(1)}, u32[]{:S(2)}, u32[]{:S(2)}) collective-permute-start(bf16[2,256,1536]{2,1,0:T(8,128)(2,1)} %copy-done.6), channel_id=1, source_target_pairs={{0,1},{1,0},{2,3},{3,2},{4,5},{5,4},{6,7},{7,6},{8,9},{9,8},{10,11... | collective-permute-start | bytes 4718600 | tf_op jit(solution)/shard_map/ppermute | solution.py:49
  31.9 1.2 copy-start.1
  37.5 1.4 copy-start.2
  40.3 39.5 %copy-start.3 = (bf16[2,256,1536]{2,1,0:T(8,128)(2,1)S(1)}, bf16[2,256,1536]{2,1,0:T(8,128)(2,1)}, u32[]{:S(2)}) copy-start(bf16[2,256,1536]{2,1,0:T(8,128)(2,1)} %copy-done.1) | copy-start | bytes 4718596
  40.3 6.6 %collective-permute-start.1 = (f32[16,2,8,512]{3,2,1,0:T(8,128)S(1)}, f32[16,2,8,512]{3,2,1,0:T(8,128)S(1)}, u32[]{:S(2)}, u32[]{:S(2)}) collective-permute-start(f32[16,2,8,512]{3,2,1,0:T(8,128)S(1)} %get-tuple-element.16), channel_id=1, source_target_pairs={{0,1},{1,0},{2,3},{3,2},{4,5},{5,4},{6,7},{7,6},{8,9},{9,8},{10,11... | collective-permute-start | bytes 1572872 | tf_op jit(solution)/shard_map/ppermute | solution.py:49
  74.2 5.5 %collective-permute-start.2 = (bf16[16,2,8,512]{3,2,1,0:T(8,128)(2,1)S(1)}, bf16[16,2,8,512]{3,2,1,0:T(8,128)(2,1)S(1)}, u32[]{:S(2)}, u32[]{:S(2)}) collective-permute-start(bf16[16,2,8,512]{3,2,1,0:T(8,128)(2,1)S(1)} %all_to_all.36.back), channel_id=1, source_target_pairs={{0,1},{1,0},{2,3},{3,2},{4,5},{5,4},{6,7},{7,6},{8,9},{9,8},{10,11... | collective-permute-start | bytes 786440 | tf_op jit(solution)/shard_map/ppermute | solution.py:49

commit v4 on v3

v4 whole, which is shorter than its diff:
```python
import functools
import itertools

import jax
import jax.numpy as jnp
from jax import lax
from jax.experimental import pallas as pl
from jax.experimental.pallas import tpu as pltpu
from jax.sharding import Mesh
from jax.sharding import PartitionSpec as P

NZ, NYH, NYL, NX, NC = 8, 2, 4, 4, 2
AXES = ("z", "yh", "yl", "x", "c")
BF = jnp.bfloat16
F32 = jnp.float32
VMEM = pl.BlockSpec(memory_space=pltpu.VMEM)
HBM = pl.BlockSpec(memory_space=pltpu.HBM)
LIMIT = 16 * 2**20


def device(z, yh, yl, x, c):
    return (((z * NYH + yh) * NYL + yl) * NX + x) * NC + c


def everyone():
    return itertools.product(range(NZ), range(NYH), range(NYL), range(NX), range(NC))


def groups(key, order):
    found = {}
    for at in everyone():
        found.setdefault(key(*at), []).append((order(*at), device(*at)))
    return [[d for _, d in sorted(members)] for members in found.values()]


def cube_groups(key, order):
    def named(names):
        def value(z, yh, yl, x, c):
            zs, ys, xs = (z + c) % NZ, (yh * NYL + yl + c) % (NYH * NYL), (x + c) % NX
            place = {"z1": zs // 2, "z0": zs % 2, "y2": ys // 4, "y1": ys // 2 % 2, "y0": ys % 2}
            place |= {"x1": xs // 2, "x0": xs % 2, "yl": yl, "x": x, "c": c}
            return tuple(place[name] for name in names)

        return value

    return groups(named(key), named(order))


LIGHT = cube_groups(("c", "z1", "z0", "y2", "y0", "x0"), ("y1", "x1"))
HEAVY = cube_groups(("c", "z1", "y2", "y1", "x1"), ("y0", "x0", "z0"))
SPREAD = cube_groups(("c", "y2", "y0", "x0", "z0"), ("y1", "x1", "z1"))
COPIES = cube_groups(("c", "yl", "x"), ("z1", "z0", "y2"))
PLANE = groups(
    lambda z, yh, yl, x, c: (z, yh, c),
    lambda z, yh, yl, x, c: ((yl + 2 * c) % NYL, (x + 2 * c) % NX),
)


def other_core(v):
    return lax.ppermute(v, "c", [(0, 1), (1, 0)])


def exchange(v, members):
    return lax.all_to_all(v, AXES, split_axis=0, concat_axis=0, axis_index_groups=members, tiled=True)


def half_shards():
    for yl, x, half in itertools.product(range(NYL), range(NX), range(2)):
        places = []
        for c in range(NC):
            ys, xs = (yl + c) % NYL, (x + c) % NX
            places.append((((ys % 2 * 2 + xs % 2) * 2 + half) * 2 + ys // 2) * 2 + xs // 2)
        yield yl, x, half, *places


def prepare_kernel(norm, value, own, away):
    c = lax.axis_index("c")
    width = value.shape[1]
    rows = width // (NYL * NX * NC)
    block = NX * NC * rows
    part = block // 2
    source = lax.broadcasted_iota(jnp.int32, (block, block), 0)
    k = lax.broadcasted_iota(jnp.int32, (block, block), 1)
    second = (k >= part).astype(jnp.int32)
    k = k - part * second
    wanted = k + rows * (second + c - 2 * c * second)
    for b in range(1, NX):
        wanted = wanted + rows * (k >= b * rows).astype(jnp.int32)
    pick = (source == wanted).astype(F32).astype(BF)
    if norm:
        wide = value[...].astype(F32)
        r = lax.rsqrt(jnp.mean(wide * wide, axis=-1, keepdims=True) + 1e-06)
    for a in range(NYL):
        tokens = value[:, a * block : (a + 1) * block]
        if norm:
            tokens = (tokens.astype(F32) * r).astype(BF)
        moved = jnp.dot(tokens, pick, preferred_element_type=F32).astype(BF)
        own[:, a * part : (a + 1) * part] = moved[:, :part]
        away[:, a * part : (a + 1) * part] = moved[:, part:]


def prepare(value, norm):
    tokens, width = value.shape
    shape = jax.ShapeDtypeStruct((tokens, width // 2), BF)
    return pl.pallas_call(
        functools.partial(prepare_kernel, norm),
        out_shape=(shape, shape),
        in_specs=[VMEM],
        out_specs=(VMEM, VMEM),
        compiler_params=pltpu.CompilerParams(vmem_limit_bytes=LIMIT),
        name="prepare",
    )(value)


def multiply(lat, cot, w, mine, theirs):
    c = lax.axis_index("c")
    head = w.shape[1] // 4
    count = lat.shape[0] // 2
    for tokens, at in ((lat, slice(0, 3 * head)), (cot, slice(3 * head, 4 * head))):
        value = jnp.dot(tokens[...], w[:, at], preferred_element_type=F32)
        to = (mine.shape[0], mine.shape[1], at.stop - at.start)
        low, high = value[:count], value[count:]
        mine[:, :, at] = jnp.where(c == 0, low, high).reshape(to)
        theirs[:, :, at] = jnp.where(c == 0, high, low).reshape(to).astype(BF)


def project_own_kernel(blocks, lat, cot, w, mine, theirs):
    c = lax.axis_index("c")
    rows = blocks.shape[1]
    for yl, x, half, even, odd in half_shards():
        place = (yl * NX + x) * 2 + half
        w[place * rows : (place + 1) * rows] = blocks[jnp.where(c == 0, even, odd)]
    multiply(lat, cot, w, mine, theirs)


def project_both_kernel(w, lat, cot, own_mine, own_theirs, mine, theirs, new_mine, new_theirs):
    c = lax.axis_index("c")
    multiply(lat, cot, w, new_mine, new_theirs)
    for own, new, to in ((own_mine, new_mine, mine), (own_theirs, new_theirs, theirs)):
        to[:, c] = own[...]
        to[:, 1 - c] = new[...]


def project(blocks, own_l, own_c, arr_l, arr_c):
    tokens, width = own_l.shape
    columns = blocks.shape[-1]
    chips = NYL * NX
    rows = tokens // (chips * NC)
    half, whole = (chips, rows, columns), (chips, NC, rows, columns)
    params = pltpu.CompilerParams(vmem_limit_bytes=LIMIT)
    w, mine, theirs = pl.pallas_call(
        project_own_kernel,
        out_shape=(
            jax.ShapeDtypeStruct((width, columns), BF),
            jax.ShapeDtypeStruct(half, F32),
            jax.ShapeDtypeStruct(half, BF),
        ),
        in_specs=[VMEM] * 3,
        out_specs=(VMEM,) * 3,
        compiler_params=params,
        name="project_own",
    )(blocks, own_l, own_c)
    return pl.pallas_call(
        project_both_kernel,
        out_shape=(jax.ShapeDtypeStruct(whole, F32), jax.ShapeDtypeStruct(whole, BF)),
        in_specs=[VMEM] * 5,
        out_specs=(VMEM,) * 2,
        scratch_shapes=[pltpu.VMEM(half, F32), pltpu.VMEM(half, BF)],
        compiler_params=params,
        name="project_both",
    )(w, arr_l, arr_c, mine, theirs)


def weight_kernel(columns, back, own, arrived, *rest):
    blocks, grads = rest[-2:]
    c = lax.axis_index("c")
    _, chips, _, patches, _ = back.shape
    count = chips * patches
    rows = blocks.shape[1]
    source, to = columns
    for index, frame in ((0, c), (1, 1 - c)):
        for half in range(2):
            value = back[half, :, frame, :, source].astype(F32)
            grads[index, half * count : (half + 1) * count] = value.reshape(count, -1).astype(BF)
    wide = NX * 2 * rows
    for yl in range(NYL):
        part = slice(yl * wide, (yl + 1) * wide)
        value = 0.0
        for index, tokens in ((0, own), (1, arrived)):
            value = value + lax.dot_general(
                tokens[:, part], grads[index], (((0,), (0,)), ((), ())), preferred_element_type=F32
            )
        value = value.astype(BF)
        for y, x, half, even, odd in half_shards():
            if y == yl:
                piece = value[(x * 2 + half) * rows : (x * 2 + half + 1) * rows]
                blocks[jnp.where(c == 0, even, odd), :, to] = piece


def weight_parts(back, own_l, own_c, arr_l, arr_c):
    tokens, width = own_l.shape
    columns = back.shape[-1]
    head = columns // 4
    count = NYL * NX * 2

    def call(source, to, own, arrived, *blocks):
        return pl.pallas_call(
            functools.partial(weight_kernel, (source, to)),
            out_shape=jax.ShapeDtypeStruct((count, width // count, columns), BF),
            in_specs=[VMEM] * (3 + len(blocks)),
            out_specs=VMEM,
            scratch_shapes=[pltpu.VMEM((2, tokens, source.stop - source.start), BF)],
            input_output_aliases={3: 0} if blocks else {},
            compiler_params=pltpu.CompilerParams(vmem_limit_bytes=LIMIT),
            name="weight_parts",
        )(back, own, arrived, *blocks)

    blocks = call(slice(head, 4 * head), slice(0, 3 * head), own_l, arr_l)
    return call(slice(0, head), slice(3 * head, 4 * head), own_c, arr_c, blocks)


def attend_kernel(packed, result):
    tokens, columns = packed.shape
    head = columns // 4
    scale = 1.0 / head**0.5
    patches = tokens // (NYL * NX * NC)
    query, keys, values, grad_out = (packed[:, i * head : (i + 1) * head] for i in range(4))
    row = lax.broadcasted_iota(jnp.int32, (tokens, tokens), 0)
    column = lax.broadcasted_iota(jnp.int32, (tokens, tokens), 1)
    same = lax.rem(row, patches) == lax.rem(column, patches)
    across, down = (((1,), (1,)), ((), ())), (((0,), (0,)), ((), ()))
    scores = lax.dot_general(query, keys, across, preferred_element_type=F32) * scale
    scores = jnp.where(same, scores, -jnp.inf)
    weights = jnp.exp(scores - jnp.max(scores, axis=-1, keepdims=True))
    probs = weights / jnp.sum(weights, axis=-1, keepdims=True)
    probs_b = probs.astype(BF)
    out = jnp.dot(probs_b, values, preferred_element_type=F32).astype(BF)
    result[:, :head] = out
    grad_v = lax.dot_general(probs_b, grad_out, down, preferred_element_type=F32)
    result[:, 3 * head :] = grad_v.astype(BF)
    grad_probs = lax.dot_general(grad_out, values, across, preferred_element_type=F32)
    delta = jnp.sum(grad_out.astype(F32) * out.astype(F32), axis=-1, keepdims=True)
    grad_scores = jnp.where(same, probs * (grad_probs - delta), 0.0).astype(BF)
    grad_q = jnp.dot(grad_scores, keys, preferred_element_type=F32) * scale
    result[:, head : 2 * head] = grad_q.astype(BF)
    grad_k = lax.dot_general(grad_scores, query, down, preferred_element_type=F32) * scale
    result[:, 2 * head : 3 * head] = grad_k.astype(BF)


def attend(packed):
    return pl.pallas_call(
        attend_kernel,
        out_shape=jax.ShapeDtypeStruct(packed.shape, BF),
        in_specs=[VMEM],
        out_specs=VMEM,
        compiler_params=pltpu.CompilerParams(vmem_limit_bytes=LIMIT),
        name="attend",
    )(packed)


def repeat_kernel(value, copies, sems):
    started = [pltpu.make_async_copy(value, copies.at[i], sems.at[i]) for i in range(copies.shape[0])]
    for copy in started:
        copy.start()
    for copy in started:
        copy.wait()


def repeat(value, count):
    return pl.pallas_call(
        repeat_kernel,
        out_shape=jax.ShapeDtypeStruct((count, *value.shape), value.dtype),
        in_specs=[VMEM],
        out_specs=HBM,
        scratch_shapes=[pltpu.SemaphoreType.DMA((count,))],
        compiler_params=pltpu.CompilerParams(vmem_limit_bytes=LIMIT),
        name="repeat",
    )(value)


def finish_kernel(copies, total):
    _, _, rows, columns = copies.shape
    for z1, z0 in itertools.product(range(NZ // 2), range(2)):
        index = z1 * 2 + z0
        value = copies[index, 0].astype(F32) + copies[index, 1].astype(F32)
        total[z0 * rows : (z0 + 1) * rows, z1 * columns : (z1 + 1) * columns] = value


def finish(copies):
    _, _, rows, columns = copies.shape
    return pl.pallas_call(
        finish_kernel,
        out_shape=jax.ShapeDtypeStruct((2 * rows, NZ // 2 * columns), F32),
        in_specs=[VMEM],
        out_specs=VMEM,
        compiler_params=pltpu.CompilerParams(vmem_limit_bytes=LIMIT),
        name="finish",
    )(copies)


def gather(weights, own):
    rows, columns = weights.shape
    z0 = lax.rem(lax.axis_index("z") + lax.axis_index("c"), 2)
    half = lax.dynamic_slice_in_dim(weights, z0 * (rows // 2), rows // 2)
    four = exchange(jnp.broadcast_to(half[None], (4, rows // 2, columns)), LIGHT)
    four, own = lax.optimization_barrier((four, own))
    blocks = exchange(repeat(four, 8), HEAVY)
    return blocks.reshape(32, rows // 2, columns), own


def reduce(blocks):
    _, rows, columns = blocks.shape
    heavy = exchange(blocks.reshape(8, 4, rows, columns), HEAVY)
    four = jnp.sum(heavy.astype(F32), axis=0).astype(BF)
    pieces = four.reshape(4, rows, 4, columns // 4).transpose(0, 2, 1, 3).reshape(16, rows, columns // 4)
    piece = jnp.sum(exchange(pieces, SPREAD).astype(F32), axis=0).astype(BF)
    copies = exchange(jnp.broadcast_to(piece[None], (NZ * NYH, *piece.shape)), COPIES)
    return finish(copies.reshape(NZ, NYH, *piece.shape))


def shards(latents, cotangent, weights):
    width = latents.shape[-1]
    columns = weights.shape[1]
    own_l, away_l = prepare(latents.reshape(-1, width), True)
    own_c, away_c = prepare(cotangent.reshape(-1, width), False)
    blocks, own_l = gather(weights, own_l)
    tokens = own_l, own_c, other_core(away_l), other_core(away_c)
    mine, theirs = project(blocks, *tokens)
    both = lax.all_gather(theirs, "c")
    part = lax.dynamic_index_in_dim(both, 1 - lax.axis_index("c"), keepdims=False)
    packed = exchange((mine + part.astype(F32)).astype(BF), PLANE)
    result = attend(packed.reshape(-1, columns))
    back = lax.all_gather(exchange(result.reshape(packed.shape), PLANE), "c")
    return reduce(weight_parts(back, *tokens))


def solution(mesh):
    fine = Mesh(mesh.devices.reshape(NZ, NYH, NYL, NX, NC), AXES)
    dp, seq = ("z", "yh"), ("yl", "x", "c")
    placed = (P(dp, seq, None, None), P(dp, seq, None, None), P(seq, None))
    return jax.shard_map(shards, mesh=fine, in_specs=placed, out_specs=P(seq, None), check_vma=False)
```

time: 145 us -> 137 us (0.945); the launches traced: 144 us -> 134 us
  waiting for transfers between devices: 13.6 us -> 2.45 us
  Pallas kernels: 6.72 us -> 11 us
  blocking collectives: 87.9 us -> 83.8 us
  starting transfers between devices: 24.8 us -> 27.8 us
  local copies, waits for them, and re-layouts: 10.4 us -> 8.6 us
    all_to_all x3 -> x0, blocking collectives: 45.8 us -> none  [the longest x1 19.3 us: reduce(): lax.all_to_all(copies, ('z', 'yh'), split_axis=0, concat_axis=0, tiled=True)]
    all_to_all x2 -> x5, blocking collectives: 42.2 us -> 73.3 us  [exchange(): lax.all_to_all(v, AXES, split_axis=0, concat_axis=0, axis_index_groups=me...]
    all_to_all x2, starting transfers between devices: 12.1 us -> 23.5 us  [exchange(): lax.all_to_all(v, AXES, split_axis=0, concat_axis=0, axis_index_groups=me...]
    all_gather x0 -> x2, blocking collectives: none -> 10.5 us  [the longest x1 8.3 us: shards(): back = lax.all_gather(exchange(result.reshape(packed.shape), PLANE), 'c')]
    ppermute x3 -> x2, starting transfers between devices: 12.8 us -> 4.3 us  [other_core(): return lax.ppermute(v, 'c', [(0, 1), (1, 0)])]
    ppermute x3 -> x2, waiting for transfers between devices: 5.88 us -> 0.01 us  [other_core(): return lax.ppermute(v, 'c', [(0, 1), (1, 0)])]
    all_to_all x2, waiting for transfers between devices: 7.69 us -> 2.44 us  [exchange(): lax.all_to_all(v, AXES, split_axis=0, concat_axis=0, axis_index_groups=me...]
    pallas_call x3 -> x8, Pallas kernels: 5.86 us -> 10.2 us  [the longest x2 5.01 us: prepare(): pl.pallas_call(functools.partial(prepare_kernel, norm), out_shape=(shape,...]
  transfers between devices with their start and end apart: 5 -> 4, of which waited for: 5 -> 2; matrix products, arithmetic and copies ran while one was open for 0% -> 0% of each run, Pallas kernels for 2% -> 4%
where the time goes in v4:
time: 137 us; the launch traced here: 134 us
  blocking collectives  83.8 us (61%)
  starting transfers between devices  27.8 us (20%)
  Pallas kernels  11 us (8%)
  local copies, waits for them, and re-layouts  8.6 us (6%)
  waiting for transfers between devices  2.45 us (2%)
    all_to_all x5, blocking collectives, exchange(): lax.all_to_all(v, AXES, split_axis=0, concat_axis=0, axis_index_groups=me...  73.3 us
    all_to_all x2, starting transfers between devices, exchange(): lax.all_to_all(v, AXES, split_axis=0, concat_axis=0, axis_index_groups=me...  23.5 us
    all_gather x1, blocking collectives, shards(): back = lax.all_gather(exchange(result.reshape(packed.shape), PLANE), 'c')  8.3 us
    unnamed x18, local copies, waits for them, and re-layouts  7.84 us
    pallas_call x2, Pallas kernels, prepare(): pl.pallas_call(functools.partial(prepare_kernel, norm), out_shape=(shape,...  5.01 us
    ppermute x2, starting transfers between devices, other_core(): return lax.ppermute(v, 'c', [(0, 1), (1, 0)])  4.3 us
  transfers between devices with their start and end apart: 4, of which 2 were waited for; matrix products, arithmetic and copies ran while one was open for 0% of the time, Pallas kernels for 4%

profile of v4, /device:TPU:1, one launch (start us, length us, event | category | flops | bytes accessed | tf_op | source)
XLA Modules:
  0.0 134.1 jit_solution(7654453043141024055)
XLA Ops:
  0.0 0.9 copy-done
  1.6 6.9 %all-to-all-start = ((bf16[4,48,512]{2,1,0:T(8,128)(2,1)}), bf16[4,48,512]{2,1,0:T(8,128)(2,1)S(1)}, u32[]{:S(2)}, u32[]{:S(2)}) async-start(bf16[4,48,512]{2,1,0:T(8,128)(2,1)} %broadcast_in_dim.4), calls=%async_computation | async-start | bytes 393216 | tf_op jit(solution)/shard_map/all_to_all | solution.py:64
  8.5 1.4 %copy-done.7 = bf16[1,1,256,3072]{3,2,1,0:T(8,128)(2,1)S(1)} copy-done((bf16[1,1,256,3072]{3,2,1,0:T(8,128)(2,1)S(1)}, bf16[1,1,256,3072]{3,2,1,0:T(8,128)(2,1)}, u32[]{:S(2)}) %copy-start.7) | copy-done | bytes 1572888
  9.9 2.7 %prepare.2 = (bf16[256,1536]{1,0:T(8,128)(2,1)S(1)}, bf16[256,1536]{1,0:T(8,128)(2,1)}) custom-call(bf16[256,3072]{1,0:T(8,128)(2,1)S(1)} %bitcast.17), custom_call_target="tpu_custom_call" | custom-call | tf_op jit(solution)/shard_map/prepare/pallas_call | solution.py:105
  12.5 0.9 copy-done.1
  13.4 1.5 %all-to-all-done.value = bf16[4,48,512]{2,1,0:T(8,128)(2,1)S(1)} async-done(((bf16[4,48,512]{2,1,0:T(8,128)(2,1)}), bf16[4,48,512]{2,1,0:T(8,128)(2,1)S(1)}, u32[]{:S(2)}, u32[]{:S(2)}) %all-to-all-start) | async-done | bytes 196640 | tf_op jit(solution)/shard_map/all_to_all | solution.py:64
  14.9 1.2 repeat.1
  16.2 16.6 %all-to-all-start.1 = ((bf16[8,4,48,512]{3,2,1,0:T(8,128)(2,1)}), bf16[8,4,48,512]{3,2,1,0:T(8,128)(2,1)S(1)}, u32[]{:S(2)}, u32[]{:S(2)}) async-start(bf16[8,4,48,512]{3,2,1,0:T(8,128)(2,1)} %repeat.1), calls=%async_computation.1 | async-start | bytes 3145728 | tf_op jit(solution)/shard_map/all_to_all | solution.py:64
  32.8 1.9 %collective-permute-start = (bf16[256,1536]{1,0:T(8,128)(2,1)}, bf16[256,1536]{1,0:T(8,128)(2,1)S(1)}, u32[]{:S(2)}, u32[]{:S(2)}) collective-permute-start(bf16[256,1536]{1,0:T(8,128)(2,1)} %get-tuple-element.21), channel_id=1, source_target_pairs={{0,1},{1,0},{2,3},{3,2},{4,5},{5,4},{6,7},{7,6},{8,9},{9,8},{10,11... | collective-permute-start | bytes 2359304 | tf_op jit(solution)/shard_map/ppermute | solution.py:60
  34.8 1.4 %copy-done.8 = bf16[1,1,256,3072]{3,2,1,0:T(8,128)(2,1)S(1)} copy-done((bf16[1,1,256,3072]{3,2,1,0:T(8,128)(2,1)S(1)}, bf16[1,1,256,3072]{3,2,1,0:T(8,128)(2,1)}, u32[]{:S(2)}) %copy-start.8) | copy-done | bytes 1572888
  36.2 2.3 %prepare.3 = (bf16[256,1536]{1,0:T(8,128)(2,1)S(1)}, bf16[256,1536]{1,0:T(8,128)(2,1)}) custom-call(bf16[256,3072]{1,0:T(8,128)(2,1)S(1)} %bitcast.18), custom_call_target="tpu_custom_call" | custom-call | tf_op jit(solution)/shard_map/prepare/pallas_call | solution.py:105
  38.5 0.9 copy-done.4
  39.4 2.4 %collective-permute-start.1 = (bf16[256,1536]{1,0:T(8,128)(2,1)}, bf16[256,1536]{1,0:T(8,128)(2,1)S(1)}, u32[]{:S(2)}, u32[]{:S(2)}) collective-permute-start(bf16[256,1536]{1,0:T(8,128)(2,1)} %get-tuple-element.22), channel_id=1, source_target_pairs={{0,1},{1,0},{2,3},{3,2},{4,5},{5,4},{6,7},{7,6},{8,9},{9,8},{10,11... | collective-permute-start | bytes 2359304 | tf_op jit(solution)/shard_map/ppermute | solution.py:60
  41.8 0.9 all-to-all-done.1
  42.7 1.1 copy-done.2
  43.9 1.1 copy-done.5
  46.6 2.2 %all-gather = bf16[32,2,8,512]{3,2,1,0:T(8,128)(2,1)S(1)} all-gather(bf16[16,2,8,512]{3,2,1,0:T(8,128)(2,1)S(1)} %get-tuple-element.26), channel_id=2, replica_groups=mesh['z'=8,'yh'=2,'yl'=4,'x'=4,'c'=2] {'c'}, dimensions={0}, use_global_device_ids=true | all-gather | bytes 786432 | tf_op jit(solution)/shard_map/all_gather | solution.py:329
  48.8 11.8 %all_to_all.35 = bf16[16,2,8,512]{3,2,1,0:T(8,128)(2,1)S(1)} all-to-all(bf16[16,2,8,512]{3,2,1,0:T(8,128)(2,1)S(1)} %fusion), channel_id=1, replica_groups={{0,2,4,6,8,10,12,14,16,18,20,22,24,26,28,30},{21,23,17,19,29,31,25,27,5..., dimensions={0} | all-to-all | bytes 524288 | tf_op jit(solution)/shard_map/all_to_all | solution.py:64
  61.6 12.1 %all_to_all.36 = bf16[16,2,8,512]{3,2,1,0:T(8,128)(2,1)S(1)} all-to-all(bf16[16,2,8,512]{3,2,1,0:T(8,128)(2,1)S(1)} %bitcast.20), channel_id=1, replica_groups={{0,2,4,6,8,10,12,14,16,18,20,22,24,26,28,30},{21,23,17,19,29,31,25,27,5..., dimensions={0} | all-to-all | bytes 524288 | tf_op jit(solution)/shard_map/all_to_all | solution.py:64
  73.6 8.3 %all-gather.1 = bf16[32,2,8,512]{3,2,1,0:T(8,128)(2,1)S(1)} all-gather(bf16[16,2,8,512]{3,2,1,0:T(8,128)(2,1)S(1)} %all_to_all.36), channel_id=3, replica_groups=mesh['z'=8,'yh'=2,'yl'=4,'x'=4,'c'=2] {'c'}, dimensions={0}, use_global_device_ids=true | all-gather | bytes 786432 | tf_op jit(solution)/shard_map/all_gather | solution.py:333
  81.9 1.0 weight_parts.2.rest_0_
  83.7 17.8 %all_to_all.37 = bf16[8,4,48,512]{3,2,1,0:T(8,128)(2,1)S(1)} all-to-all(bf16[8,4,48,512]{3,2,1,0:T(8,128)(2,1)S(1)} %bitcast.13), channel_id=1, replica_groups={{0,64,2,66,8,72,10,74},{511,63,505,57,455,7,449,1},{507,59,509,61,451,3..., dimensions={0} | all-to-all | bytes 3145728 | tf_op jit(solution)/shard_map/all_to_all | solution.py:64
  101.8 14.6 %all_to_all.38 = bf16[16,48,128]{2,1,0:T(8,128)(2,1)S(1)} all-to-all(bf16[16,48,128]{2,1,0:T(8,128)(2,1)S(1)} %bitcast.23), channel_id=1, replica_groups={{0,128,256,384,4,132,260,388,16,144,272,400,20,148,276,404},{1,129,257,..., dimensions={0} | all-to-all | bytes 393216 | tf_op jit(solution)/shard_map/all_to_all | solution.py:64
  116.5 17.0 %all_to_all.39 = bf16[16,48,128]{2,1,0:T(8,128)(2,1)S(1)} all-to-all(bf16[16,48,128]{2,1,0:T(8,128)(2,1)S(1)} %broadcast_in_dim.5), channel_id=1, replica_groups={{0,32,64,96,128,160,192,224,256,288,320,352,384,416,448,480},{449,481,1..., dimensions={0} | all-to-all | bytes 393216 | tf_op jit(solution)/shard_map/all_to_all | solution.py:64
  (26 shorter events, 5.0 us)
Async XLA Ops:
  0.0 0.9 copy-start
  1.6 13.4 %all-to-all-start = ((bf16[4,48,512]{2,1,0:T(8,128)(2,1)}), bf16[4,48,512]{2,1,0:T(8,128)(2,1)S(1)}, u32[]{:S(2)}, u32[]{:S(2)}) async-start(bf16[4,48,512]{2,1,0:T(8,128)(2,1)} %broadcast_in_dim.4), calls=%async_computation | async-start | bytes 393216 | tf_op jit(solution)/shard_map/all_to_all | solution.py:64
  8.5 1.4 %copy-start.7 = (bf16[1,1,256,3072]{3,2,1,0:T(8,128)(2,1)S(1)}, bf16[1,1,256,3072]{3,2,1,0:T(8,128)(2,1)}, u32[]{:S(2)}) copy-start(bf16[1,1,256,3072]{3,2,1,0:T(8,128)(2,1)} %param.3) | copy-start | bytes 4718596
  12.5 0.9 copy-start.1
  16.2 26.5 %all-to-all-start.1 = ((bf16[8,4,48,512]{3,2,1,0:T(8,128)(2,1)}), bf16[8,4,48,512]{3,2,1,0:T(8,128)(2,1)S(1)}, u32[]{:S(2)}, u32[]{:S(2)}) async-start(bf16[8,4,48,512]{3,2,1,0:T(8,128)(2,1)} %repeat.1), calls=%async_computation.1 | async-start | bytes 3145728 | tf_op jit(solution)/shard_map/all_to_all | solution.py:64
  32.8 12.9 %collective-permute-start = (bf16[256,1536]{1,0:T(8,128)(2,1)}, bf16[256,1536]{1,0:T(8,128)(2,1)S(1)}, u32[]{:S(2)}, u32[]{:S(2)}) collective-permute-start(bf16[256,1536]{1,0:T(8,128)(2,1)} %get-tuple-element.21), channel_id=1, source_target_pairs={{0,1},{1,0},{2,3},{3,2},{4,5},{5,4},{6,7},{7,6},{8,9},{9,8},{10,11... | collective-permute-start | bytes 2359304 | tf_op jit(solution)/shard_map/ppermute | solution.py:60
  34.7 1.4 %copy-start.8 = (bf16[1,1,256,3072]{3,2,1,0:T(8,128)(2,1)S(1)}, bf16[1,1,256,3072]{3,2,1,0:T(8,128)(2,1)}, u32[]{:S(2)}) copy-start(bf16[1,1,256,3072]{3,2,1,0:T(8,128)(2,1)} %param.4) | copy-start | bytes 4718596
  38.5 0.9 copy-start.4
  39.4 6.4 %collective-permute-start.1 = (bf16[256,1536]{1,0:T(8,128)(2,1)}, bf16[256,1536]{1,0:T(8,128)(2,1)S(1)}, u32[]{:S(2)}, u32[]{:S(2)}) collective-permute-start(bf16[256,1536]{1,0:T(8,128)(2,1)} %get-tuple-element.22), channel_id=1, source_target_pairs={{0,1},{1,0},{2,3},{3,2},{4,5},{5,4},{6,7},{7,6},{8,9},{9,8},{10,11... | collective-permute-start | bytes 2359304 | tf_op jit(solution)/shard_map/ppermute | solution.py:60
  42.7 1.1 copy-start.2
  43.9 1.1 copy-start.5
  48.8 33.2 %copy-start.3 = (bf16[256,1536]{1,0:T(8,128)(2,1)S(1)}, bf16[256,1536]{1,0:T(8,128)(2,1)}, u32[]{:S(2)}) copy-start(bf16[256,1536]{1,0:T(8,128)(2,1)} %copy-done.1) | copy-start | bytes 2359300
  81.9 1.1 copy-start.6

commit v5 on v4

--- a/solution.py
+++ b/solution.py
@@ -52,7 +52,7 @@
 COPIES = cube_groups(("c", "yl", "x"), ("z1", "z0", "y2"))
 PLANE = groups(
     lambda z, yh, yl, x, c: (z, yh, c),
-    lambda z, yh, yl, x, c: ((yl + 2 * c) % NYL, (x + 2 * c) % NX),
+    lambda z, yh, yl, x, c: ((yl + 1 + 2 * c) % NYL, (x + 2 * c) % NX),
 )
 
 

time: 137 us -> 136 us (level)
    all_gather x1, blocking collectives: 8.3 us -> 5.77 us  [shards(): back = lax.all_gather(exchange(result.reshape(packed.shape), PLANE), 'c')]
    all_to_all x5, blocking collectives: 73.3 us -> 75.3 us  [exchange(): lax.all_to_all(v, AXES, split_axis=0, concat_axis=0, axis_index_groups=me...]
where the time goes in v5:
time: 136 us; the launch traced here: 134 us
  blocking collectives  83.2 us (61%)
  starting transfers between devices  27.8 us (20%)
  Pallas kernels  11 us (8%)
  local copies, waits for them, and re-layouts  8.6 us (6%)
  waiting for transfers between devices  2.45 us (2%)
    all_to_all x5, blocking collectives, exchange(): lax.all_to_all(v, AXES, split_axis=0, concat_axis=0, axis_index_groups=me...  75.3 us
    all_to_all x2, starting transfers between devices, exchange(): lax.all_to_all(v, AXES, split_axis=0, concat_axis=0, axis_index_groups=me...  23.5 us
    unnamed x18, local copies, waits for them, and re-layouts  7.84 us
    all_gather x1, blocking collectives, shards(): back = lax.all_gather(exchange(result.reshape(packed.shape), PLANE), 'c')  5.77 us
    pallas_call x2, Pallas kernels, prepare(): pl.pallas_call(functools.partial(prepare_kernel, norm), out_shape=(shape,...  5.01 us
    ppermute x2, starting transfers between devices, other_core(): return lax.ppermute(v, 'c', [(0, 1), (1, 0)])  4.3 us
  transfers between devices with their start and end apart: 4, of which 2 were waited for; matrix products, arithmetic and copies ran while one was open for 0% of the time, Pallas kernels for 4%

profile of v5, /device:TPU:1, one launch (start us, length us, event | category | flops | bytes accessed | tf_op | source)
XLA Modules:
  0.0 133.6 jit_solution(6539983261830481593)
XLA Ops:
  0.0 0.9 copy-done
  1.6 6.9 %all-to-all-start = ((bf16[4,48,512]{2,1,0:T(8,128)(2,1)}), bf16[4,48,512]{2,1,0:T(8,128)(2,1)S(1)}, u32[]{:S(2)}, u32[]{:S(2)}) async-start(bf16[4,48,512]{2,1,0:T(8,128)(2,1)} %broadcast_in_dim.4), calls=%async_computation | async-start | bytes 393216 | tf_op jit(solution)/shard_map/all_to_all | solution.py:64
  8.5 1.4 %copy-done.7 = bf16[1,1,256,3072]{3,2,1,0:T(8,128)(2,1)S(1)} copy-done((bf16[1,1,256,3072]{3,2,1,0:T(8,128)(2,1)S(1)}, bf16[1,1,256,3072]{3,2,1,0:T(8,128)(2,1)}, u32[]{:S(2)}) %copy-start.7) | copy-done | bytes 1572888
  9.9 2.7 %prepare.2 = (bf16[256,1536]{1,0:T(8,128)(2,1)S(1)}, bf16[256,1536]{1,0:T(8,128)(2,1)}) custom-call(bf16[256,3072]{1,0:T(8,128)(2,1)S(1)} %bitcast.17), custom_call_target="tpu_custom_call" | custom-call | tf_op jit(solution)/shard_map/prepare/pallas_call | solution.py:105
  12.5 0.9 copy-done.1
  13.4 1.5 %all-to-all-done.value = bf16[4,48,512]{2,1,0:T(8,128)(2,1)S(1)} async-done(((bf16[4,48,512]{2,1,0:T(8,128)(2,1)}), bf16[4,48,512]{2,1,0:T(8,128)(2,1)S(1)}, u32[]{:S(2)}, u32[]{:S(2)}) %all-to-all-start) | async-done | bytes 196640 | tf_op jit(solution)/shard_map/all_to_all | solution.py:64
  14.9 1.2 repeat.1
  16.2 16.6 %all-to-all-start.1 = ((bf16[8,4,48,512]{3,2,1,0:T(8,128)(2,1)}), bf16[8,4,48,512]{3,2,1,0:T(8,128)(2,1)S(1)}, u32[]{:S(2)}, u32[]{:S(2)}) async-start(bf16[8,4,48,512]{3,2,1,0:T(8,128)(2,1)} %repeat.1), calls=%async_computation.1 | async-start | bytes 3145728 | tf_op jit(solution)/shard_map/all_to_all | solution.py:64
  32.8 1.9 %collective-permute-start = (bf16[256,1536]{1,0:T(8,128)(2,1)}, bf16[256,1536]{1,0:T(8,128)(2,1)S(1)}, u32[]{:S(2)}, u32[]{:S(2)}) collective-permute-start(bf16[256,1536]{1,0:T(8,128)(2,1)} %get-tuple-element.21), channel_id=1, source_target_pairs={{0,1},{1,0},{2,3},{3,2},{4,5},{5,4},{6,7},{7,6},{8,9},{9,8},{10,11... | collective-permute-start | bytes 2359304 | tf_op jit(solution)/shard_map/ppermute | solution.py:60
  34.8 1.4 %copy-done.8 = bf16[1,1,256,3072]{3,2,1,0:T(8,128)(2,1)S(1)} copy-done((bf16[1,1,256,3072]{3,2,1,0:T(8,128)(2,1)S(1)}, bf16[1,1,256,3072]{3,2,1,0:T(8,128)(2,1)}, u32[]{:S(2)}) %copy-start.8) | copy-done | bytes 1572888
  36.2 2.3 %prepare.3 = (bf16[256,1536]{1,0:T(8,128)(2,1)S(1)}, bf16[256,1536]{1,0:T(8,128)(2,1)}) custom-call(bf16[256,3072]{1,0:T(8,128)(2,1)S(1)} %bitcast.18), custom_call_target="tpu_custom_call" | custom-call | tf_op jit(solution)/shard_map/prepare/pallas_call | solution.py:105
  38.5 0.9 copy-done.4
  39.4 2.4 %collective-permute-start.1 = (bf16[256,1536]{1,0:T(8,128)(2,1)}, bf16[256,1536]{1,0:T(8,128)(2,1)S(1)}, u32[]{:S(2)}, u32[]{:S(2)}) collective-permute-start(bf16[256,1536]{1,0:T(8,128)(2,1)} %get-tuple-element.22), channel_id=1, source_target_pairs={{0,1},{1,0},{2,3},{3,2},{4,5},{5,4},{6,7},{7,6},{8,9},{9,8},{10,11... | collective-permute-start | bytes 2359304 | tf_op jit(solution)/shard_map/ppermute | solution.py:60
  41.8 0.9 all-to-all-done.1
  42.7 1.1 copy-done.2
  43.9 1.1 copy-done.5
  46.6 2.2 %all-gather = bf16[32,2,8,512]{3,2,1,0:T(8,128)(2,1)S(1)} all-gather(bf16[16,2,8,512]{3,2,1,0:T(8,128)(2,1)S(1)} %get-tuple-element.26), channel_id=2, replica_groups=mesh['z'=8,'yh'=2,'yl'=4,'x'=4,'c'=2] {'c'}, dimensions={0}, use_global_device_ids=true | all-gather | bytes 786432 | tf_op jit(solution)/shard_map/all_gather | solution.py:329
  48.8 12.7 %all_to_all.35 = bf16[16,2,8,512]{3,2,1,0:T(8,128)(2,1)S(1)} all-to-all(bf16[16,2,8,512]{3,2,1,0:T(8,128)(2,1)S(1)} %fusion), channel_id=1, replica_groups={{24,26,28,30,0,2,4,6,8,10,12,14,16,18,20,22},{13,15,9,11,21,23,17,19,29..., dimensions={0} | all-to-all | bytes 524288 | tf_op jit(solution)/shard_map/all_to_all | solution.py:64
  62.4 11.3 %all_to_all.36 = bf16[16,2,8,512]{3,2,1,0:T(8,128)(2,1)S(1)} all-to-all(bf16[16,2,8,512]{3,2,1,0:T(8,128)(2,1)S(1)} %bitcast.20), channel_id=1, replica_groups={{24,26,28,30,0,2,4,6,8,10,12,14,16,18,20,22},{13,15,9,11,21,23,17,19,29..., dimensions={0} | all-to-all | bytes 524288 | tf_op jit(solution)/shard_map/all_to_all | solution.py:64
  73.7 5.8 %all-gather.1 = bf16[32,2,8,512]{3,2,1,0:T(8,128)(2,1)S(1)} all-gather(bf16[16,2,8,512]{3,2,1,0:T(8,128)(2,1)S(1)} %all_to_all.36), channel_id=3, replica_groups=mesh['z'=8,'yh'=2,'yl'=4,'x'=4,'c'=2] {'c'}, dimensions={0}, use_global_device_ids=true | all-gather | bytes 786432 | tf_op jit(solution)/shard_map/all_gather | solution.py:333
  79.5 1.0 weight_parts.2.rest_0_
  81.3 17.8 %all_to_all.37 = bf16[8,4,48,512]{3,2,1,0:T(8,128)(2,1)S(1)} all-to-all(bf16[8,4,48,512]{3,2,1,0:T(8,128)(2,1)S(1)} %bitcast.13), channel_id=1, replica_groups={{0,64,2,66,8,72,10,74},{511,63,505,57,455,7,449,1},{507,59,509,61,451,3..., dimensions={0} | all-to-all | bytes 3145728 | tf_op jit(solution)/shard_map/all_to_all | solution.py:64
  99.4 15.6 %all_to_all.38 = bf16[16,48,128]{2,1,0:T(8,128)(2,1)S(1)} all-to-all(bf16[16,48,128]{2,1,0:T(8,128)(2,1)S(1)} %bitcast.23), channel_id=1, replica_groups={{0,128,256,384,4,132,260,388,16,144,272,400,20,148,276,404},{1,129,257,..., dimensions={0} | all-to-all | bytes 393216 | tf_op jit(solution)/shard_map/all_to_all | solution.py:64
  115.1 17.8 %all_to_all.39 = bf16[16,48,128]{2,1,0:T(8,128)(2,1)S(1)} all-to-all(bf16[16,48,128]{2,1,0:T(8,128)(2,1)S(1)} %broadcast_in_dim.5), channel_id=1, replica_groups={{0,32,64,96,128,160,192,224,256,288,320,352,384,416,448,480},{449,481,1..., dimensions={0} | all-to-all | bytes 393216 | tf_op jit(solution)/shard_map/all_to_all | solution.py:64
  (26 shorter events, 5.0 us)
Async XLA Ops:
  0.0 0.9 copy-start
  1.6 13.4 %all-to-all-start = ((bf16[4,48,512]{2,1,0:T(8,128)(2,1)}), bf16[4,48,512]{2,1,0:T(8,128)(2,1)S(1)}, u32[]{:S(2)}, u32[]{:S(2)}) async-start(bf16[4,48,512]{2,1,0:T(8,128)(2,1)} %broadcast_in_dim.4), calls=%async_computation | async-start | bytes 393216 | tf_op jit(solution)/shard_map/all_to_all | solution.py:64
  8.5 1.4 %copy-start.7 = (bf16[1,1,256,3072]{3,2,1,0:T(8,128)(2,1)S(1)}, bf16[1,1,256,3072]{3,2,1,0:T(8,128)(2,1)}, u32[]{:S(2)}) copy-start(bf16[1,1,256,3072]{3,2,1,0:T(8,128)(2,1)} %param.3) | copy-start | bytes 4718596
  12.5 0.9 copy-start.1
  16.2 26.5 %all-to-all-start.1 = ((bf16[8,4,48,512]{3,2,1,0:T(8,128)(2,1)}), bf16[8,4,48,512]{3,2,1,0:T(8,128)(2,1)S(1)}, u32[]{:S(2)}, u32[]{:S(2)}) async-start(bf16[8,4,48,512]{3,2,1,0:T(8,128)(2,1)} %repeat.1), calls=%async_computation.1 | async-start | bytes 3145728 | tf_op jit(solution)/shard_map/all_to_all | solution.py:64
  32.8 12.9 %collective-permute-start = (bf16[256,1536]{1,0:T(8,128)(2,1)}, bf16[256,1536]{1,0:T(8,128)(2,1)S(1)}, u32[]{:S(2)}, u32[]{:S(2)}) collective-permute-start(bf16[256,1536]{1,0:T(8,128)(2,1)} %get-tuple-element.21), channel_id=1, source_target_pairs={{0,1},{1,0},{2,3},{3,2},{4,5},{5,4},{6,7},{7,6},{8,9},{9,8},{10,11... | collective-permute-start | bytes 2359304 | tf_op jit(solution)/shard_map/ppermute | solution.py:60
  34.7 1.4 %copy-start.8 = (bf16[1,1,256,3072]{3,2,1,0:T(8,128)(2,1)S(1)}, bf16[1,1,256,3072]{3,2,1,0:T(8,128)(2,1)}, u32[]{:S(2)}) copy-start(bf16[1,1,256,3072]{3,2,1,0:T(8,128)(2,1)} %param.4) | copy-start | bytes 4718596
  38.5 0.9 copy-start.4
  39.4 6.4 %collective-permute-start.1 = (bf16[256,1536]{1,0:T(8,128)(2,1)}, bf16[256,1536]{1,0:T(8,128)(2,1)S(1)}, u32[]{:S(2)}, u32[]{:S(2)}) collective-permute-start(bf16[256,1536]{1,0:T(8,128)(2,1)} %get-tuple-element.22), channel_id=1, source_target_pairs={{0,1},{1,0},{2,3},{3,2},{4,5},{5,4},{6,7},{7,6},{8,9},{9,8},{10,11... | collective-permute-start | bytes 2359304 | tf_op jit(solution)/shard_map/ppermute | solution.py:60
  42.7 1.1 copy-start.2
  43.9 1.1 copy-start.5
  48.8 30.7 %copy-start.3 = (bf16[256,1536]{1,0:T(8,128)(2,1)S(1)}, bf16[256,1536]{1,0:T(8,128)(2,1)}, u32[]{:S(2)}) copy-start(bf16[256,1536]{1,0:T(8,128)(2,1)} %copy-done.1) | copy-start | bytes 2359300
  79.5 1.1 copy-start.6

commit v6 on v5

--- a/solution.py
+++ b/solution.py
@@ -124,8 +124,10 @@
         theirs[:, :, at] = jnp.where(c == 0, high, low).reshape(to).astype(BF)
 
 
-def project_own_kernel(blocks, lat, cot, w, mine, theirs):
-    c = lax.axis_index("c")
+def project_arrived_kernel(blocks, lat, cot, w, mine, theirs, keep_lat, keep_cot):
+    c = lax.axis_index("c")
+    keep_lat[...] = lat[...]
+    keep_cot[...] = cot[...]
     rows = blocks.shape[1]
     for yl, x, half, even, odd in half_shards():
         place = (yl * NX + x) * 2 + half
@@ -133,12 +135,12 @@
     multiply(lat, cot, w, mine, theirs)
 
 
-def project_both_kernel(w, lat, cot, own_mine, own_theirs, mine, theirs, new_mine, new_theirs):
+def project_own_kernel(w, lat, cot, arr_mine, arr_theirs, mine, theirs, new_mine, new_theirs):
     c = lax.axis_index("c")
     multiply(lat, cot, w, new_mine, new_theirs)
-    for own, new, to in ((own_mine, new_mine, mine), (own_theirs, new_theirs, theirs)):
-        to[:, c] = own[...]
-        to[:, 1 - c] = new[...]
+    for old, new, to in ((arr_mine, new_mine, mine), (arr_theirs, new_theirs, theirs)):
+        to[:, c] = new[...]
+        to[:, 1 - c] = old[...]
 
 
 def project(blocks, own_l, own_c, arr_l, arr_c):
@@ -148,27 +150,30 @@
     rows = tokens // (chips * NC)
     half, whole = (chips, rows, columns), (chips, NC, rows, columns)
     params = pltpu.CompilerParams(vmem_limit_bytes=LIMIT)
-    w, mine, theirs = pl.pallas_call(
-        project_own_kernel,
+    w, mine, theirs, arr_l, arr_c = pl.pallas_call(
+        project_arrived_kernel,
         out_shape=(
             jax.ShapeDtypeStruct((width, columns), BF),
             jax.ShapeDtypeStruct(half, F32),
             jax.ShapeDtypeStruct(half, BF),
+            jax.ShapeDtypeStruct(arr_l.shape, BF),
+            jax.ShapeDtypeStruct(arr_c.shape, BF),
         ),
         in_specs=[VMEM] * 3,
-        out_specs=(VMEM,) * 3,
+        out_specs=(VMEM,) * 5,
         compiler_params=params,
-        name="project_own",
-    )(blocks, own_l, own_c)
-    return pl.pallas_call(
-        project_both_kernel,
+        name="project_arrived",
+    )(blocks, arr_l, arr_c)
+    mine, theirs = pl.pallas_call(
+        project_own_kernel,
         out_shape=(jax.ShapeDtypeStruct(whole, F32), jax.ShapeDtypeStruct(whole, BF)),
         in_specs=[VMEM] * 5,
         out_specs=(VMEM,) * 2,
         scratch_shapes=[pltpu.VMEM(half, F32), pltpu.VMEM(half, BF)],
         compiler_params=params,
-        name="project_both",
-    )(w, arr_l, arr_c, mine, theirs)
+        name="project_own",
+    )(w, own_l, own_c, mine, theirs)
+    return mine, theirs, arr_l, arr_c
 
 
 def weight_kernel(columns, back, own, arrived, *rest):
@@ -325,7 +330,8 @@
     own_c, away_c = prepare(cotangent.reshape(-1, width), False)
     blocks, own_l = gather(weights, own_l)
     tokens = own_l, own_c, other_core(away_l), other_core(away_c)
-    mine, theirs = project(blocks, *tokens)
+    mine, theirs, *arrived = project(blocks, *tokens)
+    tokens = *tokens[:2], *arrived
     both = lax.all_gather(theirs, "c")
     part = lax.dynamic_index_in_dim(both, 1 - lax.axis_index("c"), keepdims=False)
     packed = exchange((mine + part.astype(F32)).astype(BF), PLANE)

time: 136 us -> 135 us (level)
  local copies, waits for them, and re-layouts: 8.6 us -> 4.46 us
  waiting for transfers between devices: 2.45 us -> 4.63 us
  Pallas kernels: 11 us -> 12.5 us
    unnamed x18 -> x6, local copies, waits for them, and re-layouts: 7.84 us -> 3.7 us
    ppermute x2, waiting for transfers between devices: 0.01 us -> 2.22 us  [other_core(): return lax.ppermute(v, 'c', [(0, 1), (1, 0)])]
    pallas_call x2, Pallas kernels: 1.56 us -> 3.04 us  [the longest x1 2.25 us: project(): pl.pallas_call(project_arrived_kernel, out_shape=(jax.ShapeDtypeStruct((w...]
where the time goes in v6:
time: 135 us; the launch traced here: 133 us
  blocking collectives  82.7 us (61%)
  starting transfers between devices  27.8 us (21%)
  Pallas kernels  12.5 us (9%)
  waiting for transfers between devices  4.63 us (3%)
  local copies, waits for them, and re-layouts  4.46 us (3%)
    all_to_all x5, blocking collectives, exchange(): lax.all_to_all(v, AXES, split_axis=0, concat_axis=0, axis_index_groups=me...  74.7 us
    all_to_all x2, starting transfers between devices, exchange(): lax.all_to_all(v, AXES, split_axis=0, concat_axis=0, axis_index_groups=me...  23.5 us
    all_gather x1, blocking collectives, shards(): back = lax.all_gather(exchange(result.reshape(packed.shape), PLANE), 'c')  5.77 us
    pallas_call x2, Pallas kernels, prepare(): pl.pallas_call(functools.partial(prepare_kernel, norm), out_shape=(shape,...  5.03 us
    ppermute x2, starting transfers between devices, other_core(): return lax.ppermute(v, 'c', [(0, 1), (1, 0)])  4.3 us
    unnamed x6, local copies, waits for them, and re-layouts  3.7 us
  transfers between devices with their start and end apart: 4, of which 2 were waited for; matrix products, arithmetic and copies ran while one was open for 0% of the time, Pallas kernels for 4%

profile of v6, /device:TPU:1, one launch (start us, length us, event | category | flops | bytes accessed | tf_op | source)
XLA Modules:
  0.0 132.5 jit_solution(5862018576905338609)
XLA Ops:
  0.0 0.9 copy-done
  1.6 6.9 %all-to-all-start = ((bf16[4,48,512]{2,1,0:T(8,128)(2,1)}), bf16[4,48,512]{2,1,0:T(8,128)(2,1)S(1)}, u32[]{:S(2)}, u32[]{:S(2)}) async-start(bf16[4,48,512]{2,1,0:T(8,128)(2,1)} %broadcast_in_dim.4), calls=%async_computation | async-start | bytes 393216 | tf_op jit(solution)/shard_map/all_to_all | solution.py:64
  8.5 1.4 %copy-done.1 = bf16[1,1,256,3072]{3,2,1,0:T(8,128)(2,1)S(1)} copy-done((bf16[1,1,256,3072]{3,2,1,0:T(8,128)(2,1)S(1)}, bf16[1,1,256,3072]{3,2,1,0:T(8,128)(2,1)}, u32[]{:S(2)}) %copy-start.1) | copy-done | bytes 1572888
  9.9 2.7 %prepare.2 = (bf16[256,1536]{1,0:T(8,128)(2,1)S(1)}, bf16[256,1536]{1,0:T(8,128)(2,1)}) custom-call(bf16[256,3072]{1,0:T(8,128)(2,1)S(1)} %bitcast.17), custom_call_target="tpu_custom_call" | custom-call | tf_op jit(solution)/shard_map/prepare/pallas_call | solution.py:105
  12.5 2.4 %all-to-all-done.value = bf16[4,48,512]{2,1,0:T(8,128)(2,1)S(1)} async-done(((bf16[4,48,512]{2,1,0:T(8,128)(2,1)}), bf16[4,48,512]{2,1,0:T(8,128)(2,1)S(1)}, u32[]{:S(2)}, u32[]{:S(2)}) %all-to-all-start) | async-done | bytes 196640 | tf_op jit(solution)/shard_map/all_to_all | solution.py:64
  14.9 1.2 repeat.1
  16.2 16.6 %all-to-all-start.1 = ((bf16[8,4,48,512]{3,2,1,0:T(8,128)(2,1)}), bf16[8,4,48,512]{3,2,1,0:T(8,128)(2,1)S(1)}, u32[]{:S(2)}, u32[]{:S(2)}) async-start(bf16[8,4,48,512]{3,2,1,0:T(8,128)(2,1)} %repeat.1), calls=%async_computation.1 | async-start | bytes 3145728 | tf_op jit(solution)/shard_map/all_to_all | solution.py:64
  32.8 1.9 %collective-permute-start = (bf16[256,1536]{1,0:T(8,128)(2,1)}, bf16[256,1536]{1,0:T(8,128)(2,1)}, u32[]{:S(2)}, u32[]{:S(2)}) collective-permute-start(bf16[256,1536]{1,0:T(8,128)(2,1)} %get-tuple-element.20), channel_id=1, source_target_pairs={{0,1},{1,0},{2,3},{3,2},{4,5},{5,4},{6,7},{7,6},{8,9},{9,8},{10,11... | collective-permute-start | bytes 2359304 | tf_op jit(solution)/shard_map/ppermute | solution.py:60
  34.7 1.4 %copy-done.2 = bf16[1,1,256,3072]{3,2,1,0:T(8,128)(2,1)S(1)} copy-done((bf16[1,1,256,3072]{3,2,1,0:T(8,128)(2,1)S(1)}, bf16[1,1,256,3072]{3,2,1,0:T(8,128)(2,1)}, u32[]{:S(2)}) %copy-start.2) | copy-done | bytes 1572888
  36.1 2.4 %prepare.3 = (bf16[256,1536]{1,0:T(8,128)(2,1)S(1)}, bf16[256,1536]{1,0:T(8,128)(2,1)}) custom-call(bf16[256,3072]{1,0:T(8,128)(2,1)S(1)} %bitcast.18), custom_call_target="tpu_custom_call" | custom-call | tf_op jit(solution)/shard_map/prepare/pallas_call | solution.py:105
  38.5 2.4 %collective-permute-start.1 = (bf16[256,1536]{1,0:T(8,128)(2,1)}, bf16[256,1536]{1,0:T(8,128)(2,1)}, u32[]{:S(2)}, u32[]{:S(2)}) collective-permute-start(bf16[256,1536]{1,0:T(8,128)(2,1)} %get-tuple-element.21), channel_id=1, source_target_pairs={{0,1},{1,0},{2,3},{3,2},{4,5},{5,4},{6,7},{7,6},{8,9},{9,8},{10,11... | collective-permute-start | bytes 2359304 | tf_op jit(solution)/shard_map/ppermute | solution.py:60
  40.9 2.2 %collective-permute-done.1.cot = bf16[256,1536]{1,0:T(8,128)(2,1)} collective-permute-done((bf16[256,1536]{1,0:T(8,128)(2,1)}, bf16[256,1536]{1,0:T(8,128)(2,1)}, u32[]{:S(2)}, u32[]{:S(2)}) %collective-permute-start.1) | collective-permute-done | bytes 786464 | tf_op jit(solution)/shard_map/ppermute | solution.py:60
  43.1 2.2 %project_arrived.1 = (bf16[1536,512]{1,0:T(8,128)(2,1)S(1)}, f32[16,8,512]{2,1,0:T(8,128)S(1)}, bf16[16,8,512]{2,1,0:T(8,128)(2,1)S(1)}, bf16[256,1536]{1,0:T(8,128)(2,1)S(1)}, bf16[256,1536]{1,0:T(8,128)(2,1)S(1)}) custom-call(bf16[32,48,512]{2,1,0:T(8,128)(2,1)S(1)} %bitcast.14, bf16[256,1536]{1,0:T(8,128)(2,1)} %collective-permute-done.lat, ...), custom_call_target="tpu_custom_call" | custom-call | tf_op jit(solution)/shard_map/project_arrived/pallas_call | solution.py:153
  45.4 0.8 project_own.1
  46.2 2.2 %all-gather = bf16[32,2,8,512]{3,2,1,0:T(8,128)(2,1)S(1)} all-gather(bf16[16,2,8,512]{3,2,1,0:T(8,128)(2,1)S(1)} %get-tuple-element.28), channel_id=2, replica_groups=mesh['z'=8,'yh'=2,'yl'=4,'x'=4,'c'=2] {'c'}, dimensions={0}, use_global_device_ids=true | all-gather | bytes 786432 | tf_op jit(solution)/shard_map/all_gather | solution.py:335
  48.5 12.1 %all_to_all.35 = bf16[16,2,8,512]{3,2,1,0:T(8,128)(2,1)S(1)} all-to-all(bf16[16,2,8,512]{3,2,1,0:T(8,128)(2,1)S(1)} %fusion), channel_id=1, replica_groups={{24,26,28,30,0,2,4,6,8,10,12,14,16,18,20,22},{13,15,9,11,21,23,17,19,29..., dimensions={0} | all-to-all | bytes 524288 | tf_op jit(solution)/shard_map/all_to_all | solution.py:64
  60.6 0.9 attend.1
  61.5 11.3 %all_to_all.36 = bf16[16,2,8,512]{3,2,1,0:T(8,128)(2,1)S(1)} all-to-all(bf16[16,2,8,512]{3,2,1,0:T(8,128)(2,1)S(1)} %bitcast.20), channel_id=1, replica_groups={{24,26,28,30,0,2,4,6,8,10,12,14,16,18,20,22},{13,15,9,11,21,23,17,19,29..., dimensions={0} | all-to-all | bytes 524288 | tf_op jit(solution)/shard_map/all_to_all | solution.py:64
  72.8 5.8 %all-gather.1 = bf16[32,2,8,512]{3,2,1,0:T(8,128)(2,1)S(1)} all-gather(bf16[16,2,8,512]{3,2,1,0:T(8,128)(2,1)S(1)} %all_to_all.36), channel_id=3, replica_groups=mesh['z'=8,'yh'=2,'yl'=4,'x'=4,'c'=2] {'c'}, dimensions={0}, use_global_device_ids=true | all-gather | bytes 786432 | tf_op jit(solution)/shard_map/all_gather | solution.py:339
  78.5 1.0 weight_parts.2.rest_0_
  80.2 18.2 %all_to_all.37 = bf16[8,4,48,512]{3,2,1,0:T(8,128)(2,1)S(1)} all-to-all(bf16[8,4,48,512]{3,2,1,0:T(8,128)(2,1)S(1)} %bitcast.13), channel_id=1, replica_groups={{0,64,2,66,8,72,10,74},{511,63,505,57,455,7,449,1},{507,59,509,61,451,3..., dimensions={0} | all-to-all | bytes 3145728 | tf_op jit(solution)/shard_map/all_to_all | solution.py:64
  98.7 15.3 %all_to_all.38 = bf16[16,48,128]{2,1,0:T(8,128)(2,1)S(1)} all-to-all(bf16[16,48,128]{2,1,0:T(8,128)(2,1)S(1)} %bitcast.23), channel_id=1, replica_groups={{0,128,256,384,4,132,260,388,16,144,272,400,20,148,276,404},{1,129,257,..., dimensions={0} | all-to-all | bytes 393216 | tf_op jit(solution)/shard_map/all_to_all | solution.py:64
  114.0 17.8 %all_to_all.39 = bf16[16,48,128]{2,1,0:T(8,128)(2,1)S(1)} all-to-all(bf16[16,48,128]{2,1,0:T(8,128)(2,1)S(1)} %broadcast_in_dim.5), channel_id=1, replica_groups={{0,32,64,96,128,160,192,224,256,288,320,352,384,416,448,480},{449,481,1..., dimensions={0} | all-to-all | bytes 393216 | tf_op jit(solution)/shard_map/all_to_all | solution.py:64
  131.8 0.7 finish.1
  (14 shorter events, 1.8 us)
Async XLA Ops:
  0.0 0.9 copy-start
  1.6 13.4 %all-to-all-start = ((bf16[4,48,512]{2,1,0:T(8,128)(2,1)}), bf16[4,48,512]{2,1,0:T(8,128)(2,1)S(1)}, u32[]{:S(2)}, u32[]{:S(2)}) async-start(bf16[4,48,512]{2,1,0:T(8,128)(2,1)} %broadcast_in_dim.4), calls=%async_computation | async-start | bytes 393216 | tf_op jit(solution)/shard_map/all_to_all | solution.py:64
  8.5 1.4 %copy-start.1 = (bf16[1,1,256,3072]{3,2,1,0:T(8,128)(2,1)S(1)}, bf16[1,1,256,3072]{3,2,1,0:T(8,128)(2,1)}, u32[]{:S(2)}) copy-start(bf16[1,1,256,3072]{3,2,1,0:T(8,128)(2,1)} %param.3) | copy-start | bytes 4718596
  16.2 27.0 %all-to-all-start.1 = ((bf16[8,4,48,512]{3,2,1,0:T(8,128)(2,1)}), bf16[8,4,48,512]{3,2,1,0:T(8,128)(2,1)S(1)}, u32[]{:S(2)}, u32[]{:S(2)}) async-start(bf16[8,4,48,512]{3,2,1,0:T(8,128)(2,1)} %repeat.1), calls=%async_computation.1 | async-start | bytes 3145728 | tf_op jit(solution)/shard_map/all_to_all | solution.py:64
  32.8 8.1 %collective-permute-start = (bf16[256,1536]{1,0:T(8,128)(2,1)}, bf16[256,1536]{1,0:T(8,128)(2,1)}, u32[]{:S(2)}, u32[]{:S(2)}) collective-permute-start(bf16[256,1536]{1,0:T(8,128)(2,1)} %get-tuple-element.20), channel_id=1, source_target_pairs={{0,1},{1,0},{2,3},{3,2},{4,5},{5,4},{6,7},{7,6},{8,9},{9,8},{10,11... | collective-permute-start | bytes 2359304 | tf_op jit(solution)/shard_map/ppermute | solution.py:60
  34.7 1.4 %copy-start.2 = (bf16[1,1,256,3072]{3,2,1,0:T(8,128)(2,1)S(1)}, bf16[1,1,256,3072]{3,2,1,0:T(8,128)(2,1)}, u32[]{:S(2)}) copy-start(bf16[1,1,256,3072]{3,2,1,0:T(8,128)(2,1)} %param.4) | copy-start | bytes 4718596
  38.5 4.6 %collective-permute-start.1 = (bf16[256,1536]{1,0:T(8,128)(2,1)}, bf16[256,1536]{1,0:T(8,128)(2,1)}, u32[]{:S(2)}, u32[]{:S(2)}) collective-permute-start(bf16[256,1536]{1,0:T(8,128)(2,1)} %get-tuple-element.21), channel_id=1, source_target_pairs={{0,1},{1,0},{2,3},{3,2},{4,5},{5,4},{6,7},{7,6},{8,9},{9,8},{10,11... | collective-permute-start | bytes 2359304 | tf_op jit(solution)/shard_map/ppermute | solution.py:60

commit v7 on v5

--- a/solution.py
+++ b/solution.py
@@ -73,9 +73,9 @@
         yield yl, x, half, *places
 
 
-def prepare_kernel(norm, value, own, away):
+def prepare_kernel(lat, cot, own_l, own_c, away):
     c = lax.axis_index("c")
-    width = value.shape[1]
+    width = lat.shape[1]
     rows = width // (NYL * NX * NC)
     block = NX * NC * rows
     part = block // 2
@@ -87,136 +87,112 @@
     for b in range(1, NX):
         wanted = wanted + rows * (k >= b * rows).astype(jnp.int32)
     pick = (source == wanted).astype(F32).astype(BF)
-    if norm:
-        wide = value[...].astype(F32)
-        r = lax.rsqrt(jnp.mean(wide * wide, axis=-1, keepdims=True) + 1e-06)
+    wide = lat[...].astype(F32)
+    r = lax.rsqrt(jnp.mean(wide * wide, axis=-1, keepdims=True) + 1e-06)
     for a in range(NYL):
-        tokens = value[:, a * block : (a + 1) * block]
-        if norm:
-            tokens = (tokens.astype(F32) * r).astype(BF)
-        moved = jnp.dot(tokens, pick, preferred_element_type=F32).astype(BF)
-        own[:, a * part : (a + 1) * part] = moved[:, :part]
-        away[:, a * part : (a + 1) * part] = moved[:, part:]
-
-
-def prepare(value, norm):
-    tokens, width = value.shape
-    shape = jax.ShapeDtypeStruct((tokens, width // 2), BF)
-    return pl.pallas_call(
-        functools.partial(prepare_kernel, norm),
-        out_shape=(shape, shape),
-        in_specs=[VMEM],
-        out_specs=(VMEM, VMEM),
+        at, to = slice(a * block, (a + 1) * block), slice(a * part, (a + 1) * part)
+        normed = (lat[:, at].astype(F32) * r).astype(BF)
+        for index, own, tokens in ((0, own_l, normed), (1, own_c, cot[:, at])):
+            moved = jnp.dot(tokens, pick, preferred_element_type=F32).astype(BF)
+            own[:, to] = moved[:, :part]
+            away[index, :, to] = moved[:, part:]
+
+
+def prepare(lat, cot):
+    tokens, width = lat.shape
+    shape = tokens, width // 2
+    one = jax.ShapeDtypeStruct(shape, BF)
+    return pl.pallas_call(
+        prepare_kernel,
+        out_shape=(one, one, jax.ShapeDtypeStruct((2, *shape), BF)),
+        in_specs=[VMEM] * 2,
+        out_specs=(VMEM,) * 3,
         compiler_params=pltpu.CompilerParams(vmem_limit_bytes=LIMIT),
         name="prepare",
-    )(value)
-
-
-def multiply(lat, cot, w, mine, theirs):
-    c = lax.axis_index("c")
-    head = w.shape[1] // 4
-    count = lat.shape[0] // 2
-    for tokens, at in ((lat, slice(0, 3 * head)), (cot, slice(3 * head, 4 * head))):
-        value = jnp.dot(tokens[...], w[:, at], preferred_element_type=F32)
-        to = (mine.shape[0], mine.shape[1], at.stop - at.start)
-        low, high = value[:count], value[count:]
-        mine[:, :, at] = jnp.where(c == 0, low, high).reshape(to)
-        theirs[:, :, at] = jnp.where(c == 0, high, low).reshape(to).astype(BF)
-
-
-def project_own_kernel(blocks, lat, cot, w, mine, theirs):
+    )(lat, cot)
+
+
+def project_kernel(blocks, own_l, own_c, arrived, mine, theirs, keep, w):
     c = lax.axis_index("c")
     rows = blocks.shape[1]
     for yl, x, half, even, odd in half_shards():
         place = (yl * NX + x) * 2 + half
         w[place * rows : (place + 1) * rows] = blocks[jnp.where(c == 0, even, odd)]
-    multiply(lat, cot, w, mine, theirs)
-
-
-def project_both_kernel(w, lat, cot, own_mine, own_theirs, mine, theirs, new_mine, new_theirs):
-    c = lax.axis_index("c")
-    multiply(lat, cot, w, new_mine, new_theirs)
-    for own, new, to in ((own_mine, new_mine, mine), (own_theirs, new_theirs, theirs)):
-        to[:, c] = own[...]
-        to[:, 1 - c] = new[...]
-
-
-def project(blocks, own_l, own_c, arr_l, arr_c):
+    head = w.shape[1] // 4
+    count = own_l.shape[0] // 2
+    for frame, lat, cot in ((c, own_l, own_c), (1 - c, arrived.at[0], arrived.at[1])):
+        for tokens, at in ((lat, slice(0, 3 * head)), (cot, slice(3 * head, 4 * head))):
+            value = jnp.dot(tokens[...], w[:, at], preferred_element_type=F32)
+            to = (mine.shape[0], mine.shape[2], at.stop - at.start)
+            low, high = value[:count], value[count:]
+            mine[:, frame, :, at] = jnp.where(c == 0, low, high).reshape(to)
+            theirs[:, frame, :, at] = jnp.where(c == 0, high, low).reshape(to).astype(BF)
+    keep[...] = arrived[...]
+
+
+def project(blocks, own_l, own_c, arrived):
     tokens, width = own_l.shape
     columns = blocks.shape[-1]
     chips = NYL * NX
-    rows = tokens // (chips * NC)
-    half, whole = (chips, rows, columns), (chips, NC, rows, columns)
-    params = pltpu.CompilerParams(vmem_limit_bytes=LIMIT)
-    w, mine, theirs = pl.pallas_call(
-        project_own_kernel,
-        out_shape=(
-            jax.ShapeDtypeStruct((width, columns), BF),
-            jax.ShapeDtypeStruct(half, F32),
-            jax.ShapeDtypeStruct(half, BF),
-        ),
-        in_specs=[VMEM] * 3,
+    shape = (chips, NC, tokens // (chips * NC), columns)
+    kept = jax.ShapeDtypeStruct(arrived.shape, BF)
+    return pl.pallas_call(
+        project_kernel,
+        out_shape=(jax.ShapeDtypeStruct(shape, F32), jax.ShapeDtypeStruct(shape, BF), kept),
+        in_specs=[VMEM] * 4,
         out_specs=(VMEM,) * 3,
-        compiler_params=params,
-        name="project_own",
-    )(blocks, own_l, own_c)
-    return pl.pallas_call(
-        project_both_kernel,
-        out_shape=(jax.ShapeDtypeStruct(whole, F32), jax.ShapeDtypeStruct(whole, BF)),
-        in_specs=[VMEM] * 5,
-        out_specs=(VMEM,) * 2,
-        scratch_shapes=[pltpu.VMEM(half, F32), pltpu.VMEM(half, BF)],
-        compiler_params=params,
-        name="project_both",
-    )(w, arr_l, arr_c, mine, theirs)
-
-
-def weight_kernel(columns, back, own, arrived, *rest):
-    blocks, grads = rest[-2:]
+        scratch_shapes=[pltpu.VMEM((width, columns), BF)],
+        compiler_params=pltpu.CompilerParams(vmem_limit_bytes=LIMIT),
+        name="project",
+    )(blocks, own_l, own_c, arrived)
+
+
+def weight_kernel(back, own_l, own_c, arrived, blocks, grads):
     c = lax.axis_index("c")
-    _, chips, _, patches, _ = back.shape
+    _, chips, _, patches, columns = back.shape
+    head = columns // 4
     count = chips * patches
     rows = blocks.shape[1]
-    source, to = columns
     for index, frame in ((0, c), (1, 1 - c)):
         for half in range(2):
-            value = back[half, :, frame, :, source].astype(F32)
-            grads[index, half * count : (half + 1) * count] = value.reshape(count, -1).astype(BF)
+            value = back[half, :, frame].astype(F32).reshape(count, columns)
+            grads[index, half * count : (half + 1) * count] = value.astype(BF)
     wide = NX * 2 * rows
-    for yl in range(NYL):
-        part = slice(yl * wide, (yl + 1) * wide)
-        value = 0.0
-        for index, tokens in ((0, own), (1, arrived)):
-            value = value + lax.dot_general(
-                tokens[:, part], grads[index], (((0,), (0,)), ((), ())), preferred_element_type=F32
-            )
-        value = value.astype(BF)
-        for y, x, half, even, odd in half_shards():
-            if y == yl:
-                piece = value[(x * 2 + half) * rows : (x * 2 + half + 1) * rows]
-                blocks[jnp.where(c == 0, even, odd), :, to] = piece
-
-
-def weight_parts(back, own_l, own_c, arr_l, arr_c):
+
+    def multiply(own, arrived, at, to):
+        for yl in range(NYL):
+            part = slice(yl * wide, (yl + 1) * wide)
+            value = 0.0
+            for index, tokens in ((0, own), (1, arrived)):
+                value = value + lax.dot_general(
+                    tokens[:, part],
+                    grads[index, :, at],
+                    (((0,), (0,)), ((), ())),
+                    preferred_element_type=F32,
+                )
+            value = value.astype(BF)
+            for y, x, half, even, odd in half_shards():
+                if y == yl:
+                    piece = value[(x * 2 + half) * rows : (x * 2 + half + 1) * rows]
+                    blocks[jnp.where(c == 0, even, odd), :, to] = piece
+
+    multiply(own_l, arrived.at[0], slice(head, 4 * head), slice(0, 3 * head))
+    multiply(own_c, arrived.at[1], slice(0, head), slice(3 * head, 4 * head))
+
+
+def weight_parts(back, own_l, own_c, arrived):
     tokens, width = own_l.shape
     columns = back.shape[-1]
-    head = columns // 4
     count = NYL * NX * 2
-
-    def call(source, to, own, arrived, *blocks):
-        return pl.pallas_call(
-            functools.partial(weight_kernel, (source, to)),
-            out_shape=jax.ShapeDtypeStruct((count, width // count, columns), BF),
-            in_specs=[VMEM] * (3 + len(blocks)),
-            out_specs=VMEM,
-            scratch_shapes=[pltpu.VMEM((2, tokens, source.stop - source.start), BF)],
-            input_output_aliases={3: 0} if blocks else {},
-            compiler_params=pltpu.CompilerParams(vmem_limit_bytes=LIMIT),
-            name="weight_parts",
-        )(back, own, arrived, *blocks)
-
-    blocks = call(slice(head, 4 * head), slice(0, 3 * head), own_l, arr_l)
-    return call(slice(0, head), slice(3 * head, 4 * head), own_c, arr_c, blocks)
+    return pl.pallas_call(
+        weight_kernel,
+        out_shape=jax.ShapeDtypeStruct((count, width // count, columns), BF),
+        in_specs=[VMEM] * 4,
+        out_specs=VMEM,
+        scratch_shapes=[pltpu.VMEM((2, tokens, columns), BF)],
+        compiler_params=pltpu.CompilerParams(vmem_limit_bytes=LIMIT),
+        name="weight_parts",
+    )(back, own_l, own_c, arrived)
 
 
 def attend_kernel(packed, result):
@@ -321,11 +297,10 @@
 def shards(latents, cotangent, weights):
     width = latents.shape[-1]
     columns = weights.shape[1]
-    own_l, away_l = prepare(latents.reshape(-1, width), True)
-    own_c, away_c = prepare(cotangent.reshape(-1, width), False)
+    own_l, own_c, away = prepare(latents.reshape(-1, width), cotangent.reshape(-1, width))
     blocks, own_l = gather(weights, own_l)
-    tokens = own_l, own_c, other_core(away_l), other_core(away_c)
-    mine, theirs = project(blocks, *tokens)
+    mine, theirs, arrived = project(blocks, own_l, own_c, other_core(away))
+    tokens = own_l, own_c, arrived
     both = lax.all_gather(theirs, "c")
     part = lax.dynamic_index_in_dim(both, 1 - lax.axis_index("c"), keepdims=False)
     packed = exchange((mine + part.astype(F32)).astype(BF), PLANE)

time: 136 us -> 135 us (level)
  waiting for transfers between devices: 2.45 us -> 7.97 us
  local copies, waits for them, and re-layouts: 8.6 us -> 5.62 us
  starting transfers between devices: 27.8 us -> 24.9 us
    ppermute x2 -> x1, waiting for transfers between devices: 0.01 us -> 3.72 us  [other_core(): return lax.ppermute(v, 'c', [(0, 1), (1, 0)])]
    unnamed x18 -> x8, local copies, waits for them, and re-layouts: 7.84 us -> 4.86 us
    ppermute x2 -> x1, starting transfers between devices: 4.3 us -> 1.91 us  [other_core(): return lax.ppermute(v, 'c', [(0, 1), (1, 0)])]
    all_to_all x2, waiting for transfers between devices: 2.44 us -> 4.26 us  [exchange(): lax.all_to_all(v, AXES, split_axis=0, concat_axis=0, axis_index_groups=me...]
    pallas_call x6 -> x3, Pallas kernels: 8.22 us -> 7.32 us  [the longest x1 2.99 us: prepare(): pl.pallas_call(prepare_kernel, out_shape=(one, one, jax.ShapeDtypeStruct(...]
  transfers between devices with their start and end apart: 4 -> 3, of which waited for: 2 -> 2; matrix products, arithmetic and copies ran while one was open for 0% -> 0% of each run, Pallas kernels for 4% -> 2%
where the time goes in v7:
time: 135 us; the launch traced here: 132 us
  blocking collectives  83.1 us (62%)
  starting transfers between devices  24.9 us (18%)
  Pallas kernels  10.1 us (7%)
  waiting for transfers between devices  7.97 us (6%)
  local copies, waits for them, and re-layouts  5.62 us (4%)
    all_to_all x5, blocking collectives, exchange(): lax.all_to_all(v, AXES, split_axis=0, concat_axis=0, axis_index_groups=me...  74.4 us
    all_to_all x2, starting transfers between devices, exchange(): lax.all_to_all(v, AXES, split_axis=0, concat_axis=0, axis_index_groups=me...  23 us
    all_gather x1, blocking collectives, shards(): back = lax.all_gather(exchange(result.reshape(packed.shape), PLANE), 'c')  6.5 us
    unnamed x8, local copies, waits for them, and re-layouts  4.86 us
    all_to_all x2, waiting for transfers between devices, exchange(): lax.all_to_all(v, AXES, split_axis=0, concat_axis=0, axis_index_groups=me...  4.26 us
    ppermute x1, waiting for transfers between devices, other_core(): return lax.ppermute(v, 'c', [(0, 1), (1, 0)])  3.72 us
    pallas_call x1, Pallas kernels, prepare(): pl.pallas_call(prepare_kernel, out_shape=(one, one, jax.ShapeDtypeStruct(...  2.99 us
    pallas_call x1, Pallas kernels, project(): pl.pallas_call(project_kernel, out_shape=(jax.ShapeDtypeStruct(shape, F32...  2.91 us
  transfers between devices with their start and end apart: 3, of which 2 were waited for; matrix products, arithmetic and copies ran while one was open for 0% of the time, Pallas kernels for 2%

profile of v7, /device:TPU:1, one launch (start us, length us, event | category | flops | bytes accessed | tf_op | source)
XLA Modules:
  0.0 132.2 jit_solution(2905710218774254573)
XLA Ops:
  0.0 0.9 copy-done
  0.9 0.7 broadcast_in_dim.4
  1.6 6.9 %all-to-all-start = ((bf16[4,48,512]{2,1,0:T(8,128)(2,1)}), bf16[4,48,512]{2,1,0:T(8,128)(2,1)S(1)}, u32[]{:S(2)}, u32[]{:S(2)}) async-start(bf16[4,48,512]{2,1,0:T(8,128)(2,1)} %broadcast_in_dim.4), calls=%async_computation | async-start | bytes 393216 | tf_op jit(solution)/shard_map/all_to_all | solution.py:64
  8.5 1.4 %copy-done.1 = bf16[1,1,256,3072]{3,2,1,0:T(8,128)(2,1)S(1)} copy-done((bf16[1,1,256,3072]{3,2,1,0:T(8,128)(2,1)S(1)}, bf16[1,1,256,3072]{3,2,1,0:T(8,128)(2,1)}, u32[]{:S(2)}) %copy-start.1) | copy-done | bytes 1572888
  9.9 1.4 %copy-done.2 = bf16[1,1,256,3072]{3,2,1,0:T(8,128)(2,1)S(1)} copy-done((bf16[1,1,256,3072]{3,2,1,0:T(8,128)(2,1)S(1)}, bf16[1,1,256,3072]{3,2,1,0:T(8,128)(2,1)}, u32[]{:S(2)}) %copy-start.2) | copy-done | bytes 1572888
  11.3 3.0 %prepare.1 = (bf16[256,1536]{1,0:T(8,128)(2,1)S(1)}, bf16[256,1536]{1,0:T(8,128)(2,1)S(1)}, bf16[2,256,1536]{2,1,0:T(8,128)(2,1)S(1)}) custom-call(bf16[256,3072]{1,0:T(8,128)(2,1)S(1)} %bitcast.16, bf16[256,3072]{1,0:T(8,128)(2,1)S(1)} %bitcast.17), custom_call_target="tpu_custom_call" | custom-call | tf_op jit(solution)/shard_map/prepare/pallas_call | solution.py:105
  14.3 1.2 copy-done.3
  15.4 1.2 repeat.1
  16.7 16.1 %all-to-all-start.1 = ((bf16[8,4,48,512]{3,2,1,0:T(8,128)(2,1)}), bf16[8,4,48,512]{3,2,1,0:T(8,128)(2,1)S(1)}, u32[]{:S(2)}, u32[]{:S(2)}) async-start(bf16[8,4,48,512]{3,2,1,0:T(8,128)(2,1)} %repeat.1), calls=%async_computation.1 | async-start | bytes 3145728 | tf_op jit(solution)/shard_map/all_to_all | solution.py:64
  32.8 1.9 %collective-permute-start = (bf16[2,256,1536]{2,1,0:T(8,128)(2,1)}, bf16[2,256,1536]{2,1,0:T(8,128)(2,1)}, u32[]{:S(2)}, u32[]{:S(2)}) collective-permute-start(bf16[2,256,1536]{2,1,0:T(8,128)(2,1)} %copy-done.3), channel_id=1, source_target_pairs={{0,1},{1,0},{2,3},{3,2},{4,5},{5,4},{6,7},{7,6},{8,9},{9,8},{10,11... | collective-permute-start | bytes 4718600 | tf_op jit(solution)/shard_map/ppermute | solution.py:60
  34.7 3.7 %collective-permute-done.arrived = bf16[2,256,1536]{2,1,0:T(8,128)(2,1)} collective-permute-done((bf16[2,256,1536]{2,1,0:T(8,128)(2,1)}, bf16[2,256,1536]{2,1,0:T(8,128)(2,1)}, u32[]{:S(2)}, u32[]{:S(2)}) %collective-permute-start) | collective-permute-done | bytes 1572896 | tf_op jit(solution)/shard_map/ppermute | solution.py:60
  38.4 4.3 %all-to-all-done.1 = bf16[8,4,48,512]{3,2,1,0:T(8,128)(2,1)S(1)} async-done(((bf16[8,4,48,512]{3,2,1,0:T(8,128)(2,1)}), bf16[8,4,48,512]{3,2,1,0:T(8,128)(2,1)S(1)}, u32[]{:S(2)}, u32[]{:S(2)}) %all-to-all-start.1) | async-done | bytes 1572896 | tf_op jit(solution)/shard_map/all_to_all | solution.py:64
  42.7 2.9 %project.1 = (f32[16,2,8,512]{3,2,1,0:T(8,128)S(1)}, bf16[16,2,8,512]{3,2,1,0:T(8,128)(2,1)S(1)}, bf16[2,256,1536]{2,1,0:T(8,128)(2,1)S(1)}) custom-call(bf16[32,48,512]{2,1,0:T(8,128)(2,1)S(1)} %bitcast.13, bf16[256,1536]{1,0:T(8,128)(2,1)S(1)} %get-tuple-element.15.own_l, bf16[256,1536]{1,0:T(8,128)(2,1)S(1)} %get-tuple-element.16.own_c, ...), custom_call_target="tpu_custom_call" | custom-call | tf_op jit(solution)/shard_map/project/pallas_call | solution.py:139
  45.6 2.2 %all-gather = bf16[32,2,8,512]{3,2,1,0:T(8,128)(2,1)S(1)} all-gather(bf16[16,2,8,512]{3,2,1,0:T(8,128)(2,1)S(1)} %get-tuple-element.19), channel_id=2, replica_groups=mesh['z'=8,'yh'=2,'yl'=4,'x'=4,'c'=2] {'c'}, dimensions={0}, use_global_device_ids=true | all-gather | bytes 786432 | tf_op jit(solution)/shard_map/all_gather | solution.py:304
  47.9 11.7 %all_to_all.35 = bf16[16,2,8,512]{3,2,1,0:T(8,128)(2,1)S(1)} all-to-all(bf16[16,2,8,512]{3,2,1,0:T(8,128)(2,1)S(1)} %fusion), channel_id=1, replica_groups={{24,26,28,30,0,2,4,6,8,10,12,14,16,18,20,22},{13,15,9,11,21,23,17,19,29..., dimensions={0} | all-to-all | bytes 524288 | tf_op jit(solution)/shard_map/all_to_all | solution.py:64
  59.6 0.9 attend.1
  60.5 11.9 %all_to_all.36 = bf16[16,2,8,512]{3,2,1,0:T(8,128)(2,1)S(1)} all-to-all(bf16[16,2,8,512]{3,2,1,0:T(8,128)(2,1)S(1)} %bitcast.19), channel_id=1, replica_groups={{24,26,28,30,0,2,4,6,8,10,12,14,16,18,20,22},{13,15,9,11,21,23,17,19,29..., dimensions={0} | all-to-all | bytes 524288 | tf_op jit(solution)/shard_map/all_to_all | solution.py:64
  72.4 6.5 %all-gather.1 = bf16[32,2,8,512]{3,2,1,0:T(8,128)(2,1)S(1)} all-gather(bf16[16,2,8,512]{3,2,1,0:T(8,128)(2,1)S(1)} %all_to_all.36), channel_id=3, replica_groups=mesh['z'=8,'yh'=2,'yl'=4,'x'=4,'c'=2] {'c'}, dimensions={0}, use_global_device_ids=true | all-gather | bytes 786432 | tf_op jit(solution)/shard_map/all_gather | solution.py:308
  78.9 1.4 %weight_parts.1 = bf16[32,48,512]{2,1,0:T(8,128)(2,1)S(1)} custom-call(bf16[2,16,2,8,512]{4,3,2,1,0:T(8,128)(2,1)S(1)} %bitcast.15, bf16[256,1536]{1,0:T(8,128)(2,1)S(1)} %get-tuple-element.15.own_l, bf16[256,1536]{1,0:T(8,128)(2,1)S(1)} %get-tuple-element.16.own_c, bf16[2,256,1536]{2,1,0:T(8,128)(2,1)S(1)} %get-tuple-element.20.arrived), custom_call_target="tpu_custom_call" | custom-call | tf_op jit(solution)/shard_map/weight_parts/pallas_call | solution.py:187
  80.3 18.7 %all_to_all.37 = bf16[8,4,48,512]{3,2,1,0:T(8,128)(2,1)S(1)} all-to-all(bf16[8,4,48,512]{3,2,1,0:T(8,128)(2,1)S(1)} %bitcast.14), channel_id=1, replica_groups={{0,64,2,66,8,72,10,74},{511,63,505,57,455,7,449,1},{507,59,509,61,451,3..., dimensions={0} | all-to-all | bytes 3145728 | tf_op jit(solution)/shard_map/all_to_all | solution.py:64
  99.0 0.3 reduce_sum.24
  99.4 14.5 %all_to_all.38 = bf16[16,48,128]{2,1,0:T(8,128)(2,1)S(1)} all-to-all(bf16[16,48,128]{2,1,0:T(8,128)(2,1)S(1)} %bitcast.22), channel_id=1, replica_groups={{0,128,256,384,4,132,260,388,16,144,272,400,20,148,276,404},{1,129,257,..., dimensions={0} | all-to-all | bytes 393216 | tf_op jit(solution)/shard_map/all_to_all | solution.py:64
  114.0 17.5 %all_to_all.39 = bf16[16,48,128]{2,1,0:T(8,128)(2,1)S(1)} all-to-all(bf16[16,48,128]{2,1,0:T(8,128)(2,1)S(1)} %broadcast_in_dim.5), channel_id=1, replica_groups={{0,32,64,96,128,160,192,224,256,288,320,352,384,416,448,480},{449,481,1..., dimensions={0} | all-to-all | bytes 393216 | tf_op jit(solution)/shard_map/all_to_all | solution.py:64
  131.5 0.7 finish.1
  (11 shorter events, 0.2 us)
Async XLA Ops:
  0.0 0.9 copy-start
  1.6 13.8 %all-to-all-start = ((bf16[4,48,512]{2,1,0:T(8,128)(2,1)}), bf16[4,48,512]{2,1,0:T(8,128)(2,1)S(1)}, u32[]{:S(2)}, u32[]{:S(2)}) async-start(bf16[4,48,512]{2,1,0:T(8,128)(2,1)} %broadcast_in_dim.4), calls=%async_computation | async-start | bytes 393216 | tf_op jit(solution)/shard_map/all_to_all | solution.py:64
  8.5 1.4 %copy-start.1 = (bf16[1,1,256,3072]{3,2,1,0:T(8,128)(2,1)S(1)}, bf16[1,1,256,3072]{3,2,1,0:T(8,128)(2,1)}, u32[]{:S(2)}) copy-start(bf16[1,1,256,3072]{3,2,1,0:T(8,128)(2,1)} %param.3) | copy-start | bytes 4718596
  9.9 1.4 %copy-start.2 = (bf16[1,1,256,3072]{3,2,1,0:T(8,128)(2,1)S(1)}, bf16[1,1,256,3072]{3,2,1,0:T(8,128)(2,1)}, u32[]{:S(2)}) copy-start(bf16[1,1,256,3072]{3,2,1,0:T(8,128)(2,1)} %param.4) | copy-start | bytes 4718596
  14.3 1.2 copy-start.3
  16.7 26.0 %all-to-all-start.1 = ((bf16[8,4,48,512]{3,2,1,0:T(8,128)(2,1)}), bf16[8,4,48,512]{3,2,1,0:T(8,128)(2,1)S(1)}, u32[]{:S(2)}, u32[]{:S(2)}) async-start(bf16[8,4,48,512]{3,2,1,0:T(8,128)(2,1)} %repeat.1), calls=%async_computation.1 | async-start | bytes 3145728 | tf_op jit(solution)/shard_map/all_to_all | solution.py:64
  32.8 5.6 %collective-permute-start = (bf16[2,256,1536]{2,1,0:T(8,128)(2,1)}, bf16[2,256,1536]{2,1,0:T(8,128)(2,1)}, u32[]{:S(2)}, u32[]{:S(2)}) collective-permute-start(bf16[2,256,1536]{2,1,0:T(8,128)(2,1)} %copy-done.3), channel_id=1, source_target_pairs={{0,1},{1,0},{2,3},{3,2},{4,5},{5,4},{6,7},{7,6},{8,9},{9,8},{10,11... | collective-permute-start | bytes 4718600 | tf_op jit(solution)/shard_map/ppermute | solution.py:60

commit v8 on v7

--- a/solution.py
+++ b/solution.py
@@ -79,23 +79,25 @@
     rows = width // (NYL * NX * NC)
     block = NX * NC * rows
     part = block // 2
-    source = lax.broadcasted_iota(jnp.int32, (block, block), 0)
-    k = lax.broadcasted_iota(jnp.int32, (block, block), 1)
-    second = (k >= part).astype(jnp.int32)
-    k = k - part * second
-    wanted = k + rows * (second + c - 2 * c * second)
-    for b in range(1, NX):
-        wanted = wanted + rows * (k >= b * rows).astype(jnp.int32)
-    pick = (source == wanted).astype(F32).astype(BF)
+    source = lax.broadcasted_iota(jnp.int32, (part, part), 0)
+    k = lax.broadcasted_iota(jnp.int32, (part, part), 1)
+    second = (k >= part // 2).astype(jnp.int32)
+    k = k - part // 2 * second
+    k = k + rows * (k >= rows).astype(jnp.int32)
+    parity = second + c - 2 * c * second
+    low = (source == k + rows * parity).astype(F32).astype(BF)
+    high = (source == k + rows * (1 - parity)).astype(F32).astype(BF)
+    first = lax.broadcasted_iota(jnp.int32, (lat.shape[0], part), 1) < part // 2
     wide = lat[...].astype(F32)
     r = lax.rsqrt(jnp.mean(wide * wide, axis=-1, keepdims=True) + 1e-06)
     for a in range(NYL):
         at, to = slice(a * block, (a + 1) * block), slice(a * part, (a + 1) * part)
         normed = (lat[:, at].astype(F32) * r).astype(BF)
         for index, own, tokens in ((0, own_l, normed), (1, own_c, cot[:, at])):
-            moved = jnp.dot(tokens, pick, preferred_element_type=F32).astype(BF)
-            own[:, to] = moved[:, :part]
-            away[index, :, to] = moved[:, part:]
+            one = jnp.dot(tokens[:, :part], low, preferred_element_type=F32)
+            two = jnp.dot(tokens[:, part:], high, preferred_element_type=F32)
+            own[:, to] = jnp.where(first, one, two).astype(BF)
+            away[index, :, to] = pltpu.roll(jnp.where(first, two, one), part // 2, 1).astype(BF)
 
 
 def prepare(lat, cot):

time: 135 us -> 135 us (level)
  no operation moved by 1% of the time
where the time goes in v8:
time: 135 us; the launch traced here: 132 us
  blocking collectives  83.1 us (62%)
  starting transfers between devices  25.4 us (19%)
  Pallas kernels  9.65 us (7%)
  waiting for transfers between devices  7.97 us (6%)
  local copies, waits for them, and re-layouts  5.62 us (4%)
    all_to_all x5, blocking collectives, exchange(): lax.all_to_all(v, AXES, split_axis=0, concat_axis=0, axis_index_groups=me...  75 us
    all_to_all x2, starting transfers between devices, exchange(): lax.all_to_all(v, AXES, split_axis=0, concat_axis=0, axis_index_groups=me...  23.5 us
    all_gather x1, blocking collectives, shards(): back = lax.all_gather(exchange(result.reshape(packed.shape), PLANE), 'c')  6.01 us
    unnamed x8, local copies, waits for them, and re-layouts  4.86 us
    all_to_all x2, waiting for transfers between devices, exchange(): lax.all_to_all(v, AXES, split_axis=0, concat_axis=0, axis_index_groups=me...  4.26 us
    ppermute x1, waiting for transfers between devices, other_core(): return lax.ppermute(v, 'c', [(0, 1), (1, 0)])  3.72 us
    pallas_call x1, Pallas kernels, project(): pl.pallas_call(project_kernel, out_shape=(jax.ShapeDtypeStruct(shape, F32...  2.91 us
  transfers between devices with their start and end apart: 3, of which 2 were waited for; matrix products, arithmetic and copies ran while one was open for 0% of the time, Pallas kernels for 2%

profile of v8, /device:TPU:1, one launch (start us, length us, event | category | flops | bytes accessed | tf_op | source)
XLA Modules:
  0.0 132.2 jit_solution(7093454143806936434)
XLA Ops:
  0.0 0.9 copy-done
  0.9 0.7 broadcast_in_dim.4
  1.6 6.9 %all-to-all-start = ((bf16[4,48,512]{2,1,0:T(8,128)(2,1)}), bf16[4,48,512]{2,1,0:T(8,128)(2,1)S(1)}, u32[]{:S(2)}, u32[]{:S(2)}) async-start(bf16[4,48,512]{2,1,0:T(8,128)(2,1)} %broadcast_in_dim.4), calls=%async_computation | async-start | bytes 393216 | tf_op jit(solution)/shard_map/all_to_all | solution.py:64
  8.5 1.4 %copy-done.1 = bf16[1,1,256,3072]{3,2,1,0:T(8,128)(2,1)S(1)} copy-done((bf16[1,1,256,3072]{3,2,1,0:T(8,128)(2,1)S(1)}, bf16[1,1,256,3072]{3,2,1,0:T(8,128)(2,1)}, u32[]{:S(2)}) %copy-start.1) | copy-done | bytes 1572888
  9.9 1.4 %copy-done.2 = bf16[1,1,256,3072]{3,2,1,0:T(8,128)(2,1)S(1)} copy-done((bf16[1,1,256,3072]{3,2,1,0:T(8,128)(2,1)S(1)}, bf16[1,1,256,3072]{3,2,1,0:T(8,128)(2,1)}, u32[]{:S(2)}) %copy-start.2) | copy-done | bytes 1572888
  11.3 2.5 %prepare.1 = (bf16[256,1536]{1,0:T(8,128)(2,1)S(1)}, bf16[256,1536]{1,0:T(8,128)(2,1)S(1)}, bf16[2,256,1536]{2,1,0:T(8,128)(2,1)S(1)}) custom-call(bf16[256,3072]{1,0:T(8,128)(2,1)S(1)} %bitcast.16, bf16[256,3072]{1,0:T(8,128)(2,1)S(1)} %bitcast.17), custom_call_target="tpu_custom_call" | custom-call | tf_op jit(solution)/shard_map/prepare/pallas_call | solution.py:107
  13.8 1.2 copy-done.3
  15.0 1.2 repeat.1
  16.2 16.6 %all-to-all-start.1 = ((bf16[8,4,48,512]{3,2,1,0:T(8,128)(2,1)}), bf16[8,4,48,512]{3,2,1,0:T(8,128)(2,1)S(1)}, u32[]{:S(2)}, u32[]{:S(2)}) async-start(bf16[8,4,48,512]{3,2,1,0:T(8,128)(2,1)} %repeat.1), calls=%async_computation.1 | async-start | bytes 3145728 | tf_op jit(solution)/shard_map/all_to_all | solution.py:64
  32.8 1.9 %collective-permute-start = (bf16[2,256,1536]{2,1,0:T(8,128)(2,1)}, bf16[2,256,1536]{2,1,0:T(8,128)(2,1)}, u32[]{:S(2)}, u32[]{:S(2)}) collective-permute-start(bf16[2,256,1536]{2,1,0:T(8,128)(2,1)} %copy-done.3), channel_id=1, source_target_pairs={{0,1},{1,0},{2,3},{3,2},{4,5},{5,4},{6,7},{7,6},{8,9},{9,8},{10,11... | collective-permute-start | bytes 4718600 | tf_op jit(solution)/shard_map/ppermute | solution.py:60
  34.7 3.7 %collective-permute-done.arrived = bf16[2,256,1536]{2,1,0:T(8,128)(2,1)} collective-permute-done((bf16[2,256,1536]{2,1,0:T(8,128)(2,1)}, bf16[2,256,1536]{2,1,0:T(8,128)(2,1)}, u32[]{:S(2)}, u32[]{:S(2)}) %collective-permute-start) | collective-permute-done | bytes 1572896 | tf_op jit(solution)/shard_map/ppermute | solution.py:60
  38.4 4.3 %all-to-all-done.1 = bf16[8,4,48,512]{3,2,1,0:T(8,128)(2,1)S(1)} async-done(((bf16[8,4,48,512]{3,2,1,0:T(8,128)(2,1)}), bf16[8,4,48,512]{3,2,1,0:T(8,128)(2,1)S(1)}, u32[]{:S(2)}, u32[]{:S(2)}) %all-to-all-start.1) | async-done | bytes 1572896 | tf_op jit(solution)/shard_map/all_to_all | solution.py:64
  42.7 2.9 %project.1 = (f32[16,2,8,512]{3,2,1,0:T(8,128)S(1)}, bf16[16,2,8,512]{3,2,1,0:T(8,128)(2,1)S(1)}, bf16[2,256,1536]{2,1,0:T(8,128)(2,1)S(1)}) custom-call(bf16[32,48,512]{2,1,0:T(8,128)(2,1)S(1)} %bitcast.13, bf16[256,1536]{1,0:T(8,128)(2,1)S(1)} %get-tuple-element.15.own_l, bf16[256,1536]{1,0:T(8,128)(2,1)S(1)} %get-tuple-element.16.own_c, ...), custom_call_target="tpu_custom_call" | custom-call | tf_op jit(solution)/shard_map/project/pallas_call | solution.py:141
  45.6 2.2 %all-gather = bf16[32,2,8,512]{3,2,1,0:T(8,128)(2,1)S(1)} all-gather(bf16[16,2,8,512]{3,2,1,0:T(8,128)(2,1)S(1)} %get-tuple-element.19), channel_id=2, replica_groups=mesh['z'=8,'yh'=2,'yl'=4,'x'=4,'c'=2] {'c'}, dimensions={0}, use_global_device_ids=true | all-gather | bytes 786432 | tf_op jit(solution)/shard_map/all_gather | solution.py:306
  47.9 12.2 %all_to_all.35 = bf16[16,2,8,512]{3,2,1,0:T(8,128)(2,1)S(1)} all-to-all(bf16[16,2,8,512]{3,2,1,0:T(8,128)(2,1)S(1)} %fusion), channel_id=1, replica_groups={{24,26,28,30,0,2,4,6,8,10,12,14,16,18,20,22},{13,15,9,11,21,23,17,19,29..., dimensions={0} | all-to-all | bytes 524288 | tf_op jit(solution)/shard_map/all_to_all | solution.py:64
  60.0 0.9 attend.1
  60.9 11.5 %all_to_all.36 = bf16[16,2,8,512]{3,2,1,0:T(8,128)(2,1)S(1)} all-to-all(bf16[16,2,8,512]{3,2,1,0:T(8,128)(2,1)S(1)} %bitcast.19), channel_id=1, replica_groups={{24,26,28,30,0,2,4,6,8,10,12,14,16,18,20,22},{13,15,9,11,21,23,17,19,29..., dimensions={0} | all-to-all | bytes 524288 | tf_op jit(solution)/shard_map/all_to_all | solution.py:64
  72.4 6.0 %all-gather.1 = bf16[32,2,8,512]{3,2,1,0:T(8,128)(2,1)S(1)} all-gather(bf16[16,2,8,512]{3,2,1,0:T(8,128)(2,1)S(1)} %all_to_all.36), channel_id=3, replica_groups=mesh['z'=8,'yh'=2,'yl'=4,'x'=4,'c'=2] {'c'}, dimensions={0}, use_global_device_ids=true | all-gather | bytes 786432 | tf_op jit(solution)/shard_map/all_gather | solution.py:310
  78.4 1.4 %weight_parts.1 = bf16[32,48,512]{2,1,0:T(8,128)(2,1)S(1)} custom-call(bf16[2,16,2,8,512]{4,3,2,1,0:T(8,128)(2,1)S(1)} %bitcast.15, bf16[256,1536]{1,0:T(8,128)(2,1)S(1)} %get-tuple-element.15.own_l, bf16[256,1536]{1,0:T(8,128)(2,1)S(1)} %get-tuple-element.16.own_c, bf16[2,256,1536]{2,1,0:T(8,128)(2,1)S(1)} %get-tuple-element.20.arrived), custom_call_target="tpu_custom_call" | custom-call | tf_op jit(solution)/shard_map/weight_parts/pallas_call | solution.py:189
  79.8 18.7 %all_to_all.37 = bf16[8,4,48,512]{3,2,1,0:T(8,128)(2,1)S(1)} all-to-all(bf16[8,4,48,512]{3,2,1,0:T(8,128)(2,1)S(1)} %bitcast.14), channel_id=1, replica_groups={{0,64,2,66,8,72,10,74},{511,63,505,57,455,7,449,1},{507,59,509,61,451,3..., dimensions={0} | all-to-all | bytes 3145728 | tf_op jit(solution)/shard_map/all_to_all | solution.py:64
  98.6 0.3 reduce_sum.24
  98.9 14.7 %all_to_all.38 = bf16[16,48,128]{2,1,0:T(8,128)(2,1)S(1)} all-to-all(bf16[16,48,128]{2,1,0:T(8,128)(2,1)S(1)} %bitcast.22), channel_id=1, replica_groups={{0,128,256,384,4,132,260,388,16,144,272,400,20,148,276,404},{1,129,257,..., dimensions={0} | all-to-all | bytes 393216 | tf_op jit(solution)/shard_map/all_to_all | solution.py:64
  113.6 17.9 %all_to_all.39 = bf16[16,48,128]{2,1,0:T(8,128)(2,1)S(1)} all-to-all(bf16[16,48,128]{2,1,0:T(8,128)(2,1)S(1)} %broadcast_in_dim.5), channel_id=1, replica_groups={{0,32,64,96,128,160,192,224,256,288,320,352,384,416,448,480},{449,481,1..., dimensions={0} | all-to-all | bytes 393216 | tf_op jit(solution)/shard_map/all_to_all | solution.py:64
  131.5 0.7 finish.1
  (11 shorter events, 0.2 us)
Async XLA Ops:
  0.0 0.9 copy-start
  1.6 13.4 %all-to-all-start = ((bf16[4,48,512]{2,1,0:T(8,128)(2,1)}), bf16[4,48,512]{2,1,0:T(8,128)(2,1)S(1)}, u32[]{:S(2)}, u32[]{:S(2)}) async-start(bf16[4,48,512]{2,1,0:T(8,128)(2,1)} %broadcast_in_dim.4), calls=%async_computation | async-start | bytes 393216 | tf_op jit(solution)/shard_map/all_to_all | solution.py:64
  8.5 1.4 %copy-start.1 = (bf16[1,1,256,3072]{3,2,1,0:T(8,128)(2,1)S(1)}, bf16[1,1,256,3072]{3,2,1,0:T(8,128)(2,1)}, u32[]{:S(2)}) copy-start(bf16[1,1,256,3072]{3,2,1,0:T(8,128)(2,1)} %param.3) | copy-start | bytes 4718596
  9.9 1.4 %copy-start.2 = (bf16[1,1,256,3072]{3,2,1,0:T(8,128)(2,1)S(1)}, bf16[1,1,256,3072]{3,2,1,0:T(8,128)(2,1)}, u32[]{:S(2)}) copy-start(bf16[1,1,256,3072]{3,2,1,0:T(8,128)(2,1)} %param.4) | copy-start | bytes 4718596
  13.8 1.2 copy-start.3
  16.2 26.5 %all-to-all-start.1 = ((bf16[8,4,48,512]{3,2,1,0:T(8,128)(2,1)}), bf16[8,4,48,512]{3,2,1,0:T(8,128)(2,1)S(1)}, u32[]{:S(2)}, u32[]{:S(2)}) async-start(bf16[8,4,48,512]{3,2,1,0:T(8,128)(2,1)} %repeat.1), calls=%async_computation.1 | async-start | bytes 3145728 | tf_op jit(solution)/shard_map/all_to_all | solution.py:64
  32.8 5.6 %collective-permute-start = (bf16[2,256,1536]{2,1,0:T(8,128)(2,1)}, bf16[2,256,1536]{2,1,0:T(8,128)(2,1)}, u32[]{:S(2)}, u32[]{:S(2)}) collective-permute-start(bf16[2,256,1536]{2,1,0:T(8,128)(2,1)} %copy-done.3), channel_id=1, source_target_pairs={{0,1},{1,0},{2,3},{3,2},{4,5},{5,4},{6,7},{7,6},{8,9},{9,8},{10,11... | collective-permute-start | bytes 4718600 | tf_op jit(solution)/shard_map/ppermute | solution.py:60

commit v9 on v7

--- a/solution.py
+++ b/solution.py
@@ -73,9 +73,9 @@
         yield yl, x, half, *places
 
 
-def prepare_kernel(lat, cot, own_l, own_c, away):
+def prepare_kernel(norm, value, own, away):
     c = lax.axis_index("c")
-    width = lat.shape[1]
+    width = value.shape[1]
     rows = width // (NYL * NX * NC)
     block = NX * NC * rows
     part = block // 2
@@ -87,32 +87,32 @@
     for b in range(1, NX):
         wanted = wanted + rows * (k >= b * rows).astype(jnp.int32)
     pick = (source == wanted).astype(F32).astype(BF)
-    wide = lat[...].astype(F32)
-    r = lax.rsqrt(jnp.mean(wide * wide, axis=-1, keepdims=True) + 1e-06)
+    if norm:
+        wide = value[...].astype(F32)
+        r = lax.rsqrt(jnp.mean(wide * wide, axis=-1, keepdims=True) + 1e-06)
     for a in range(NYL):
-        at, to = slice(a * block, (a + 1) * block), slice(a * part, (a + 1) * part)
-        normed = (lat[:, at].astype(F32) * r).astype(BF)
-        for index, own, tokens in ((0, own_l, normed), (1, own_c, cot[:, at])):
-            moved = jnp.dot(tokens, pick, preferred_element_type=F32).astype(BF)
-            own[:, to] = moved[:, :part]
-            away[index, :, to] = moved[:, part:]
-
-
-def prepare(lat, cot):
-    tokens, width = lat.shape
-    shape = tokens, width // 2
-    one = jax.ShapeDtypeStruct(shape, BF)
-    return pl.pallas_call(
-        prepare_kernel,
-        out_shape=(one, one, jax.ShapeDtypeStruct((2, *shape), BF)),
-        in_specs=[VMEM] * 2,
-        out_specs=(VMEM,) * 3,
+        tokens = value[:, a * block : (a + 1) * block]
+        if norm:
+            tokens = (tokens.astype(F32) * r).astype(BF)
+        moved = jnp.dot(tokens, pick, preferred_element_type=F32).astype(BF)
+        own[:, a * part : (a + 1) * part] = moved[:, :part]
+        away[:, a * part : (a + 1) * part] = moved[:, part:]
+
+
+def prepare(value, norm):
+    tokens, width = value.shape
+    shape = jax.ShapeDtypeStruct((tokens, width // 2), BF)
+    return pl.pallas_call(
+        functools.partial(prepare_kernel, norm),
+        out_shape=(shape, shape),
+        in_specs=[VMEM],
+        out_specs=(VMEM, VMEM),
         compiler_params=pltpu.CompilerParams(vmem_limit_bytes=LIMIT),
         name="prepare",
-    )(lat, cot)
-
-
-def project_kernel(blocks, own_l, own_c, arrived, mine, theirs, keep, w):
+    )(value)
+
+
+def project_kernel(blocks, own_l, own_c, arr_l, arr_c, mine, theirs, keep_l, keep_c, w):
     c = lax.axis_index("c")
     rows = blocks.shape[1]
     for yl, x, half, even, odd in half_shards():
@@ -120,34 +120,35 @@
         w[place * rows : (place + 1) * rows] = blocks[jnp.where(c == 0, even, odd)]
     head = w.shape[1] // 4
     count = own_l.shape[0] // 2
-    for frame, lat, cot in ((c, own_l, own_c), (1 - c, arrived.at[0], arrived.at[1])):
+    for frame, lat, cot in ((c, own_l, own_c), (1 - c, arr_l, arr_c)):
         for tokens, at in ((lat, slice(0, 3 * head)), (cot, slice(3 * head, 4 * head))):
             value = jnp.dot(tokens[...], w[:, at], preferred_element_type=F32)
             to = (mine.shape[0], mine.shape[2], at.stop - at.start)
             low, high = value[:count], value[count:]
             mine[:, frame, :, at] = jnp.where(c == 0, low, high).reshape(to)
             theirs[:, frame, :, at] = jnp.where(c == 0, high, low).reshape(to).astype(BF)
-    keep[...] = arrived[...]
-
-
-def project(blocks, own_l, own_c, arrived):
+    keep_l[...] = arr_l[...]
+    keep_c[...] = arr_c[...]
+
+
+def project(blocks, own_l, own_c, arr_l, arr_c):
     tokens, width = own_l.shape
     columns = blocks.shape[-1]
     chips = NYL * NX
     shape = (chips, NC, tokens // (chips * NC), columns)
-    kept = jax.ShapeDtypeStruct(arrived.shape, BF)
+    kept = jax.ShapeDtypeStruct(arr_l.shape, BF)
     return pl.pallas_call(
         project_kernel,
-        out_shape=(jax.ShapeDtypeStruct(shape, F32), jax.ShapeDtypeStruct(shape, BF), kept),
-        in_specs=[VMEM] * 4,
-        out_specs=(VMEM,) * 3,
+        out_shape=(jax.ShapeDtypeStruct(shape, F32), jax.ShapeDtypeStruct(shape, BF), kept, kept),
+        in_specs=[VMEM] * 5,
+        out_specs=(VMEM,) * 4,
         scratch_shapes=[pltpu.VMEM((width, columns), BF)],
         compiler_params=pltpu.CompilerParams(vmem_limit_bytes=LIMIT),
         name="project",
-    )(blocks, own_l, own_c, arrived)
-
-
-def weight_kernel(back, own_l, own_c, arrived, blocks, grads):
+    )(blocks, own_l, own_c, arr_l, arr_c)
+
+
+def weight_kernel(back, own_l, arr_l, own_c, arr_c, blocks, grads):
     c = lax.axis_index("c")
     _, chips, _, patches, columns = back.shape
     head = columns // 4
@@ -176,23 +177,23 @@
                     piece = value[(x * 2 + half) * rows : (x * 2 + half + 1) * rows]
                     blocks[jnp.where(c == 0, even, odd), :, to] = piece
 
-    multiply(own_l, arrived.at[0], slice(head, 4 * head), slice(0, 3 * head))
-    multiply(own_c, arrived.at[1], slice(0, head), slice(3 * head, 4 * head))
-
-
-def weight_parts(back, own_l, own_c, arrived):
+    multiply(own_l, arr_l, slice(head, 4 * head), slice(0, 3 * head))
+    multiply(own_c, arr_c, slice(0, head), slice(3 * head, 4 * head))
+
+
+def weight_parts(back, own_l, own_c, arr_l, arr_c):
     tokens, width = own_l.shape
     columns = back.shape[-1]
     count = NYL * NX * 2
     return pl.pallas_call(
         weight_kernel,
         out_shape=jax.ShapeDtypeStruct((count, width // count, columns), BF),
-        in_specs=[VMEM] * 4,
+        in_specs=[VMEM] * 5,
         out_specs=VMEM,
         scratch_shapes=[pltpu.VMEM((2, tokens, columns), BF)],
         compiler_params=pltpu.CompilerParams(vmem_limit_bytes=LIMIT),
         name="weight_parts",
-    )(back, own_l, own_c, arrived)
+    )(back, own_l, arr_l, own_c, arr_c)
 
 
 def attend_kernel(packed, result):
@@ -297,10 +298,12 @@
 def shards(latents, cotangent, weights):
     width = latents.shape[-1]
     columns = weights.shape[1]
-    own_l, own_c, away = prepare(latents.reshape(-1, width), cotangent.reshape(-1, width))
+    own_l, away_l = prepare(latents.reshape(-1, width), True)
+    own_c, away_c = prepare(cotangent.reshape(-1, width), False)
     blocks, own_l = gather(weights, own_l)
-    mine, theirs, arrived = project(blocks, own_l, own_c, other_core(away))
-    tokens = own_l, own_c, arrived
+    tokens = own_l, own_c, other_core(away_l), other_core(away_c)
+    mine, theirs, *arrived = project(blocks, *tokens)
+    tokens = *tokens[:2], *arrived
     both = lax.all_gather(theirs, "c")
     part = lax.dynamic_index_in_dim(both, 1 - lax.axis_index("c"), keepdims=False)
     packed = exchange((mine + part.astype(F32)).astype(BF), PLANE)

time: 135 us -> 135 us (level)
  waiting for transfers between devices: 7.97 us -> 4.63 us
  starting transfers between devices: 24.9 us -> 27.8 us
  Pallas kernels: 10.1 us -> 12.1 us
    ppermute x1 -> x2, starting transfers between devices: 1.91 us -> 4.3 us  [other_core(): return lax.ppermute(v, 'c', [(0, 1), (1, 0)])]
    pallas_call x1 -> x2, Pallas kernels: 2.99 us -> 5.01 us  [prepare(): pl.pallas_call(functools.partial(prepare_kernel, norm), out_shape=(shape,...]
    all_to_all x2, waiting for transfers between devices: 4.26 us -> 2.4 us  [exchange(): lax.all_to_all(v, AXES, split_axis=0, concat_axis=0, axis_index_groups=me...]
    ppermute x1 -> x2, waiting for transfers between devices: 3.72 us -> 2.22 us  [other_core(): return lax.ppermute(v, 'c', [(0, 1), (1, 0)])]
    unnamed x8 -> x6, local copies, waits for them, and re-layouts: 4.86 us -> 3.7 us
  transfers between devices with their start and end apart: 3 -> 4, of which waited for: 2 -> 2; matrix products, arithmetic and copies ran while one was open for 0% -> 0% of each run, Pallas kernels for 2% -> 4%
where the time goes in v9:
time: 135 us; the launch traced here: 132 us
  blocking collectives  82.7 us (61%)
  starting transfers between devices  27.8 us (21%)
  Pallas kernels  12.1 us (9%)
  waiting for transfers between devices  4.63 us (3%)
  local copies, waits for them, and re-layouts  4.46 us (3%)
    all_to_all x5, blocking collectives, exchange(): lax.all_to_all(v, AXES, split_axis=0, concat_axis=0, axis_index_groups=me...  74.7 us
    all_to_all x2, starting transfers between devices, exchange(): lax.all_to_all(v, AXES, split_axis=0, concat_axis=0, axis_index_groups=me...  23.5 us
    all_gather x1, blocking collectives, shards(): back = lax.all_gather(exchange(result.reshape(packed.shape), PLANE), 'c')  5.77 us
    pallas_call x2, Pallas kernels, prepare(): pl.pallas_call(functools.partial(prepare_kernel, norm), out_shape=(shape,...  5.01 us
    ppermute x2, starting transfers between devices, other_core(): return lax.ppermute(v, 'c', [(0, 1), (1, 0)])  4.3 us
    unnamed x6, local copies, waits for them, and re-layouts  3.7 us
    pallas_call x1, Pallas kernels, project(): pl.pallas_call(project_kernel, out_shape=(jax.ShapeDtypeStruct(shape, F32...  2.87 us
  transfers between devices with their start and end apart: 4, of which 2 were waited for; matrix products, arithmetic and copies ran while one was open for 0% of the time, Pallas kernels for 4%

profile of v9, /device:TPU:1, one launch (start us, length us, event | category | flops | bytes accessed | tf_op | source)
XLA Modules:
  0.0 132.1 jit_solution(15640790922266239331)
XLA Ops:
  0.0 0.9 copy-done
  0.9 0.7 broadcast_in_dim.4
  1.6 6.9 %all-to-all-start = ((bf16[4,48,512]{2,1,0:T(8,128)(2,1)}), bf16[4,48,512]{2,1,0:T(8,128)(2,1)S(1)}, u32[]{:S(2)}, u32[]{:S(2)}) async-start(bf16[4,48,512]{2,1,0:T(8,128)(2,1)} %broadcast_in_dim.4), calls=%async_computation | async-start | bytes 393216 | tf_op jit(solution)/shard_map/all_to_all | solution.py:64
  8.5 1.4 %copy-done.1 = bf16[1,1,256,3072]{3,2,1,0:T(8,128)(2,1)S(1)} copy-done((bf16[1,1,256,3072]{3,2,1,0:T(8,128)(2,1)S(1)}, bf16[1,1,256,3072]{3,2,1,0:T(8,128)(2,1)}, u32[]{:S(2)}) %copy-start.1) | copy-done | bytes 1572888
  9.9 2.7 %prepare.2 = (bf16[256,1536]{1,0:T(8,128)(2,1)S(1)}, bf16[256,1536]{1,0:T(8,128)(2,1)}) custom-call(bf16[256,3072]{1,0:T(8,128)(2,1)S(1)} %bitcast.16), custom_call_target="tpu_custom_call" | custom-call | tf_op jit(solution)/shard_map/prepare/pallas_call | solution.py:105
  12.5 2.4 %all-to-all-done.value = bf16[4,48,512]{2,1,0:T(8,128)(2,1)S(1)} async-done(((bf16[4,48,512]{2,1,0:T(8,128)(2,1)}), bf16[4,48,512]{2,1,0:T(8,128)(2,1)S(1)}, u32[]{:S(2)}, u32[]{:S(2)}) %all-to-all-start) | async-done | bytes 196640 | tf_op jit(solution)/shard_map/all_to_all | solution.py:64
  14.9 1.2 repeat.1
  16.2 16.6 %all-to-all-start.1 = ((bf16[8,4,48,512]{3,2,1,0:T(8,128)(2,1)}), bf16[8,4,48,512]{3,2,1,0:T(8,128)(2,1)S(1)}, u32[]{:S(2)}, u32[]{:S(2)}) async-start(bf16[8,4,48,512]{3,2,1,0:T(8,128)(2,1)} %repeat.1), calls=%async_computation.1 | async-start | bytes 3145728 | tf_op jit(solution)/shard_map/all_to_all | solution.py:64
  32.8 1.9 %collective-permute-start = (bf16[256,1536]{1,0:T(8,128)(2,1)}, bf16[256,1536]{1,0:T(8,128)(2,1)}, u32[]{:S(2)}, u32[]{:S(2)}) collective-permute-start(bf16[256,1536]{1,0:T(8,128)(2,1)} %get-tuple-element.19), channel_id=1, source_target_pairs={{0,1},{1,0},{2,3},{3,2},{4,5},{5,4},{6,7},{7,6},{8,9},{9,8},{10,11... | collective-permute-start | bytes 2359304 | tf_op jit(solution)/shard_map/ppermute | solution.py:60
  34.7 1.4 %copy-done.2 = bf16[1,1,256,3072]{3,2,1,0:T(8,128)(2,1)S(1)} copy-done((bf16[1,1,256,3072]{3,2,1,0:T(8,128)(2,1)S(1)}, bf16[1,1,256,3072]{3,2,1,0:T(8,128)(2,1)}, u32[]{:S(2)}) %copy-start.2) | copy-done | bytes 1572888
  36.1 2.3 %prepare.3 = (bf16[256,1536]{1,0:T(8,128)(2,1)S(1)}, bf16[256,1536]{1,0:T(8,128)(2,1)}) custom-call(bf16[256,3072]{1,0:T(8,128)(2,1)S(1)} %bitcast.17), custom_call_target="tpu_custom_call" | custom-call | tf_op jit(solution)/shard_map/prepare/pallas_call | solution.py:105
  38.5 2.4 %collective-permute-start.1 = (bf16[256,1536]{1,0:T(8,128)(2,1)}, bf16[256,1536]{1,0:T(8,128)(2,1)}, u32[]{:S(2)}, u32[]{:S(2)}) collective-permute-start(bf16[256,1536]{1,0:T(8,128)(2,1)} %get-tuple-element.20), channel_id=1, source_target_pairs={{0,1},{1,0},{2,3},{3,2},{4,5},{5,4},{6,7},{7,6},{8,9},{9,8},{10,11... | collective-permute-start | bytes 2359304 | tf_op jit(solution)/shard_map/ppermute | solution.py:60
  40.9 2.2 %collective-permute-done.1.arr_c = bf16[256,1536]{1,0:T(8,128)(2,1)} collective-permute-done((bf16[256,1536]{1,0:T(8,128)(2,1)}, bf16[256,1536]{1,0:T(8,128)(2,1)}, u32[]{:S(2)}, u32[]{:S(2)}) %collective-permute-start.1) | collective-permute-done | bytes 786464 | tf_op jit(solution)/shard_map/ppermute | solution.py:60
  43.1 2.9 %project.1 = (f32[16,2,8,512]{3,2,1,0:T(8,128)S(1)}, bf16[16,2,8,512]{3,2,1,0:T(8,128)(2,1)S(1)}, bf16[256,1536]{1,0:T(8,128)(2,1)S(1)}, bf16[256,1536]{1,0:T(8,128)(2,1)S(1)}) custom-call(bf16[32,48,512]{2,1,0:T(8,128)(2,1)S(1)} %bitcast.13, bf16[256,1536]{1,0:T(8,128)(2,1)S(1)} %get-tuple-element.17.own_l, bf16[256,1536]{1,0:T(8,128)(2,1)S(1)} %get-tuple-element.18.own_c, ...), custom_call_target="tpu_custom_call" | custom-call | tf_op jit(solution)/shard_map/project/pallas_call | solution.py:140
  46.0 2.2 %all-gather = bf16[32,2,8,512]{3,2,1,0:T(8,128)(2,1)S(1)} all-gather(bf16[16,2,8,512]{3,2,1,0:T(8,128)(2,1)S(1)} %get-tuple-element.22), channel_id=2, replica_groups=mesh['z'=8,'yh'=2,'yl'=4,'x'=4,'c'=2] {'c'}, dimensions={0}, use_global_device_ids=true | all-gather | bytes 786432 | tf_op jit(solution)/shard_map/all_gather | solution.py:307
  48.3 12.2 %all_to_all.35 = bf16[16,2,8,512]{3,2,1,0:T(8,128)(2,1)S(1)} all-to-all(bf16[16,2,8,512]{3,2,1,0:T(8,128)(2,1)S(1)} %fusion), channel_id=1, replica_groups={{24,26,28,30,0,2,4,6,8,10,12,14,16,18,20,22},{13,15,9,11,21,23,17,19,29..., dimensions={0} | all-to-all | bytes 524288 | tf_op jit(solution)/shard_map/all_to_all | solution.py:64
  60.4 0.9 attend.1
  61.3 11.3 %all_to_all.36 = bf16[16,2,8,512]{3,2,1,0:T(8,128)(2,1)S(1)} all-to-all(bf16[16,2,8,512]{3,2,1,0:T(8,128)(2,1)S(1)} %bitcast.19), channel_id=1, replica_groups={{24,26,28,30,0,2,4,6,8,10,12,14,16,18,20,22},{13,15,9,11,21,23,17,19,29..., dimensions={0} | all-to-all | bytes 524288 | tf_op jit(solution)/shard_map/all_to_all | solution.py:64
  72.6 5.8 %all-gather.1 = bf16[32,2,8,512]{3,2,1,0:T(8,128)(2,1)S(1)} all-gather(bf16[16,2,8,512]{3,2,1,0:T(8,128)(2,1)S(1)} %all_to_all.36), channel_id=3, replica_groups=mesh['z'=8,'yh'=2,'yl'=4,'x'=4,'c'=2] {'c'}, dimensions={0}, use_global_device_ids=true | all-gather | bytes 786432 | tf_op jit(solution)/shard_map/all_gather | solution.py:311
  78.4 1.4 %weight_parts.1 = bf16[32,48,512]{2,1,0:T(8,128)(2,1)S(1)} custom-call(bf16[2,16,2,8,512]{4,3,2,1,0:T(8,128)(2,1)S(1)} %bitcast.15, bf16[256,1536]{1,0:T(8,128)(2,1)S(1)} %get-tuple-element.17.own_l, bf16[256,1536]{1,0:T(8,128)(2,1)S(1)} %get-tuple-element.23.arr_l, bf16[256,1536]{1,0:T(8,128)(2,1)S(1)} %get-tuple-element.18.own_c, ...), custom_call_target="tpu_custom_call" | custom-call | tf_op jit(solution)/shard_map/weight_parts/pallas_call | solution.py:188
  79.8 18.2 %all_to_all.37 = bf16[8,4,48,512]{3,2,1,0:T(8,128)(2,1)S(1)} all-to-all(bf16[8,4,48,512]{3,2,1,0:T(8,128)(2,1)S(1)} %bitcast.14), channel_id=1, replica_groups={{0,64,2,66,8,72,10,74},{511,63,505,57,455,7,449,1},{507,59,509,61,451,3..., dimensions={0} | all-to-all | bytes 3145728 | tf_op jit(solution)/shard_map/all_to_all | solution.py:64
  98.3 15.3 %all_to_all.38 = bf16[16,48,128]{2,1,0:T(8,128)(2,1)S(1)} all-to-all(bf16[16,48,128]{2,1,0:T(8,128)(2,1)S(1)} %bitcast.22), channel_id=1, replica_groups={{0,128,256,384,4,132,260,388,16,144,272,400,20,148,276,404},{1,129,257,..., dimensions={0} | all-to-all | bytes 393216 | tf_op jit(solution)/shard_map/all_to_all | solution.py:64
  113.6 17.8 %all_to_all.39 = bf16[16,48,128]{2,1,0:T(8,128)(2,1)S(1)} all-to-all(bf16[16,48,128]{2,1,0:T(8,128)(2,1)S(1)} %broadcast_in_dim.5), channel_id=1, replica_groups={{0,32,64,96,128,160,192,224,256,288,320,352,384,416,448,480},{449,481,1..., dimensions={0} | all-to-all | bytes 393216 | tf_op jit(solution)/shard_map/all_to_all | solution.py:64
  131.4 0.7 finish.1
  (12 shorter events, 0.5 us)
Async XLA Ops:
  0.0 0.9 copy-start
  1.6 13.4 %all-to-all-start = ((bf16[4,48,512]{2,1,0:T(8,128)(2,1)}), bf16[4,48,512]{2,1,0:T(8,128)(2,1)S(1)}, u32[]{:S(2)}, u32[]{:S(2)}) async-start(bf16[4,48,512]{2,1,0:T(8,128)(2,1)} %broadcast_in_dim.4), calls=%async_computation | async-start | bytes 393216 | tf_op jit(solution)/shard_map/all_to_all | solution.py:64
  8.5 1.4 %copy-start.1 = (bf16[1,1,256,3072]{3,2,1,0:T(8,128)(2,1)S(1)}, bf16[1,1,256,3072]{3,2,1,0:T(8,128)(2,1)}, u32[]{:S(2)}) copy-start(bf16[1,1,256,3072]{3,2,1,0:T(8,128)(2,1)} %param.3) | copy-start | bytes 4718596
  16.2 26.9 %all-to-all-start.1 = ((bf16[8,4,48,512]{3,2,1,0:T(8,128)(2,1)}), bf16[8,4,48,512]{3,2,1,0:T(8,128)(2,1)S(1)}, u32[]{:S(2)}, u32[]{:S(2)}) async-start(bf16[8,4,48,512]{3,2,1,0:T(8,128)(2,1)} %repeat.1), calls=%async_computation.1 | async-start | bytes 3145728 | tf_op jit(solution)/shard_map/all_to_all | solution.py:64
  32.8 8.1 %collective-permute-start = (bf16[256,1536]{1,0:T(8,128)(2,1)}, bf16[256,1536]{1,0:T(8,128)(2,1)}, u32[]{:S(2)}, u32[]{:S(2)}) collective-permute-start(bf16[256,1536]{1,0:T(8,128)(2,1)} %get-tuple-element.19), channel_id=1, source_target_pairs={{0,1},{1,0},{2,3},{3,2},{4,5},{5,4},{6,7},{7,6},{8,9},{9,8},{10,11... | collective-permute-start | bytes 2359304 | tf_op jit(solution)/shard_map/ppermute | solution.py:60
  34.7 1.4 %copy-start.2 = (bf16[1,1,256,3072]{3,2,1,0:T(8,128)(2,1)S(1)}, bf16[1,1,256,3072]{3,2,1,0:T(8,128)(2,1)}, u32[]{:S(2)}) copy-start(bf16[1,1,256,3072]{3,2,1,0:T(8,128)(2,1)} %param.4) | copy-start | bytes 4718596
  38.5 4.6 %collective-permute-start.1 = (bf16[256,1536]{1,0:T(8,128)(2,1)}, bf16[256,1536]{1,0:T(8,128)(2,1)}, u32[]{:S(2)}, u32[]{:S(2)}) collective-permute-start(bf16[256,1536]{1,0:T(8,128)(2,1)} %get-tuple-element.20), channel_id=1, source_target_pairs={{0,1},{1,0},{2,3},{3,2},{4,5},{5,4},{6,7},{7,6},{8,9},{9,8},{10,11... | collective-permute-start | bytes 2359304 | tf_op jit(solution)/shard_map/ppermute | solution.py:60
